TPU v7x, 32 devices: a whole 2x2x4 slice. The times are simulated.
32 devices in a mesh: groups: 2 (over x), tensor: 16 (over z, y, core).
Axes of the slice: x: 2, y: 2, z: 4, core: 2. Of those that a mesh axis runs over, the one named last changes fastest.
Arguments:
- tokens: bfloat16 [768, 4096], P(('groups', 'tensor')), parts along dimension 0, may hold values from -6 to 6
- targets: bfloat16 [768, 4096], P(('groups', 'tensor')), parts along dimension 0, may hold values from -6 to 6
- gate_weight: bfloat16 [4096, 16384], P(None, 'tensor'), may hold values from -0.09375 to 0.09375
- up_weight: bfloat16 [4096, 16384], P(None, 'tensor'), may hold values from -0.09375 to 0.09375
- down_weight: bfloat16 [16384, 4096], P('tensor'), may hold values from -0.046875 to 0.046875
- probe: bfloat16 [8192, 16384], P('groups', 'tensor'), parts along dimension 0, may hold values from -1 to 1, as said below
Outputs:
- hvp: bfloat16 [8192, 16384], P('groups', 'tensor'), parts along dimension 0
There are 2 independent parts, one for each index of `groups`. A program takes and returns all parts, laid end to end along the dimension named above; an argument that names none is the same for every part. Nothing has to cross between parts.
Inputs may be any that keep to these rules, and one draw needn't show every extreme that they name: Every entry of the probe is -1 or 1.
All inputs are finite; a program needn't handle non-finite values.
Results may differ from a plain program's by a relative error of at most 0.006.
Values may be sent and summed in bfloat16 or wider, within the bound.
No kernel may reach another device: no remote copies, remote signals or barrier semaphores. Data moves between devices by JAX's collectives and lax.ppermute only.
A program may use at most 128 MiB of HBM per device.

v0:
```python
import jax
import jax.numpy as jnp
from jax import lax
from jax.sharding import PartitionSpec as P


def back_dot(left, weight):
    return lax.dot_general(
        left, weight, (((1,), (1,)), ((), ())), preferred_element_type=jnp.float32
    )


def on_device(tokens, targets, gate_weight, up_weight, down_weight, probe):
    features = tokens.shape[1]
    everyone = lax.all_gather(tokens, "tensor", axis=0, tiled=True)
    total_rows = everyone.shape[0]
    preact = jnp.dot(everyone, gate_weight, preferred_element_type=jnp.float32)
    linear = jnp.dot(everyone, up_weight, preferred_element_type=jnp.float32)
    tangent = jnp.dot(everyone, probe, preferred_element_type=jnp.float32) * features ** (-0.5)
    logistic = jax.nn.sigmoid(preact)
    slopes = logistic * (1.0 + preact * (1.0 - logistic))
    curvature = logistic * (1.0 - logistic) * (2.0 + preact * (1.0 - 2.0 * logistic))
    hidden = (preact * logistic * linear).astype(jnp.bfloat16)
    hidden_dot = (slopes * tangent * linear).astype(jnp.bfloat16)
    output = lax.psum_scatter(
        jnp.dot(hidden, down_weight, preferred_element_type=jnp.float32),
        "tensor",
        scatter_dimension=0,
        tiled=True,
    )
    output_dot = lax.psum_scatter(
        jnp.dot(hidden_dot, down_weight, preferred_element_type=jnp.float32),
        "tensor",
        scatter_dimension=0,
        tiled=True,
    )
    errors = (output - targets.astype(jnp.float32)).astype(jnp.bfloat16)
    stacked = jnp.stack([errors, output_dot.astype(jnp.bfloat16)])
    block_rows = lax.all_gather(stacked, "tensor", axis=1, tiled=True)
    gradient = back_dot(block_rows[0], down_weight)
    gradient_dot = back_dot(block_rows[1], down_weight)
    mixed = gradient_dot * linear * slopes + gradient * linear * curvature * tangent
    weighted = mixed.astype(jnp.bfloat16)
    result = lax.dot_general(
        everyone, weighted, (((0,), (0,)), ((), ())), preferred_element_type=jnp.float32
    )
    return (result * total_rows ** (-0.5)).astype(jnp.bfloat16)


def solution(mesh):
    placed = (
        P(("groups", "tensor"), None),
        P(("groups", "tensor"), None),
        P(None, "tensor"),
        P(None, "tensor"),
        P("tensor", None),
        P("groups", "tensor"),
    )
    return jax.shard_map(
        on_device, mesh=mesh, in_specs=placed, out_specs=P("groups", "tensor"), check_vma=False
    )
```

profile of v0, /device:TPU:0, one launch (start us, length us, event | category | flops | bytes accessed | tf_op | source)
XLA Modules:
  0.0 362.0 jit_solution(2897762563891021057)
XLA Ops:
  6.5 0.0 all-gather.3.cloned.1.call-start
  6.5 0.7 all-gather.3.cloned.1.call-update
  7.3 0.0 reduce-scatter.5.cloned.1.call-start
  7.3 50.3 %all-gather.3.cloned.1.call-done = bf16[384,4096]{1,0:T(8,128)(2,1)} async-done(((bf16[24,4096]{1,0:T(8,128)(2,1)}), bf16[384,4096]{1,0:T(8,128)(2,1)}) %all-gather.3.cloned.1.call-update) | async-done | bytes 3145744 | tf_op jit(solution)/shard_map/all_gather | solution.py:15
  57.6 0.0 copy-start.1
  57.6 0.0 slice-start
  57.6 7.8 %fusion.23 = f32[384,1024]{1,0:T(8,128)S(1)} fusion(bf16[384,4096]{1,0:T(8,128)(2,1)} %all-gather.3.cloned.1.call-done, bf16[4096,1024]{1,0:T(8,128)(2,1)} %param.9), kind=kOutput, calls=%fused_computation.33 | convolution fusion | flops 3221225472 | bytes 13107200 | tf_op jit(solution)/shard_map/dot_general | solution.py:18
  65.4 0.0 copy-done.1
  65.4 0.0 copy-start.2
  65.4 0.0 slice-start.1
  65.5 0.0 slice-start.2
  65.5 6.4 %fusion.22 = f32[384,1024]{1,0:T(8,128)S(1)} fusion(bf16[384,4096]{1,0:T(8,128)(2,1)S(1)} %copy-done.1, bf16[4096,1024]{1,0:T(8,128)(2,1)} %param.8), kind=kOutput, calls=%fused_computation.32 | convolution fusion | flops 3221225472 | bytes 13107200 | tf_op jit(solution)/shard_map/dot_general | solution.py:17
  71.9 0.0 slice-done
  71.9 0.0 slice-done.1
  71.9 0.0 copy-start.3
  71.9 0.0 slice-start.3
  71.9 3.4 convolution_multiply_fusion
  75.3 0.0 copy-done.2
  75.3 0.0 copy-done.3
  75.3 0.0 copy-start.4
  75.3 1.2 copy-done.4
  76.5 0.0 slice-done.2
  76.5 0.0 slice-done.3
  76.5 5.9 %fusion.11 = f32[384,4096]{1,0:T(8,128)} fusion(bf16[1024,4096]{1,0:T(8,128)(2,1)S(1)} %bitcast.30, f32[384,1024]{1,0:T(8,128)S(1)} %fusion.23, f32[384,1024]{1,0:T(8,128)S(1)} %convolution_multiply_fusion, f32[384,1024]{1,0:T(8,128)S(1)} %fusion.22), kind=kOutput, calls=%fused_computation.20 | convolution fusion | flops 3225157632 | bytes 19398656 | tf_op jit(solution)/shard_map/dot_general | solution.py:32
  82.4 0.0 reduce-scatter.5.cloned.1.call-update
  82.4 0.0 reduce-scatter.3.cloned.1.call-start
  82.5 10.5 %fusion.10 = f32[384,4096]{1,0:T(8,128)} fusion(bf16[1024,4096]{1,0:T(8,128)(2,1)} %param.10, f32[384,1024]{1,0:T(8,128)} %copy-done.2, f32[384,1024]{1,0:T(8,128)} %copy-done.3), kind=kOutput, calls=%fused_computation.19 | convolution fusion | flops 3223584768 | bytes 17825792 | tf_op jit(solution)/shard_map/dot_general | solution.py:26
  93.0 0.0 copy-start
  93.0 0.0 reduce-scatter.3.cloned.1.call-update
  93.0 0.2 all-gather.5.cloned.1.call-start
  93.2 73.4 %reduce-scatter.5.cloned.1.call-done = f32[24,4096]{1,0:T(8,128)} async-done(((f32[384,4096]{1,0:T(8,128)}), f32[24,4096]{1,0:T(8,128)}) %reduce-scatter.5.cloned.1.call-update) | async-done | bytes 393232 | tf_op jit(solution)/shard_map/reduce_scatter | solution.py:31
  166.7 1.0 convert_bitcast_fusion
  167.7 88.0 %reduce-scatter.3.cloned.1.call-done = f32[24,4096]{1,0:T(8,128)} async-done(((f32[384,4096]{1,0:T(8,128)}), f32[24,4096]{1,0:T(8,128)}) %reduce-scatter.3.cloned.1.call-update) | async-done | bytes 393232 | tf_op jit(solution)/shard_map/reduce_scatter | solution.py:25
  255.7 0.0 copy-done
  255.7 1.0 fusion.17
  256.7 0.8 pad_maximum_fusion
  257.5 0.0 all-gather.5.cloned.1.call-update
  257.5 61.6 %all-gather.5.cloned.1.call-done = bf16[2,384,4096]{2,1,0:T(8,128)(2,1)} async-done(((bf16[2,24,4096]{2,1,0:T(8,128)(2,1)}), bf16[2,384,4096]{2,1,0:T(8,128)(2,1)}) %all-gather.5.cloned.1.call-update) | async-done | bytes 6291472 | tf_op jit(solution)/shard_map/all_gather | solution.py:39
  319.1 8.9 %fusion.1 = f32[384,1024]{1,0:T(8,128)} fusion(bf16[1024,4096]{1,0:T(8,128)(2,1)} %param.10, bf16[2,384,4096]{2,1,0:T(8,128)(2,1)} %all-gather.5.cloned.1.call-done), kind=kOutput, calls=%fused_computation.3 | convolution fusion | flops 3221225472 | bytes 13107200 | tf_op jit(solution)/shard_map/dot_general | solution.py:8
  328.0 15.5 %fusion = bf16[4096,1024]{0,1:T(8,128)(2,1)} fusion(bf16[384,4096]{1,0:T(8,128)(2,1)S(1)} %copy-done.1, f32[384,1024]{1,0:T(8,128)} %copy-done.4, f32[384,1024]{1,0:T(8,128)} %copy-done.3, f32[384,1024]{1,0:T(8,128)} %fusion.1, f32[384,1024]{1,0:T(8,128)} %copy-done.2, bf16[1024,4096]{1,0:T(8,128)(2,1)} %param.10, ...), kind=kOutput, calls=%fused_computation.1 | convolution fusion | flops 6458703872 | bytes 29360128 | tf_op jit(solution)/shard_map/dot_general | solution.py:44
  343.5 11.9 %copy.7 = bf16[4096,1024]{1,0:T(8,128)(2,1)} copy(bf16[4096,1024]{0,1:T(8,128)(2,1)} %fusion) | data formatting | bytes 16777216 | tf_op jit(solution)/shard_map/convert_element_type | solution.py:47
  (2 shorter events, 0.0 us)
Async XLA Ops:
  6.5 51.0 %all-gather.3.cloned.1.call-start = ((), (), s32[]{:S(2)}) async-start(), calls=%async_computation.2 | async-start | bytes 3342336 | tf_op jit(solution)/shard_map/all_gather | solution.py:15
  7.3 159.4 %reduce-scatter.5.cloned.1.call-start = ((), (), s32[]{:S(2)}) async-start(), calls=%async_computation.4 | async-start | bytes 6684672 | tf_op jit(solution)/shard_map/reduce_scatter | solution.py:31
  57.6 7.9 %copy-start.1 = (bf16[384,4096]{1,0:T(8,128)(2,1)S(1)}, bf16[384,4096]{1,0:T(8,128)(2,1)}, u32[]{:S(2)}) copy-start(bf16[384,4096]{1,0:T(8,128)(2,1)} %all-gather.3.cloned.1.call-done) | copy-start | bytes 9437188
  57.6 14.3 %slice-start = ((s8[8388608]{0:T(1024)(128)(4,1)}), s8[4194304]{0:T(1024)(128)(4,1)S(1)}, s32[]{:S(2)}) async-start(s8[8388608]{0:T(1024)(128)(4,1)} %bitcast.27), calls=%async_computation.6 | async-start | bytes 8388608
  65.4 9.9 %copy-start.2 = (f32[384,1024]{1,0:T(8,128)}, f32[384,1024]{1,0:T(8,128)S(1)}, u32[]{:S(2)}) copy-start(f32[384,1024]{1,0:T(8,128)S(1)} %fusion.23) | copy-start | bytes 4718596
  65.4 6.4 %slice-start.1 = ((s8[8388608]{0:T(1024)(128)(4,1)}), s8[4194304]{0:T(1024)(128)(4,1)S(1)}, s32[]{:S(2)}) async-start(s8[8388608]{0:T(1024)(128)(4,1)} %bitcast.27), calls=%async_computation.7 | async-start | bytes 8388608
  65.5 11.0 %slice-start.2 = ((s8[8388608]{0:T(1024)(128)(4,1)}), s8[4194304]{0:T(1024)(128)(4,1)S(1)}, s32[]{:S(2)}) async-start(s8[8388608]{0:T(1024)(128)(4,1)} %bitcast.29), calls=%async_computation.8 | async-start | bytes 8388608
  71.9 3.4 copy-start.3
  71.9 4.6 %slice-start.3 = ((s8[8388608]{0:T(1024)(128)(4,1)}), s8[4194304]{0:T(1024)(128)(4,1)S(1)}, s32[]{:S(2)}) async-start(s8[8388608]{0:T(1024)(128)(4,1)} %bitcast.29), calls=%async_computation.9 | async-start | bytes 8388608
  75.3 1.2 copy-start.4
  82.4 173.2 %reduce-scatter.3.cloned.1.call-start = ((), (), s32[]{:S(2)}) async-start(), calls=%async_computation.3 | async-start | bytes 6684672 | tf_op jit(solution)/shard_map/reduce_scatter | solution.py:25
  93.0 162.7 %copy-start = (bf16[24,4096]{1,0:T(8,128)(2,1)S(1)}, bf16[24,4096]{1,0:T(8,128)(2,1)}, u32[]{:S(2)}) copy-start(bf16[24,4096]{1,0:T(8,128)(2,1)} %param.7) | copy-start | bytes 589828
  93.0 226.1 %all-gather.5.cloned.1.call-start = ((), (), s32[]{:S(2)}) async-start(), calls=%async_computation.5 | async-start | bytes 6684672 | tf_op jit(solution)/shard_map/all_gather | solution.py:39
Sparse Core Ops, SparseCore 0:
  9.6 47.8 all-gather.2
  82.6 84.0 reduce-scatter.4
  171.1 84.5 reduce-scatter.2
  257.8 61.2 all-gather.4
where the time goes:
time: 362 us
  waiting for transfers between devices  274 us (76%)
  matrix products  58.4 us (16%)
  between operations  13.3 us (4%)
  local copies, waits for them, and re-layouts  13.1 us (4%)
    reduce_scatter x1, waiting for transfers between devices, on_device(): lax.psum_scatter(jnp.dot(hidden, down_weight, preferred_element_type=jnp....  88 us
    reduce_scatter x1, waiting for transfers between devices, on_device(): lax.psum_scatter(jnp.dot(hidden_dot, down_weight, preferred_element_type=...  73.4 us
    all_gather x1, waiting for transfers between devices, on_device(): block_rows = lax.all_gather(stacked, 'tensor', axis=1, tiled=True)  61.6 us
    all_gather x1, waiting for transfers between devices, on_device(): everyone = lax.all_gather(tokens, 'tensor', axis=0, tiled=True)  50.3 us
    dot_general x1, matrix products, on_device(): lax.dot_general(everyone, weighted, (((0,), (0,)), ((), ())), preferred_e...  15.5 us
    convert_element_type x1, local copies, waits for them, and re-layouts, on_device(): return (result * total_rows ** (-0.5)).astype(jnp.bfloat16)  11.9 us
    dot_general x1, matrix products, on_device(): jnp.dot(hidden, down_weight, preferred_element_type=jnp.float32)  10.5 us
    dot_general x1, matrix products, back_dot(): lax.dot_general(left, weight, (((1,), (1,)), ((), ())), preferred_element...  8.92 us
  transfers between devices with their start and end apart: 4, of which 4 were waited for; matrix products, arithmetic and copies ran while one was open for 3% of the time, Pallas kernels for 0%

commit v1 on v0

v1 whole, which is shorter than its diff:
```python
import jax
import jax.numpy as jnp
from jax import lax
from jax.experimental import pallas as pl
from jax.experimental.pallas import tpu as pltpu
from jax.sharding import PartitionSpec as P

AXIS = "tensor"


def ring_routes(devices):
    chips = devices // 2
    cycle = list(range(0, chips, 2)) + list(range(1, chips, 2))[::-1]
    onward, backward = [], []
    for place, chip in enumerate(cycle):
        following = cycle[(place + 1) % chips]
        for core in range(2):
            onward.append((chip * 2 + core, following * 2 + core))
            backward.append((following * 2 + core, chip * 2 + core))
    partner = [(device, device ^ 1) for device in range(devices)]
    return onward, backward, partner


def send(block, route):
    return lax.ppermute(block, AXIS, route)


def gather_ring(own, devices):
    onward, backward, _ = ring_routes(devices)
    chips = devices // 2
    before, after = own, own
    blocks = [own]
    for _ in range((chips - 1) // 2):
        before, after = send(before, onward), send(after, backward)
        blocks += [before, after]
    if chips % 2 == 0:
        half = own.shape[-1] // 2
        blocks.append(
            jnp.concatenate(
                [send(before[..., :half], onward), send(after[..., half:], backward)], axis=-1
            )
        )
    return blocks


def scatter_ring(blocks, devices):
    onward, backward, _ = ring_routes(devices)
    chips = devices // 2
    steps = (chips - 1) // 2
    from_before = from_after = None
    if chips % 2 == 0:
        half = blocks[0].shape[-1] // 2
        far = blocks[-1].astype(jnp.bfloat16)
        from_before, from_after = send(far[..., :half], onward), send(far[..., half:], backward)
        rest = [(0, 0)] * (far.ndim - 1)
        from_before = jnp.pad(from_before.astype(jnp.float32), rest + [(0, half)])
        from_after = jnp.pad(from_after.astype(jnp.float32), rest + [(half, 0)])
    for distance in range(steps, 0, -1):
        to_after, to_before = blocks[2 * distance], blocks[2 * distance - 1]
        if from_before is not None:
            to_after, to_before = to_after + from_before, to_before + from_after
        from_before = send(to_after.astype(jnp.bfloat16), onward).astype(jnp.float32)
        from_after = send(to_before.astype(jnp.bfloat16), backward).astype(jnp.float32)
    return blocks[0] + from_before + from_after


def outer_kernel(scale, left_ref, right_ref, out_ref):
    product = jnp.dot(left_ref[...], right_ref[...], preferred_element_type=jnp.float32)
    out_ref[...] = (product * scale).astype(out_ref.dtype)


def outer(left, right, scale):
    rows, depth = left.shape
    columns = right.shape[1]
    tile = 512
    return pl.pallas_call(
        lambda *refs: outer_kernel(scale, *refs),
        grid=(rows // tile,),
        in_specs=[
            pl.BlockSpec((tile, depth), lambda i: (i, 0)),
            pl.BlockSpec((depth, columns), lambda i: (0, 0)),
        ],
        out_specs=pl.BlockSpec((tile, columns), lambda i: (i, 0)),
        out_shape=jax.ShapeDtypeStruct((rows, columns), jnp.bfloat16),
        compiler_params=pltpu.CompilerParams(vmem_limit_bytes=32 * 2**20),
        cost_estimate=pl.CostEstimate(
            flops=2 * rows * depth * columns,
            bytes_accessed=2 * (rows * depth + depth * columns + rows * columns),
            transcendentals=0,
        ),
        name="outer",
    )(left, right)


def on_device(devices, tokens, targets, gate_weight, up_weight, down_weight, probe):
    features = tokens.shape[1]
    mine = tokens.shape[0]
    partner = ring_routes(devices)[2]
    blocks = gather_ring(tokens, devices)
    count = len(blocks)
    near = max(1, min(5, count - 1))
    groups = [list(range(near)), list(range(near, count))]

    rows_of, saved, partial = [], [], [None] * count
    for group in groups:
        same = jnp.concatenate([blocks[b] for b in group])
        rows = jnp.concatenate([same, send(same, partner)])
        rows_of.append(rows)
        preact = jnp.dot(rows, gate_weight, preferred_element_type=jnp.float32)
        linear = jnp.dot(rows, up_weight, preferred_element_type=jnp.float32)
        tangent = jnp.dot(rows, probe, preferred_element_type=jnp.float32) * features ** (-0.5)
        logistic = jax.nn.sigmoid(preact)
        slopes = logistic * (1.0 + preact * (1.0 - logistic))
        curvature = logistic * (1.0 - logistic) * (2.0 + preact * (1.0 - 2.0 * logistic))
        hidden = (preact * logistic * linear).astype(jnp.bfloat16)
        hidden_dot = (slopes * tangent * linear).astype(jnp.bfloat16)
        saved.append((linear * slopes, linear * curvature * tangent))
        product = jnp.dot(
            jnp.concatenate([hidden, hidden_dot]), down_weight, preferred_element_type=jnp.float32
        ).reshape(2, 2, len(group), mine, features)
        summed = product[:, 0] + send(product[:, 1].astype(jnp.bfloat16), partner).astype(jnp.float32)
        for at, b in enumerate(group):
            partial[b] = summed[:, at]

    output, output_dot = scatter_ring(partial, devices)
    errors = (output - targets.astype(jnp.float32)).astype(jnp.bfloat16)
    stacked = jnp.stack([errors, output_dot.astype(jnp.bfloat16)])
    back = gather_ring(stacked, devices)

    weighted = []
    for group, (by_dot, by_error) in zip(groups, saved):
        same = jnp.concatenate([back[b] for b in group], axis=1)
        both = jnp.stack([same, send(same, partner)], axis=1)
        both = both.reshape(2, -1, features)
        gradient = lax.dot_general(
            both, down_weight, (((2,), (1,)), ((), ())), preferred_element_type=jnp.float32
        )
        weighted.append((gradient[1] * by_dot + gradient[0] * by_error).astype(jnp.bfloat16))
    everyone = jnp.concatenate(rows_of)
    return outer(everyone.T, jnp.concatenate(weighted), (mine * devices) ** (-0.5))


def solution(mesh):
    placed = (
        P(("groups", "tensor"), None),
        P(("groups", "tensor"), None),
        P(None, "tensor"),
        P(None, "tensor"),
        P("tensor", None),
        P("groups", "tensor"),
    )

    def whole(*arrays):
        return on_device(mesh.shape[AXIS], *arrays)

    return jax.shard_map(
        whole, mesh=mesh, in_specs=placed, out_specs=P("groups", "tensor"), check_vma=False
    )
```

time: 362 us -> 201 us (0.56)
  waiting for transfers between devices: 274 us -> 83.8 us
  starting transfers between devices: 0.3 us -> 27.3 us
  matrix products: 58.4 us -> 37.6 us
  local copies, waits for them, and re-layouts: 13.1 us -> 33.6 us
  between operations: 13.3 us -> 0.61 us
  Pallas kernels: 0 us -> 7.44 us
  other arithmetic: 2.83 us -> 9.69 us
    reduce_scatter x2 -> x0, waiting for transfers between devices: 161 us -> none  [the longest x1 88 us: on_device(): lax.psum_scatter(jnp.dot(hidden, down_weight, preferred_element_type=jnp....]
    all_gather x2 -> x0, waiting for transfers between devices: 112 us -> none  [the longest x1 61.6 us: on_device(): block_rows = lax.all_gather(stacked, 'tensor', axis=1, tiled=True)]
    ppermute x0 -> x30, waiting for transfers between devices: none -> 83.8 us  [send(): return lax.ppermute(block, AXIS, route)]
    ppermute x0 -> x30, starting transfers between devices: none -> 27.3 us  [send(): return lax.ppermute(block, AXIS, route)]
    dot_general x7 -> x10, matrix products: 58.4 us -> 37.6 us  [the longest x2 9.8 us: on_device(): linear = jnp.dot(rows, up_weight, preferred_element_type=jnp.float32)]
    concatenate x0 -> x5, local copies, waits for them, and re-layouts: none -> 13.6 us  [the longest x1 11.4 us: on_device(): everyone = jnp.concatenate(rows_of)]
    convert_element_type x1 -> x3, local copies, waits for them, and re-layouts: 11.9 us -> 0.44 us  [the longest x2 0.4 us: on_device(): product[:, 1].astype(jnp.bfloat16)]
    ppermute x0 -> x8, local copies, waits for them, and re-layouts: none -> 10.8 us  [send(): return lax.ppermute(block, AXIS, route)]
  transfers between devices with their start and end apart: 4 -> 30, of which waited for: 4 -> 20; matrix products, arithmetic and copies ran while one was open for 3% -> 33% of each run, Pallas kernels for 0% -> 0%
where the time goes in v1:
time: 201 us; the launch traced here: 200 us
  waiting for transfers between devices  83.8 us (42%)
  matrix products  37.6 us (19%)
  local copies, waits for them, and re-layouts  33.6 us (17%)
  starting transfers between devices  27.3 us (14%)
  other arithmetic  9.69 us (5%)
  Pallas kernels  7.44 us (4%)
    ppermute x30, waiting for transfers between devices, send(): return lax.ppermute(block, AXIS, route)  83.8 us
    ppermute x30, starting transfers between devices, send(): return lax.ppermute(block, AXIS, route)  27.3 us
    concatenate x1, local copies, waits for them, and re-layouts, on_device(): everyone = jnp.concatenate(rows_of)  11.4 us
    ppermute x8, local copies, waits for them, and re-layouts, send(): return lax.ppermute(block, AXIS, route)  10.8 us
    dot_general x2, matrix products, on_device(): linear = jnp.dot(rows, up_weight, preferred_element_type=jnp.float32)  9.8 us
    dot_general x2, matrix products, on_device(): lax.dot_general(both, down_weight, (((2,), (1,)), ((), ())), preferred_el...  9.44 us
    unnamed x58, local copies, waits for them, and re-layouts  8.24 us
    dot_general x2, matrix products, on_device(): jnp.dot(rows, probe, preferred_element_type=jnp.float32)  7.82 us
  transfers between devices with their start and end apart: 30, of which 20 were waited for; matrix products, arithmetic and copies ran while one was open for 33% of the time, Pallas kernels for 0%

profile of v1, /device:TPU:0, one launch (start us, length us, event | category | flops | bytes accessed | tf_op | source)
XLA Modules:
  0.0 200.0 jit_solution(14662406859545712764)
XLA Ops:
  0.0 3.0 %collective-permute-start = (bf16[24,4096]{1,0:T(8,128)(2,1)}, bf16[24,4096]{1,0:T(8,128)(2,1)S(1)}, u32[]{:S(2)}, u32[]{:S(2)}) collective-permute-start(bf16[24,4096]{1,0:T(8,128)(2,1)} %param.6), channel_id=1, source_target_pairs={{0,4},{1,5},{4,8},{5,9},{8,12},{9,13},{12,14},{13,15},{14,10},{15,... | collective-permute-start | bytes 589832 | tf_op jit(solution)/shard_map/ppermute | solution.py:25
  3.0 5.0 %collective-permute-done = bf16[24,4096]{1,0:T(8,128)(2,1)S(1)} collective-permute-done((bf16[24,4096]{1,0:T(8,128)(2,1)}, bf16[24,4096]{1,0:T(8,128)(2,1)S(1)}, u32[]{:S(2)}, u32[]{:S(2)}) %collective-permute-start) | collective-permute-done | bytes 196640 | tf_op jit(solution)/shard_map/ppermute | solution.py:25
  8.1 1.8 collective-permute-start.2
  11.1 3.0 %collective-permute-done.2 = bf16[24,4096]{1,0:T(8,128)(2,1)S(1)} collective-permute-done((bf16[24,4096]{1,0:T(8,128)(2,1)S(1)}, bf16[24,4096]{1,0:T(8,128)(2,1)S(1)}, u32[]{:S(2)}, u32[]{:S(2)}) %collective-permute-start.2) | collective-permute-done | bytes 196640 | tf_op jit(solution)/shard_map/ppermute | solution.py:25
  14.2 1.5 collective-permute-start.5
  16.9 3.0 %collective-permute-done.5 = bf16[24,4096]{1,0:T(8,128)(2,1)S(1)} collective-permute-done((bf16[24,4096]{1,0:T(8,128)(2,1)S(1)}, bf16[24,4096]{1,0:T(8,128)(2,1)S(1)}, u32[]{:S(2)}, u32[]{:S(2)}) %collective-permute-start.5) | collective-permute-done | bytes 196640 | tf_op jit(solution)/shard_map/ppermute | solution.py:25
  19.9 1.8 collective-permute-start.7
  22.7 1.9 collective-permute-done.7
  24.6 2.7 %collective-permute-done.8 = bf16[24,2048]{1,0:T(8,128)(2,1)S(1)} collective-permute-done((bf16[24,2048]{1,0:T(8,128)(2,1)S(1)}, bf16[24,2048]{1,0:T(8,128)(2,1)S(1)}, u32[]{:S(2)}, u32[]{:S(2)}) %collective-permute-start.8) | collective-permute-done | bytes 98336 | tf_op jit(solution)/shard_map/ppermute | solution.py:25
  29.5 5.5 %convolution_multiply_fusion.1 = f32[144,1024]{1,0:T(8,128)S(1)} fusion(bf16[4096,1024]{1,0:T(8,128)(2,1)} %param.11, bf16[72,4096]{1,0:T(8,128)(2,1)S(1)} %collective-permute-done.9, bf16[24,4096]{1,0:T(8,128)(2,1)S(1)} %constant_dynamic-update-slice_fusion.5, bf16[24,4096]{1,0:T(8,128)(2,1)S(1)} %collective-permute-done.6, ...), kind=kOutput, calls=%fused_computation.16 | convolution fusion | flops 1212825600 | bytes 10158080 | tf_op jit(solution)/shard_map/dot_general | solution.py:111
  35.1 1.4 fusion.55
  36.5 2.5 %multiply_convert_fusion.3 = (bf16[144,1024]{1,0:T(8,128)(2,1)S(1)}, bf16[144,1024]{1,0:T(8,128)(2,1)S(1)}, f32[144,1024]{1,0:T(8,128)}) fusion(f32[144,1024]{1,0:T(8,128)S(1)} %fusion.55, f32[144,1024]{1,0:T(8,128)S(1)} %convolution_multiply_fusion.1, bf16[4096,1024]{1,0:T(8,128)(2,1)S(1)} %bitcast.126, bf16[72,4096]{1,0:T(8,128)(2,1)S(1)} %collective-permute-done.9, ...), kind=kOutput, calls=%fused_computation.80 | convolution fusion | flops 1214595072 | bytes 11927552 | tf_op jit(solution)/shard_map/dot_general | solution.py:110
  39.2 2.7 %fusion.44 = f32[288,4096]{1,0:T(8,128)S(1)} fusion(bf16[1024,4096]{1,0:T(8,128)(2,1)S(1)} %bitcast.128, bf16[144,1024]{1,0:T(8,128)(2,1)S(1)} %get-tuple-element.14, bf16[144,1024]{1,0:T(8,128)(2,1)S(1)} %get-tuple-element.13), kind=kOutput, calls=%fused_computation.75 | convolution fusion | flops 2417098752 | bytes 13697024 | tf_op jit(solution)/shard_map/dot_general | solution.py:118
  42.2 2.2 %fusion.58 = f32[240,1024]{1,0:T(8,128)S(1)} fusion(bf16[240,4096]{1,0:T(8,128)(2,1)S(1)} %constant_dynamic-update-slice_fusion.7, bf16[4096,1024]{1,0:T(8,128)(2,1)S(1)} %bitcast.122), kind=kOutput, calls=%fused_computation.113 | convolution fusion | flops 2013265920 | bytes 11337728 | tf_op jit(solution)/shard_map/dot_general | solution.py:109
  45.6 2.3 %convolution_multiply_fusion = f32[240,1024]{1,0:T(8,128)S(1)} fusion(bf16[240,4096]{1,0:T(8,128)(2,1)S(1)} %constant_dynamic-update-slice_fusion.7, bf16[4096,1024]{1,0:T(8,128)(2,1)S(1)} %bitcast.124), kind=kOutput, calls=%fused_computation.15 | convolution fusion | flops 2013511680 | bytes 11337728 | tf_op jit(solution)/shard_map/dot_general | solution.py:111
  48.0 7.3 %multiply_convert_fusion.1 = (bf16[240,1024]{1,0:T(8,128)(2,1)S(1)}, bf16[240,1024]{1,0:T(8,128)(2,1)S(1)}, f32[240,1024]{1,0:T(8,128)}) fusion(f32[240,1024]{1,0:T(8,128)S(1)} %fusion.58, f32[240,1024]{1,0:T(8,128)S(1)} %convolution_multiply_fusion, bf16[240,4096]{1,0:T(8,128)(2,1)S(1)} %constant_dynamic-update-slice_fusion.7, bf16[4096,1024]{1,0:T(8,128)(2,1)} %param.9), kind=kOutput, calls=%fused_computation.36 | convolution fusion | flops 2016460800 | bytes 14286848 | tf_op jit(solution)/shard_map/dot_general | solution.py:110
  55.3 4.3 %fusion.17 = f32[480,4096]{1,0:T(8,128)S(1)} fusion(bf16[1024,4096]{1,0:T(8,128)(2,1)S(1)} %bitcast.130, bf16[240,1024]{1,0:T(8,128)(2,1)S(1)} %get-tuple-element.10, bf16[240,1024]{1,0:T(8,128)(2,1)S(1)} %get-tuple-element.9), kind=kOutput, calls=%fused_computation.31 | convolution fusion | flops 4028497920 | bytes 17235968 | tf_op jit(solution)/shard_map/dot_general | solution.py:118
  60.7 1.7 collective-permute-start.12
  62.7 4.9 %collective-permute-done.12 = bf16[2,24,2048]{2,1,0:T(8,128)(2,1)S(1)} collective-permute-done((bf16[2,24,2048]{2,1,0:T(8,128)(2,1)S(1)}, bf16[2,24,2048]{2,1,0:T(8,128)(2,1)S(1)}, u32[]{:S(2)}, u32[]{:S(2)}) %collective-permute-start.12) | collective-permute-done | bytes 196640 | tf_op jit(solution)/shard_map/ppermute | solution.py:25
  67.6 1.4 collective-permute-done.16
  69.1 1.6 collective-permute-start.13
  71.9 7.3 %collective-permute-done.13 = bf16[2,24,4096]{2,1,0:T(8,128)(2,1)S(1)} collective-permute-done((bf16[2,24,4096]{2,1,0:T(8,128)(2,1)S(1)}, bf16[2,24,4096]{2,1,0:T(8,128)(2,1)S(1)}, u32[]{:S(2)}, u32[]{:S(2)}) %collective-permute-start.13) | collective-permute-done | bytes 393248 | tf_op jit(solution)/shard_map/ppermute | solution.py:25
  79.2 1.6 collective-permute-start.14
  80.9 7.5 %collective-permute-done.14 = bf16[2,24,4096]{2,1,0:T(8,128)(2,1)S(1)} collective-permute-done((bf16[2,24,4096]{2,1,0:T(8,128)(2,1)S(1)}, bf16[2,24,4096]{2,1,0:T(8,128)(2,1)S(1)}, u32[]{:S(2)}, u32[]{:S(2)}) %collective-permute-start.14) | collective-permute-done | bytes 393248 | tf_op jit(solution)/shard_map/ppermute | solution.py:25
  88.9 1.7 collective-permute-start.15
  90.6 7.1 %collective-permute-done.18 = bf16[2,24,4096]{2,1,0:T(8,128)(2,1)S(1)} collective-permute-done((bf16[2,24,4096]{2,1,0:T(8,128)(2,1)S(1)}, bf16[2,24,4096]{2,1,0:T(8,128)(2,1)S(1)}, u32[]{:S(2)}, u32[]{:S(2)}) %collective-permute-start.18) | collective-permute-done | bytes 393248 | tf_op jit(solution)/shard_map/ppermute | solution.py:25
  98.2 8.6 %collective-permute-done.19 = bf16[2,24,4096]{2,1,0:T(8,128)(2,1)S(1)} collective-permute-done((bf16[2,24,4096]{2,1,0:T(8,128)(2,1)S(1)}, bf16[2,24,4096]{2,1,0:T(8,128)(2,1)S(1)}, u32[]{:S(2)}, u32[]{:S(2)}) %collective-permute-start.19) | collective-permute-done | bytes 393248 | tf_op jit(solution)/shard_map/ppermute | solution.py:25
  108.2 1.7 collective-permute-start.20
  109.9 9.2 %collective-permute-done.21 = bf16[2,24,4096]{2,1,0:T(8,128)(2,1)S(1)} collective-permute-done((bf16[2,24,4096]{2,1,0:T(8,128)(2,1)S(1)}, bf16[2,24,4096]{2,1,0:T(8,128)(2,1)S(1)}, u32[]{:S(2)}, u32[]{:S(2)}) %collective-permute-start.21) | collective-permute-done | bytes 393248 | tf_op jit(solution)/shard_map/ppermute | solution.py:25
  119.7 1.7 collective-permute-start.22
  121.4 9.5 %collective-permute-done.23 = bf16[2,24,4096]{2,1,0:T(8,128)(2,1)S(1)} collective-permute-done((bf16[2,24,4096]{2,1,0:T(8,128)(2,1)S(1)}, bf16[2,24,4096]{2,1,0:T(8,128)(2,1)S(1)}, u32[]{:S(2)}, u32[]{:S(2)}) %collective-permute-start.23) | collective-permute-done | bytes 393248 | tf_op jit(solution)/shard_map/ppermute | solution.py:25
  131.1 1.7 collective-permute-start.25
  133.6 6.1 %collective-permute-done.26 = bf16[2,24,4096]{2,1,0:T(8,128)(2,1)S(1)} collective-permute-done((bf16[2,24,4096]{2,1,0:T(8,128)(2,1)S(1)}, bf16[2,24,4096]{2,1,0:T(8,128)(2,1)S(1)}, u32[]{:S(2)}, u32[]{:S(2)}) %collective-permute-start.26) | collective-permute-done | bytes 393248 | tf_op jit(solution)/shard_map/ppermute | solution.py:25
  140.1 2.0 %collective-permute-start.27 = (bf16[2,24,2048]{2,1,0:T(8,128)(2,1)S(1)}, bf16[2,24,2048]{2,1,0:T(8,128)(2,1)S(1)}, u32[]{:S(2)}, u32[]{:S(2)}) collective-permute-start(bf16[2,24,2048]{2,1,0:T(8,128)(2,1)S(1)} %slice.109), channel_id=1, source_target_pairs={{0,4},{1,5},{4,8},{5,9},{8,12},{9,13},{12,14},{13,15},{14,10},{15,... | collective-permute-start | bytes 589832 | tf_op jit(solution)/shard_map/ppermute | solution.py:25
  142.9 2.6 %collective-permute-done.28 = bf16[2,24,2048]{2,1,0:T(8,128)(2,1)S(1)} collective-permute-done((bf16[2,24,2048]{2,1,0:T(8,128)(2,1)S(1)}, bf16[2,24,2048]{2,1,0:T(8,128)(2,1)S(1)}, u32[]{:S(2)}, u32[]{:S(2)}) %collective-permute-start.28) | collective-permute-done | bytes 196640 | tf_op jit(solution)/shard_map/ppermute | solution.py:25
  146.1 1.7 fusion.56
  151.1 1.4 copy.19
  152.6 1.4 copy.20
  154.0 1.3 copy.21
  156.6 1.4 copy.24
  159.3 1.3 copy.26
  163.3 11.4 %concatenate.42 = bf16[384,4096]{0,1:T(8,128)(2,1)S(1)} concatenate(bf16[24,4096]{0,1:T(8,128)(2,1)} %copy.18, bf16[24,4096]{0,1:T(8,128)(2,1)} %copy.19, bf16[24,4096]{0,1:T(8,128)(2,1)} %copy.20, bf16[24,4096]{0,1:T(8,128)(2,1)} %copy.21, bf16[24,4096]{0,1:T(8,128)(2,1)} %copy.22, bf16[120,4096]{0,1:T(8,128)(2,1)} %copy.23, bf16[24,4096]{0,1:T(8,128)(2,1)} %copy.24, ...), dimensions={0} | concatenate | bytes 6291456 | tf_op jit(solution)/shard_map/concatenate | solution.py:139
  174.7 1.8 pad_maximum_fusion.1
  176.7 5.2 %fusion = f32[2,144,1024]{2,1,0:T(8,128)S(1)} fusion(bf16[2,144,4096]{2,1,0:T(8,128)(2,1)S(1)} %bitcast.120, bf16[1024,4096]{1,0:T(8,128)(2,1)} %param.10), kind=kOutput, calls=%fused_computation | convolution fusion | flops 2415919104 | bytes 11927552 | tf_op jit(solution)/shard_map/dot_general | solution.py:135
  182.4 2.6 %pad_maximum_fusion = bf16[2,2,120,4096]{3,2,0,1:T(8,128)(2,1)S(1)} fusion(bf16[2,1,120,4096]{3,2,0,1:T(8,128)(2,1)} %bitcast.18, bf16[2,1,120,4096]{3,2,0,1:T(8,128)(2,1)} %bitcast.17), kind=kLoop, calls=%fused_computation.7 | loop fusion | flops 1966080 | bytes 7864320 | tf_op jit(solution)/shard_map/stack | solution.py:133
  185.8 1.7 slice-done.11
  187.5 4.3 %fusion.2 = f32[2,240,1024]{2,1,0:T(8,128)S(1)} fusion(bf16[2,240,4096]{2,1,0:T(8,128)(2,1)S(1)} %bitcast.117, bf16[1024,4096]{1,0:T(8,128)(2,1)S(1)} %bitcast.132), kind=kOutput, calls=%fused_computation.2 | convolution fusion | flops 4026531840 | bytes 14286848 | tf_op jit(solution)/shard_map/dot_general | solution.py:135
  192.5 7.4 %outer.1 = bf16[4096,1024]{1,0:T(8,128)(2,1)} custom-call(bf16[4096,384]{1,0:T(8,128)(2,1)S(1)} %bitcast.114, bf16[384,1024]{1,0:T(8,128)(2,1)S(1)} %pad_maximum_fusion.3.refs_1_), custom_call_target="tpu_custom_call" | custom-call | flops 3221225472 | bytes 12320768 | tf_op jit(solution)/shard_map/outer/pallas_call | solution.py:76
  (127 shorter events, 26.5 us)
Async XLA Ops:
  0.0 8.1 %collective-permute-start = (bf16[24,4096]{1,0:T(8,128)(2,1)}, bf16[24,4096]{1,0:T(8,128)(2,1)S(1)}, u32[]{:S(2)}, u32[]{:S(2)}) collective-permute-start(bf16[24,4096]{1,0:T(8,128)(2,1)} %param.6), channel_id=1, source_target_pairs={{0,4},{1,5},{4,8},{5,9},{8,12},{9,13},{12,14},{13,15},{14,10},{15,... | collective-permute-start | bytes 589832 | tf_op jit(solution)/shard_map/ppermute | solution.py:25
  3.0 7.8 %collective-permute-start.1 = (bf16[24,4096]{1,0:T(8,128)(2,1)}, bf16[24,4096]{1,0:T(8,128)(2,1)S(1)}, u32[]{:S(2)}, u32[]{:S(2)}) collective-permute-start(bf16[24,4096]{1,0:T(8,128)(2,1)} %param.6), channel_id=1, source_target_pairs={{4,0},{5,1},{8,4},{9,5},{12,8},{13,9},{14,12},{15,13},{10,14},{11,... | collective-permute-start | bytes 589832 | tf_op jit(solution)/shard_map/ppermute | solution.py:25
  8.1 6.1 %collective-permute-start.2 = (bf16[24,4096]{1,0:T(8,128)(2,1)S(1)}, bf16[24,4096]{1,0:T(8,128)(2,1)S(1)}, u32[]{:S(2)}, u32[]{:S(2)}) collective-permute-start(bf16[24,4096]{1,0:T(8,128)(2,1)S(1)} %collective-permute-done), channel_id=1, source_target_pairs={{0,4},{1,5},{4,8},{5,9},{8,12},{9,13},{12,14},{13,15},{14,10},{15,... | collective-permute-start | bytes 589832 | tf_op jit(solution)/shard_map/ppermute | solution.py:25
  10.8 5.7 %collective-permute-start.3 = (bf16[24,4096]{1,0:T(8,128)(2,1)S(1)}, bf16[24,4096]{1,0:T(8,128)(2,1)S(1)}, u32[]{:S(2)}, u32[]{:S(2)}) collective-permute-start(bf16[24,4096]{1,0:T(8,128)(2,1)S(1)} %collective-permute-done.1), channel_id=1, source_target_pairs={{4,0},{5,1},{8,4},{9,5},{12,8},{13,9},{14,12},{15,13},{10,14},{11,... | collective-permute-start | bytes 589832 | tf_op jit(solution)/shard_map/ppermute | solution.py:25
  14.2 5.7 %collective-permute-start.5 = (bf16[24,4096]{1,0:T(8,128)(2,1)S(1)}, bf16[24,4096]{1,0:T(8,128)(2,1)S(1)}, u32[]{:S(2)}, u32[]{:S(2)}) collective-permute-start(bf16[24,4096]{1,0:T(8,128)(2,1)S(1)} %collective-permute-done.2), channel_id=1, source_target_pairs={{0,4},{1,5},{4,8},{5,9},{8,12},{9,13},{12,14},{13,15},{14,10},{15,... | collective-permute-start | bytes 589832 | tf_op jit(solution)/shard_map/ppermute | solution.py:25
  16.6 6.1 %collective-permute-start.6 = (bf16[24,4096]{1,0:T(8,128)(2,1)S(1)}, bf16[24,4096]{1,0:T(8,128)(2,1)S(1)}, u32[]{:S(2)}, u32[]{:S(2)}) collective-permute-start(bf16[24,4096]{1,0:T(8,128)(2,1)S(1)} %collective-permute-done.3), channel_id=1, source_target_pairs={{4,0},{5,1},{8,4},{9,5},{12,8},{13,9},{14,12},{15,13},{10,14},{11,... | collective-permute-start | bytes 589832 | tf_op jit(solution)/shard_map/ppermute | solution.py:25
  19.9 4.7 %collective-permute-start.7 = (bf16[24,2048]{1,0:T(8,128)(2,1)S(1)}, bf16[24,2048]{1,0:T(8,128)(2,1)S(1)}, u32[]{:S(2)}, u32[]{:S(2)}) collective-permute-start(bf16[24,2048]{1,0:T(8,128)(2,1)S(1)} %slice.91), channel_id=1, source_target_pairs={{0,4},{1,5},{4,8},{5,9},{8,12},{9,13},{12,14},{13,15},{14,10},{15,... | collective-permute-start | bytes 294920 | tf_op jit(solution)/shard_map/ppermute | solution.py:25
  22.7 4.7 %collective-permute-start.8 = (bf16[24,2048]{1,0:T(8,128)(2,1)S(1)}, bf16[24,2048]{1,0:T(8,128)(2,1)S(1)}, u32[]{:S(2)}, u32[]{:S(2)}) collective-permute-start(bf16[24,2048]{1,0:T(8,128)(2,1)S(1)} %slice.92), channel_id=1, source_target_pairs={{4,0},{5,1},{8,4},{9,5},{12,8},{13,9},{14,12},{15,13},{10,14},{11,... | collective-permute-start | bytes 294920 | tf_op jit(solution)/shard_map/ppermute | solution.py:25
  27.4 2.1 %collective-permute-start.9 = (bf16[72,4096]{1,0:T(8,128)(2,1)S(1)}, bf16[72,4096]{1,0:T(8,128)(2,1)S(1)}, u32[]{:S(2)}, u32[]{:S(2)}) collective-permute-start(bf16[72,4096]{1,0:T(8,128)(2,1)S(1)} %pad_maximum_fusion.4), channel_id=1, source_target_pairs={{0,1},{1,0},{2,3},{3,2},{4,5},{5,4},{6,7},{7,6},{8,9},{9,8},{10,11... | collective-permute-start | bytes 1769480 | tf_op jit(solution)/shard_map/ppermute | solution.py:25
  27.5 9.0 %slice-start.4 = ((s8[8388608]{0:T(1024)(128)(4,1)}), s8[4194304]{0:T(1024)(128)(4,1)S(1)}, s32[]{:S(2)}) async-start(s8[8388608]{0:T(1024)(128)(4,1)} %bitcast.125), calls=%async_computation.4 | async-start | bytes 8388608
  27.6 7.5 %slice-start = ((s8[8388608]{0:T(1024)(128)(4,1)}), s8[4194304]{0:T(1024)(128)(4,1)S(1)}, s32[]{:S(2)}) async-start(s8[8388608]{0:T(1024)(128)(4,1)} %bitcast.121), calls=%async_computation | async-start | bytes 8388608
  27.6 7.4 %slice-start.1 = ((s8[8388608]{0:T(1024)(128)(4,1)}), s8[4194304]{0:T(1024)(128)(4,1)S(1)}, s32[]{:S(2)}) async-start(s8[8388608]{0:T(1024)(128)(4,1)} %bitcast.121), calls=%async_computation.1 | async-start | bytes 8388608
  27.6 8.9 %slice-start.5 = ((s8[8388608]{0:T(1024)(128)(4,1)}), s8[4194304]{0:T(1024)(128)(4,1)S(1)}, s32[]{:S(2)}) async-start(s8[8388608]{0:T(1024)(128)(4,1)} %bitcast.125), calls=%async_computation.5 | async-start | bytes 8388608
  27.6 14.5 %collective-permute-start.4 = (bf16[120,4096]{1,0:T(8,128)(2,1)S(1)}, bf16[120,4096]{1,0:T(8,128)(2,1)S(1)}, u32[]{:S(2)}, u32[]{:S(2)}) collective-permute-start(bf16[120,4096]{1,0:T(8,128)(2,1)S(1)} %get-tuple-element.20), channel_id=1, source_target_pairs={{0,1},{1,0},{2,3},{3,2},{4,5},{5,4},{6,7},{7,6},{8,9},{9,8},{10,11... | collective-permute-start | bytes 2949128 | tf_op jit(solution)/shard_map/ppermute | solution.py:25
  35.0 4.0 %slice-start.6 = ((s8[8388608]{0:T(1024)(128)(4,1)}), s8[4194304]{0:T(1024)(128)(4,1)S(1)}, s32[]{:S(2)}) async-start(s8[8388608]{0:T(1024)(128)(4,1)} %bitcast.127), calls=%async_computation.6 | async-start | bytes 8388608
  42.0 18.4 %collective-permute-start.11 = (bf16[2,3,24,4096]{3,2,0,1:T(8,128)(2,1)S(1)}, bf16[2,3,24,4096]{3,2,0,1:T(8,128)(2,1)S(1)}, u32[]{:S(2)}, u32[]{:S(2)}) collective-permute-start(bf16[2,3,24,4096]{3,2,0,1:T(8,128)(2,1)S(1)} %fusion.7), channel_id=1, source_target_pairs={{0,1},{1,0},{2,3},{3,2},{4,5},{5,4},{6,7},{7,6},{8,9},{9,8},{10,11... | collective-permute-start | bytes 3538952 | tf_op jit(solution)/shard_map/ppermute | solution.py:25
  42.2 3.4 %slice-start.3 = ((s8[8388608]{0:T(1024)(128)(4,1)}), s8[4194304]{0:T(1024)(128)(4,1)S(1)}, s32[]{:S(2)}) async-start(s8[8388608]{0:T(1024)(128)(4,1)} %bitcast.123), calls=%async_computation.3 | async-start | bytes 8388608
  45.6 9.7 %slice-start.8 = ((s8[8388608]{0:T(1024)(128)(4,1)}), s8[4194304]{0:T(1024)(128)(4,1)S(1)}, s32[]{:S(2)}) async-start(s8[8388608]{0:T(1024)(128)(4,1)} %bitcast.129), calls=%async_computation.8 | async-start | bytes 8388608
  47.9 7.3 %copy-start.2 = (f32[240,1024]{1,0:T(8,128)}, f32[240,1024]{1,0:T(8,128)S(1)}, u32[]{:S(2)}) copy-start(f32[240,1024]{1,0:T(8,128)S(1)} %convolution_multiply_fusion) | copy-start | bytes 2949124
  48.0 7.3 %slice-start.9 = ((s8[8388608]{0:T(1024)(128)(4,1)}), s8[4194304]{0:T(1024)(128)(4,1)S(1)}, s32[]{:S(2)}) async-start(s8[8388608]{0:T(1024)(128)(4,1)} %bitcast.129), calls=%async_computation.9 | async-start | bytes 8388608
  59.9 11.3 %collective-permute-start.10 = (bf16[2,5,24,4096]{3,2,0,1:T(8,128)(2,1)S(1)}, bf16[2,5,24,4096]{3,2,0,1:T(8,128)(2,1)S(1)}, u32[]{:S(2)}, u32[]{:S(2)}) collective-permute-start(bf16[2,5,24,4096]{3,2,0,1:T(8,128)(2,1)S(1)} %fusion.6), channel_id=1, source_target_pairs={{0,1},{1,0},{2,3},{3,2},{4,5},{5,4},{6,7},{7,6},{8,9},{9,8},{10,11... | collective-permute-start | bytes 5898248 | tf_op jit(solution)/shard_map/ppermute | solution.py:25
  60.7 7.0 %collective-permute-start.12 = (bf16[2,24,2048]{2,1,0:T(8,128)(2,1)S(1)}, bf16[2,24,2048]{2,1,0:T(8,128)(2,1)S(1)}, u32[]{:S(2)}, u32[]{:S(2)}) collective-permute-start(bf16[2,24,2048]{2,1,0:T(8,128)(2,1)S(1)} %get-tuple-element.17), channel_id=1, source_target_pairs={{0,4},{1,5},{4,8},{5,9},{8,12},{9,13},{12,14},{13,15},{14,10},{15,... | collective-permute-start | bytes 589832 | tf_op jit(solution)/shard_map/ppermute | solution.py:25
  62.4 6.6 %collective-permute-start.16 = (bf16[2,24,2048]{2,1,0:T(8,128)(2,1)S(1)}, bf16[2,24,2048]{2,1,0:T(8,128)(2,1)S(1)}, u32[]{:S(2)}, u32[]{:S(2)}) collective-permute-start(bf16[2,24,2048]{2,1,0:T(8,128)(2,1)S(1)} %get-tuple-element.18), channel_id=1, source_target_pairs={{4,0},{5,1},{8,4},{9,5},{12,8},{13,9},{14,12},{15,13},{10,14},{11,... | collective-permute-start | bytes 589832 | tf_op jit(solution)/shard_map/ppermute | solution.py:25
  69.1 10.0 %collective-permute-start.13 = (bf16[2,24,4096]{2,1,0:T(8,128)(2,1)S(1)}, bf16[2,24,4096]{2,1,0:T(8,128)(2,1)S(1)}, u32[]{:S(2)}, u32[]{:S(2)}) collective-permute-start(bf16[2,24,4096]{2,1,0:T(8,128)(2,1)S(1)} %get-tuple-element.7), channel_id=1, source_target_pairs={{0,4},{1,5},{4,8},{5,9},{8,12},{9,13},{12,14},{13,15},{14,10},{15,... | collective-permute-start | bytes 1179656 | tf_op jit(solution)/shard_map/ppermute | solution.py:25
  70.8 10.1 %collective-permute-start.17 = (bf16[2,24,4096]{2,1,0:T(8,128)(2,1)S(1)}, bf16[2,24,4096]{2,1,0:T(8,128)(2,1)S(1)}, u32[]{:S(2)}, u32[]{:S(2)}) collective-permute-start(bf16[2,24,4096]{2,1,0:T(8,128)(2,1)S(1)} %get-tuple-element.8), channel_id=1, source_target_pairs={{4,0},{5,1},{8,4},{9,5},{12,8},{13,9},{14,12},{15,13},{10,14},{11,... | collective-permute-start | bytes 1179656 | tf_op jit(solution)/shard_map/ppermute | solution.py:25
  79.2 9.1 %collective-permute-start.14 = (bf16[2,24,4096]{2,1,0:T(8,128)(2,1)S(1)}, bf16[2,24,4096]{2,1,0:T(8,128)(2,1)S(1)}, u32[]{:S(2)}, u32[]{:S(2)}) collective-permute-start(bf16[2,24,4096]{2,1,0:T(8,128)(2,1)S(1)} %fusion.30), channel_id=1, source_target_pairs={{0,4},{1,5},{4,8},{5,9},{8,12},{9,13},{12,14},{13,15},{14,10},{15,... | collective-permute-start | bytes 1179656 | tf_op jit(solution)/shard_map/ppermute | solution.py:25
  88.5 18.5 %copy-start.11 = (bf16[24,4096]{1,0:T(8,128)(2,1)S(1)}, bf16[24,4096]{1,0:T(8,128)(2,1)}, u32[]{:S(2)}) copy-start(bf16[24,4096]{1,0:T(8,128)(2,1)} %param.7) | copy-start | bytes 589828
  88.5 9.2 %collective-permute-start.18 = (bf16[2,24,4096]{2,1,0:T(8,128)(2,1)S(1)}, bf16[2,24,4096]{2,1,0:T(8,128)(2,1)S(1)}, u32[]{:S(2)}, u32[]{:S(2)}) collective-permute-start(bf16[2,24,4096]{2,1,0:T(8,128)(2,1)S(1)} %get-tuple-element.6), channel_id=1, source_target_pairs={{4,0},{5,1},{8,4},{9,5},{12,8},{13,9},{14,12},{15,13},{10,14},{11,... | collective-permute-start | bytes 1179656 | tf_op jit(solution)/shard_map/ppermute | solution.py:25
  88.9 9.3 %collective-permute-start.15 = (bf16[2,24,4096]{2,1,0:T(8,128)(2,1)S(1)}, bf16[2,24,4096]{2,1,0:T(8,128)(2,1)S(1)}, u32[]{:S(2)}, u32[]{:S(2)}) collective-permute-start(bf16[2,24,4096]{2,1,0:T(8,128)(2,1)S(1)} %get-tuple-element.5), channel_id=1, source_target_pairs={{0,4},{1,5},{4,8},{5,9},{8,12},{9,13},{12,14},{13,15},{14,10},{15,... | collective-permute-start | bytes 1179656 | tf_op jit(solution)/shard_map/ppermute | solution.py:25
  97.8 9.1 %collective-permute-start.19 = (bf16[2,24,4096]{2,1,0:T(8,128)(2,1)S(1)}, bf16[2,24,4096]{2,1,0:T(8,128)(2,1)S(1)}, u32[]{:S(2)}, u32[]{:S(2)}) collective-permute-start(bf16[2,24,4096]{2,1,0:T(8,128)(2,1)S(1)} %fusion.26), channel_id=1, source_target_pairs={{4,0},{5,1},{8,4},{9,5},{12,8},{13,9},{14,12},{15,13},{10,14},{11,... | collective-permute-start | bytes 1179656 | tf_op jit(solution)/shard_map/ppermute | solution.py:25
  107.8 11.2 %collective-permute-start.21 = (bf16[2,24,4096]{2,1,0:T(8,128)(2,1)S(1)}, bf16[2,24,4096]{2,1,0:T(8,128)(2,1)S(1)}, u32[]{:S(2)}, u32[]{:S(2)}) collective-permute-start(bf16[2,24,4096]{2,1,0:T(8,128)(2,1)S(1)} %get-tuple-element.16), channel_id=1, source_target_pairs={{4,0},{5,1},{8,4},{9,5},{12,8},{13,9},{14,12},{15,13},{10,14},{11,... | collective-permute-start | bytes 1179656 | tf_op jit(solution)/shard_map/ppermute | solution.py:25
  108.2 11.5 %collective-permute-start.20 = (bf16[2,24,4096]{2,1,0:T(8,128)(2,1)S(1)}, bf16[2,24,4096]{2,1,0:T(8,128)(2,1)S(1)}, u32[]{:S(2)}, u32[]{:S(2)}) collective-permute-start(bf16[2,24,4096]{2,1,0:T(8,128)(2,1)S(1)} %get-tuple-element.16), channel_id=1, source_target_pairs={{0,4},{1,5},{4,8},{5,9},{8,12},{9,13},{12,14},{13,15},{14,10},{15,... | collective-permute-start | bytes 1179656 | tf_op jit(solution)/shard_map/ppermute | solution.py:25
  119.0 11.8 %collective-permute-start.23 = (bf16[2,24,4096]{2,1,0:T(8,128)(2,1)S(1)}, bf16[2,24,4096]{2,1,0:T(8,128)(2,1)S(1)}, u32[]{:S(2)}, u32[]{:S(2)}) collective-permute-start(bf16[2,24,4096]{2,1,0:T(8,128)(2,1)S(1)} %collective-permute-done.21), channel_id=1, source_target_pairs={{4,0},{5,1},{8,4},{9,5},{12,8},{13,9},{14,12},{15,13},{10,14},{11,... | collective-permute-start | bytes 1179656 | tf_op jit(solution)/shard_map/ppermute | solution.py:25
  119.7 11.4 %collective-permute-start.22 = (bf16[2,24,4096]{2,1,0:T(8,128)(2,1)S(1)}, bf16[2,24,4096]{2,1,0:T(8,128)(2,1)S(1)}, u32[]{:S(2)}, u32[]{:S(2)}) collective-permute-start(bf16[2,24,4096]{2,1,0:T(8,128)(2,1)S(1)} %collective-permute-done.20), channel_id=1, source_target_pairs={{0,4},{1,5},{4,8},{5,9},{8,12},{9,13},{12,14},{13,15},{14,10},{15,... | collective-permute-start | bytes 1179656 | tf_op jit(solution)/shard_map/ppermute | solution.py:25
  130.8 8.9 %collective-permute-start.26 = (bf16[2,24,4096]{2,1,0:T(8,128)(2,1)S(1)}, bf16[2,24,4096]{2,1,0:T(8,128)(2,1)S(1)}, u32[]{:S(2)}, u32[]{:S(2)}) collective-permute-start(bf16[2,24,4096]{2,1,0:T(8,128)(2,1)S(1)} %collective-permute-done.23), channel_id=1, source_target_pairs={{4,0},{5,1},{8,4},{9,5},{12,8},{13,9},{14,12},{15,13},{10,14},{11,... | collective-permute-start | bytes 1179656 | tf_op jit(solution)/shard_map/ppermute | solution.py:25
  131.1 9.0 %collective-permute-start.25 = (bf16[2,24,4096]{2,1,0:T(8,128)(2,1)S(1)}, bf16[2,24,4096]{2,1,0:T(8,128)(2,1)S(1)}, u32[]{:S(2)}, u32[]{:S(2)}) collective-permute-start(bf16[2,24,4096]{2,1,0:T(8,128)(2,1)S(1)} %collective-permute-done.22), channel_id=1, source_target_pairs={{0,4},{1,5},{4,8},{5,9},{8,12},{9,13},{12,14},{13,15},{14,10},{15,... | collective-permute-start | bytes 1179656 | tf_op jit(solution)/shard_map/ppermute | solution.py:25
  139.8 5.7 %collective-permute-start.28 = (bf16[2,24,2048]{2,1,0:T(8,128)(2,1)S(1)}, bf16[2,24,2048]{2,1,0:T(8,128)(2,1)S(1)}, u32[]{:S(2)}, u32[]{:S(2)}) collective-permute-start(bf16[2,24,2048]{2,1,0:T(8,128)(2,1)S(1)} %slice.110), channel_id=1, source_target_pairs={{4,0},{5,1},{8,4},{9,5},{12,8},{13,9},{14,12},{15,13},{10,14},{11,... | collective-permute-start | bytes 589832 | tf_op jit(solution)/shard_map/ppermute | solution.py:25
  140.1 5.9 %collective-permute-start.27 = (bf16[2,24,2048]{2,1,0:T(8,128)(2,1)S(1)}, bf16[2,24,2048]{2,1,0:T(8,128)(2,1)S(1)}, u32[]{:S(2)}, u32[]{:S(2)}) collective-permute-start(bf16[2,24,2048]{2,1,0:T(8,128)(2,1)S(1)} %slice.109), channel_id=1, source_target_pairs={{0,4},{1,5},{4,8},{5,9},{8,12},{9,13},{12,14},{13,15},{14,10},{15,... | collective-permute-start | bytes 589832 | tf_op jit(solution)/shard_map/ppermute | solution.py:25
  142.9 6.9 %copy-start.5 = (bf16[24,4096]{1,0:T(8,128)(2,1)S(1)}, bf16[24,4096]{1,0:T(8,128)(2,1)}, u32[]{:S(2)}) copy-start(bf16[24,4096]{1,0:T(8,128)(2,1)} %param.6) | copy-start | bytes 589828
  147.8 26.9 %collective-permute-start.29 = (bf16[2,72,4096]{2,1,0:T(8,128)(2,1)}, bf16[2,72,4096]{2,1,0:T(8,128)(2,1)}, u32[]{:S(2)}, u32[]{:S(2)}) collective-permute-start(bf16[2,72,4096]{2,1,0:T(8,128)(2,1)} %get-tuple-element.12), channel_id=1, source_target_pairs={{0,1},{1,0},{2,3},{3,2},{4,5},{5,4},{6,7},{7,6},{8,9},{9,8},{10,11... | collective-permute-start | bytes 3538952 | tf_op jit(solution)/shard_map/ppermute | solution.py:25
  149.3 33.1 %collective-permute-start.24 = (bf16[2,120,4096]{2,1,0:T(8,128)(2,1)}, bf16[2,120,4096]{2,1,0:T(8,128)(2,1)}, u32[]{:S(2)}, u32[]{:S(2)}) collective-permute-start(bf16[2,120,4096]{2,1,0:T(8,128)(2,1)} %constant_dynamic-update-slice_fusion.13), channel_id=1, source_target_pairs={{0,1},{1,0},{2,3},{3,2},{4,5},{5,4},{6,7},{7,6},{8,9},{9,8},{10,11... | collective-permute-start | bytes 5898248 | tf_op jit(solution)/shard_map/ppermute | solution.py:25
  176.7 5.2 %copy-start.7 = (f32[144,1024]{1,0:T(8,128)S(1)}, f32[144,1024]{1,0:T(8,128)}, u32[]{:S(2)}) copy-start(f32[144,1024]{1,0:T(8,128)} %copy-done.6) | copy-start | bytes 1769476
  176.7 5.2 %copy-start.9 = (f32[144,1024]{1,0:T(8,128)S(1)}, f32[144,1024]{1,0:T(8,128)}, u32[]{:S(2)}) copy-start(f32[144,1024]{1,0:T(8,128)} %copy-done.8) | copy-start | bytes 1769476
  176.7 5.2 %copy-start.10 = (f32[144,1024]{1,0:T(8,128)S(1)}, f32[144,1024]{1,0:T(8,128)}, u32[]{:S(2)}) copy-start(f32[144,1024]{1,0:T(8,128)} %get-tuple-element.30) | copy-start | bytes 1769476
  182.4 3.4 %slice-start.10 = ((s8[8388608]{0:T(1024)(128)(4,1)}), s8[4194304]{0:T(1024)(128)(4,1)S(1)}, s32[]{:S(2)}) async-start(s8[8388608]{0:T(1024)(128)(4,1)} %bitcast.131), calls=%async_computation.10 | async-start | bytes 8388608
  187.4 4.3 %copy-start.1 = (f32[240,1024]{1,0:T(8,128)S(1)}, f32[240,1024]{1,0:T(8,128)}, u32[]{:S(2)}) copy-start(f32[240,1024]{1,0:T(8,128)} %copy-done) | copy-start | bytes 2949124
  187.4 4.3 %copy-start.3 = (f32[240,1024]{1,0:T(8,128)S(1)}, f32[240,1024]{1,0:T(8,128)}, u32[]{:S(2)}) copy-start(f32[240,1024]{1,0:T(8,128)} %copy-done.2) | copy-start | bytes 2949124
  187.4 4.3 %copy-start.4 = (f32[240,1024]{1,0:T(8,128)S(1)}, f32[240,1024]{1,0:T(8,128)}, u32[]{:S(2)}) copy-start(f32[240,1024]{1,0:T(8,128)} %get-tuple-element.29) | copy-start | bytes 2949124
  (6 other events, 13.6 us)

commit v2 on v0

v2 whole, which is shorter than its diff:
```python
import functools

import jax
import jax.numpy as jnp
from jax import lax
from jax.experimental import pallas as pl
from jax.experimental.pallas import tpu as pltpu
from jax.sharding import PartitionSpec as P

AXIS = "tensor"
F32, BF16 = jnp.float32, jnp.bfloat16
MIB = 2**20
IN_VMEM = pl.BlockSpec(memory_space=pltpu.VMEM)
IN_SMEM = pl.BlockSpec(memory_space=pltpu.SMEM)


def ring_routes(devices):
    chips = devices // 2
    cycle = list(range(0, chips, 2)) + list(range(1, chips, 2))[::-1]
    onward, backward = [], []
    for place, chip in enumerate(cycle):
        following = cycle[(place + 1) % chips]
        for core in range(2):
            onward.append((chip * 2 + core, following * 2 + core))
            backward.append((following * 2 + core, chip * 2 + core))
    partner = [(device, device ^ 1) for device in range(devices)]
    return onward, backward, partner


def send(block, route):
    return lax.ppermute(block, AXIS, route)


def tie(*arrays):
    return lax.optimization_barrier(arrays)


def call(kernel, name, core, outs, scratch, flops, operands, from_hbm=()):
    limit = 6 * MIB + sum(4 * shape[0] * shape[1] for shape in scratch)
    semaphores = [pltpu.SemaphoreType.DMA((1,))] if from_hbm else []
    return pl.pallas_call(
        kernel,
        in_specs=[IN_SMEM]
        + [IN_VMEM] * len(operands)
        + [pl.BlockSpec(memory_space=pltpu.HBM)] * len(from_hbm),
        out_specs=[IN_VMEM] * len(outs),
        out_shape=[pltpu.VMEM(shape, kind) for shape, kind in outs],
        scratch_shapes=[pltpu.VMEM(shape, F32) for shape in scratch] + semaphores,
        compiler_params=pltpu.CompilerParams(vmem_limit_bytes=limit),
        cost_estimate=pl.CostEstimate(
            flops=flops, bytes_accessed=sum(x.size * 2 for x in operands), transcendentals=0
        ),
        name=name,
    )(core, *[in_vmem(x) for x in operands], *[in_hbm(x) for x in from_hbm])


def in_hbm(x):
    return pltpu.with_memory_space_constraint(x, pltpu.HBM)


def in_vmem(x):
    return pltpu.with_memory_space_constraint(x, pltpu.VMEM)


def fetch(weights, after):
    count = len(weights)

    def kernel(after_ref, *refs):
        copies = [
            pltpu.make_async_copy(refs[i], refs[count + i], refs[-1].at[i]) for i in range(count)
        ]
        for copy in copies:
            copy.start()
        for copy in copies:
            copy.wait()

    return pl.pallas_call(
        kernel,
        in_specs=[pl.BlockSpec(memory_space=pl.ANY)] + [pl.BlockSpec(memory_space=pltpu.HBM)] * count,
        out_specs=[IN_VMEM] * count,
        out_shape=[pltpu.VMEM(w.shape, w.dtype) for w in weights],
        scratch_shapes=[pltpu.SemaphoreType.DMA((count,))],
        compiler_params=pltpu.CompilerParams(vmem_limit_bytes=MIB),
        cost_estimate=pl.CostEstimate(
            flops=0, bytes_accessed=sum(2 * w.size for w in weights), transcendentals=0
        ),
        name="fetch",
    )(after, *[in_hbm(w) for w in weights])


def passes(core, half, tile):
    for own in (True, False):
        start = (core if own else 1 - core) * half
        for k in range(0, half, tile):
            yield own, slice(k, k + tile), pl.ds(pl.multiple_of(start + k, tile), tile)


def forward(core, same, other, weights, late=None, beside=None):
    count, rows = len(same), same[0].shape[0]
    total = count * rows
    depth, columns = weights[0].shape
    known = len(weights)
    coming = [w for w in (late, beside) if w is not None]

    def kernel(core_ref, *refs):
        blocks, refs = refs[: 2 * count], refs[2 * count :]
        weight_refs, refs = list(refs[:known]), refs[known:]
        source, refs = refs[: len(coming)], refs[len(coming) :]
        (hidden_ref, by_dot_ref, by_error_ref), refs = refs[:3], refs[3:]
        arriving, refs = refs[: len(coming)], refs[len(coming) :]
        sums = refs[:3]
        if coming:
            copy = pltpu.make_async_copy(source[0], arriving[0], refs[3].at[0])
            copy.start()
            if late is not None:
                weight_refs.append(arriving[0])

        def add(some):
            for own, near, at in passes(core_ref[0], depth // 2, 1024):
                part = blocks[:count] if own else blocks[count:]
                left = jnp.concatenate([b[:, near] for b in part])
                for s, w in some:
                    product = jnp.dot(left, w[at, :], preferred_element_type=F32)
                    if own and near.start == 0:
                        s[...] = product
                    else:
                        s[...] += product

        pairs = list(zip(sums, weight_refs))
        add(pairs[:known])
        if coming:
            copy.wait()
        if late is not None:
            add(pairs[known:])
        for b in range(count):
            at = slice(b * rows, (b + 1) * rows)
            preact, linear = sums[0][at, :], sums[1][at, :]
            tangent = sums[2][at, :] * depth ** (-0.5)
            logistic = jax.nn.sigmoid(preact)
            slopes = logistic * (1.0 + preact * (1.0 - logistic))
            curvature = logistic * (1.0 - logistic) * (2.0 + preact * (1.0 - 2.0 * logistic))
            by_dot = linear * slopes
            by_dot_ref[at, :] = by_dot
            by_error_ref[at, :] = linear * curvature * tangent
            hidden_ref[2 * b * rows : (2 * b + 1) * rows, :] = (preact * logistic * linear).astype(BF16)
            hidden_ref[(2 * b + 1) * rows : (2 * b + 2) * rows, :] = (by_dot * tangent).astype(BF16)

    return call(
        kernel,
        "forward",
        core,
        [((2 * total, columns), BF16), ((total, columns), F32), ((total, columns), F32)]
        + [(w.shape, w.dtype) for w in coming],
        [(total, columns)] * 3,
        6 * total * depth * columns,
        [*same, *other, *weights],
        coming,
    )


def down(core, hidden, down_weight, both=True, own_half=True):
    total = sum(h.shape[0] for h in hidden)
    depth, columns = down_weight.shape
    half = columns // 2
    places = 2 if both else 1

    def kernel(core_ref, *refs):
        hidden_refs, weight_ref, out_refs = refs[: len(hidden)], refs[len(hidden)], refs[len(hidden) + 1 :]
        left = jnp.concatenate([h[...] for h in hidden_refs])
        first = core_ref[0] if own_half and not both else 1 - core_ref[0]
        for mine, near, at in passes(first, half, 1024):
            if mine or both:
                product = jnp.dot(left, weight_ref[:, at], preferred_element_type=F32)
                out_refs[0 if mine else 1][:, near] = product.astype(BF16)

    return call(
        kernel,
        "down",
        core,
        [((total, half), BF16)] * places,
        [],
        places * total * depth * columns,
        [*hidden, down_weight],
    )


def back(core, same, other, down_weight, by_dot, by_error):
    count, rows = len(same), same[0].shape[0]
    total = count * rows
    columns, depth = down_weight.shape
    parts = len(by_dot)

    def kernel(core_ref, *refs):
        blocks, refs = refs[: 2 * count], refs[2 * count :]
        weight_ref, by_dot_refs, by_error_refs = refs[0], refs[1 : 1 + parts], refs[1 + parts : -2]
        out_ref, sum_ref = refs[-2:]
        for own, near, at in passes(core_ref[0], depth // 2, 1024):
            left = jnp.concatenate([b[:, near] for b in (blocks[:count] if own else blocks[count:])])
            product = lax.dot_general(
                left, weight_ref[:, at], (((1,), (1,)), ((), ())), preferred_element_type=F32
            )
            if own and near.start == 0:
                sum_ref[...] = product
            else:
                sum_ref[...] += product
        half = rows // 2
        b = 0
        for by_dot_ref, by_error_ref in zip(by_dot_refs, by_error_refs):
            for start in range(0, by_dot_ref.shape[0], half):
                at = slice(start, start + half)
                gradient = sum_ref[b * rows : b * rows + half, :]
                gradient_dot = sum_ref[b * rows + half : (b + 1) * rows, :]
                out_ref[b * half : (b + 1) * half, :] = (
                    gradient_dot * by_dot_ref[at, :] + gradient * by_error_ref[at, :]
                ).astype(BF16)
                b += 1

    return call(
        kernel,
        "back",
        core,
        [((total // 2, columns), BF16)],
        [(total, columns)],
        2 * total * depth * columns,
        [*same, *other, down_weight, *by_dot, *by_error],
    )[0]


def outer(core, same, other, weighted, scale):
    count, rows = len(same), same[0].shape[0]
    half = same[0].shape[1]
    total, depth = count * rows, 2 * half
    columns = weighted[0].shape[1]
    tile = 512

    def kernel(core_ref, *refs):
        blocks, refs = refs[: 2 * count], refs[2 * count :]
        weighted_refs, (out_ref, held, sems) = refs[:-3], refs[-3:]
        right = jnp.concatenate([w[...] for w in weighted_refs])
        copies = []
        for own, near, at in passes(core_ref[0], half, tile):
            left = jnp.concatenate([b[:, near] for b in (blocks[:count] if own else blocks[count:])])
            product = lax.dot_general(
                left, right, (((0,), (0,)), ((), ())), preferred_element_type=F32
            )
            slot = len(copies)
            held[slot] = (product * scale).astype(BF16)
            copies.append(pltpu.make_async_copy(held.at[slot], out_ref.at[at], sems.at[slot]))
            copies[-1].start()
        for copy in copies:
            copy.wait()

    operands = [*same, *other, *weighted]
    tiles = depth // tile
    return pl.pallas_call(
        kernel,
        in_specs=[IN_SMEM] + [IN_VMEM] * len(operands),
        out_specs=pl.BlockSpec(memory_space=pltpu.HBM),
        out_shape=jax.ShapeDtypeStruct((depth, columns), BF16),
        scratch_shapes=[pltpu.VMEM((tiles, tile, columns), BF16), pltpu.SemaphoreType.DMA((tiles,))],
        compiler_params=pltpu.CompilerParams(vmem_limit_bytes=24 * MIB),
        cost_estimate=pl.CostEstimate(
            flops=2 * total * depth * columns, bytes_accessed=2 * depth * columns, transcendentals=0
        ),
        name="outer",
    )(core, *[in_vmem(x) for x in operands])


def on_device(devices, tokens, targets, gate_weight, up_weight, down_weight, probe):
    mine, features = tokens.shape
    rows, half, quarter = 2 * mine, features // 2, features // 4
    onward, backward, partner = ring_routes(devices)
    chips = devices // 2
    steps = (chips - 1) // 2
    count = chips
    even = chips % 2 == 0
    index = lax.rem(lax.axis_index(AXIS), 2)
    core = index.astype(jnp.int32).reshape(1)

    def chip_rows(array):
        keep = lax.dynamic_slice(array, (0, index * half), (mine, half))
        give = lax.dynamic_slice(array, (0, (1 - index) * half), (mine, half))
        got = send(give, partner)
        return jnp.where(index == 0, jnp.concatenate([keep, got]), jnp.concatenate([got, keep]))

    last = 1 + 2 * steps
    cuts = [0, max(1, last - 4), max(1, last - 2), count]
    groups = [list(range(a, b)) for a, b in zip(cuts, cuts[1:]) if a < b]

    def gather(owns, work):
        chains = range(len(owns))
        same, other = [[own] for own in owns], [[] for _ in owns]
        ends = [(own, own) for own in owns]

        def swap():
            for c in chains:
                other[c] += [send(block, partner) for block in same[c][len(other[c]) :]]

        for step in range(1, steps + 1):
            moved = [(send(ends[c][0], onward), send(ends[c][1], backward)) for c in chains]
            swap()
            done = work(step, same, other)
            for c in chains:
                before, after, *_ = tie(*moved[c], *(done if c == 0 else ()))
                ends[c] = before, after
                same[c] += [before, after]
        if even:
            moved = [
                (send(ends[c][0][:, :quarter], onward), send(ends[c][1][:, quarter:], backward))
                for c in chains
            ]
            swap()
            done = work(steps + 1, same, other)
            for c in chains:
                near, far, *_ = tie(*moved[c], *(done if c == 0 else ()))
                same[c].append(jnp.concatenate([near, far], axis=1))
        swap()
        work(steps + 2, same, other)
        return same, other

    hidden, by_dot, by_error = [], [], []
    weights = {}

    def run_forward(step, same, other):
        same, other = same[0], other[0]
        if step == 1:
            weights["gate"], weights["up"] = fetch([gate_weight, up_weight], same[0])
            return [weights["gate"], weights["up"]]
        done = []
        ready = len(other) if step > steps + 1 else len(other) - 2
        while len(hidden) < len(groups) and groups[len(hidden)][-1] < ready:
            g = groups[len(hidden)]
            at = slice(g[0], g[-1] + 1)
            late = None if "probe" in weights else probe
            beside = down_weight if late is None and "down" not in weights else None
            known = [weights[n] for n in ("gate", "up", "probe") if n in weights]
            h, d, e, *came = forward(core, same[at], other[at], known, late, beside)
            hidden.append(h), by_dot.append(d), by_error.append(e)
            if came:
                weights["down" if late is None else "probe"] = came[0]
            done.append(h)
            if step <= steps + 1:
                break
        return done

    (same,), (other,) = gather([chip_rows(tokens)], run_forward)
    if "down" not in weights:
        (weights["down"],) = fetch([down_weight], hidden[-1])
    goals = chip_rows(targets).astype(F32)

    split = max(len(groups) - 1, 1)
    near_blocks = [b for g in groups[:split] for b in g]
    far_blocks = [b for g in groups[split:] for b in g]
    partial, swapped = {}, {}

    def keep(blocks, own, others):
        for at, b in enumerate(blocks):
            at = slice(2 * rows * at, 2 * rows * (at + 1))
            partial[b] = own[at]
            swapped[b] = send(others[at], partner)

    def block_of(b):
        return partial[b].astype(F32) + swapped[b].astype(F32)

    def near_work(after):
        hidden_near = tie(*hidden[:split], after)[:-1]
        others, own = down(core, hidden_near, weights["down"])
        keep(near_blocks, own, others)
        return own

    if far_blocks:
        (others,) = down(core, hidden[split:], weights["down"], both=False, own_half=False)
        (own,) = down(core, [*hidden[split:]], weights["down"], both=False)
        keep(far_blocks, own, others)
    else:
        near_work(hidden[-1])

    from_before = from_after = None
    if even:
        far = block_of(count - 1).astype(BF16)
        from_before, from_after = send(far[:, :quarter], onward), send(far[:, quarter:], backward)
        if far_blocks:
            from_before, from_after, _ = tie(from_before, from_after, near_work(far))
        from_before = jnp.pad(from_before.astype(F32), [(0, 0), (0, quarter)])
        from_after = jnp.pad(from_after.astype(F32), [(0, 0), (quarter, 0)])
    for distance in range(steps, 0, -1):
        to_after, to_before = block_of(2 * distance), block_of(2 * distance - 1)
        if from_before is not None:
            to_after, to_before = to_after + from_before, to_before + from_after
        to_after, to_before = tie(to_after.astype(BF16), to_before.astype(BF16))
        from_before, from_after = send(to_after, onward), send(to_before, backward)
        if distance == steps and not even and far_blocks:
            from_before, from_after, _ = tie(from_before, from_after, near_work(to_after))
        from_before, from_after = tie(from_before, from_after)
        from_before, from_after = from_before.astype(F32), from_after.astype(F32)
    total = block_of(0) + from_before + from_after
    message = jnp.concatenate([total[:rows] - goals, total[rows:]]).astype(BF16)

    weighted = []
    back_groups = [groups[:split], *[[g] for g in groups[split:]]]

    def run_back(step, same, other):
        done = []
        ready = len(other[0])
        while len(weighted) < len(back_groups) and back_groups[len(weighted)][-1][-1] < ready:
            gs = back_groups[len(weighted)]
            at = slice(gs[0][0], gs[-1][-1] + 1)
            first = sum(len(x) for x in back_groups[: len(weighted)])
            saved = slice(first, first + len(gs))
            weighted.append(
                back(
                    core,
                    same[0][at],
                    other[0][at],
                    weights["down"],
                    by_dot[saved],
                    by_error[saved],
                )
            )
            done.append(weighted[-1])
        return done

    gather([message], run_back)
    return outer(core, same, other, weighted, (mine * devices) ** (-0.5))


def solution(mesh):
    placed = (
        P(("groups", "tensor"), None),
        P(("groups", "tensor"), None),
        P(None, "tensor"),
        P(None, "tensor"),
        P("tensor", None),
        P("groups", "tensor"),
    )
    return jax.shard_map(
        functools.partial(on_device, mesh.shape[AXIS]),
        mesh=mesh,
        in_specs=placed,
        out_specs=P("groups", "tensor"),
        check_vma=False,
    )
```

time: 362 us -> 134 us (0.37)
  waiting for transfers between devices: 274 us -> 59.7 us
  matrix products: 58.4 us -> 0 us
  Pallas kernels: 0 us -> 39.2 us
  starting transfers between devices: 0.3 us -> 31.8 us
  between operations: 13.3 us -> 0.57 us
  local copies, waits for them, and re-layouts: 13.1 us -> 1.41 us
    reduce_scatter x2 -> x0, waiting for transfers between devices: 161 us -> none  [the longest x1 88 us: on_device(): lax.psum_scatter(jnp.dot(hidden, down_weight, preferred_element_type=jnp....]
    all_gather x2 -> x0, waiting for transfers between devices: 112 us -> none  [the longest x1 61.6 us: on_device(): block_rows = lax.all_gather(stacked, 'tensor', axis=1, tiled=True)]
    ppermute x0 -> x50, waiting for transfers between devices: none -> 59.7 us  [send(): return lax.ppermute(block, AXIS, route)]
    dot_general x7 -> x0, matrix products: 58.4 us -> none  [the longest x1 15.5 us: on_device(): lax.dot_general(everyone, weighted, (((0,), (0,)), ((), ())), preferred_e...]
    pallas_call x0 -> x10, Pallas kernels: none -> 39.2 us  [the longest x8 27.8 us: call(): pl.pallas_call(kernel, in_specs=[IN_SMEM] + [IN_VMEM] * len(operands) + [...]
    ppermute x0 -> x50, starting transfers between devices: none -> 31.8 us  [send(): return lax.ppermute(block, AXIS, route)]
    convert_element_type x1 -> x0, local copies, waits for them, and re-layouts: 11.9 us -> none  [on_device(): return (result * total_rows ** (-0.5)).astype(jnp.bfloat16)]
  transfers between devices with their start and end apart: 4 -> 50, of which waited for: 4 -> 23; matrix products, arithmetic and copies ran while one was open for 3% -> 0% of each run, Pallas kernels for 0% -> 19%
where the time goes in v2:
time: 134 us
  waiting for transfers between devices  59.7 us (45%)
  Pallas kernels  39.2 us (29%)
  starting transfers between devices  31.8 us (24%)
  other arithmetic  1.54 us (1%)
  local copies, waits for them, and re-layouts  1.41 us (1%)
    ppermute x50, waiting for transfers between devices, send(): return lax.ppermute(block, AXIS, route)  59.7 us
    ppermute x50, starting transfers between devices, send(): return lax.ppermute(block, AXIS, route)  31.8 us
    pallas_call x8, Pallas kernels, call(): pl.pallas_call(kernel, in_specs=[IN_SMEM] + [IN_VMEM] * len(operands) + [...  27.8 us
    pallas_call x1, Pallas kernels, fetch(): pl.pallas_call(kernel, in_specs=[pl.BlockSpec(memory_space=pl.ANY)] + [pl...  5.78 us
    pallas_call x1, Pallas kernels, outer(): pl.pallas_call(kernel, in_specs=[IN_SMEM] + [IN_VMEM] * len(operands), ou...  5.62 us
  transfers between devices with their start and end apart: 50, of which 23 were waited for; matrix products, arithmetic and copies ran while one was open for 0% of the time, Pallas kernels for 19%

profile of v2, /device:TPU:0, one launch (start us, length us, event | category | flops | bytes accessed | tf_op | source)
XLA Modules:
  0.0 134.2 jit_solution(3991679822024052729)
XLA Ops:
  0.0 1.0 constant_dynamic-slice_fusion.3
  1.5 0.9 collective-permute-done
  2.5 3.0 %collective-permute-start.1 = (bf16[48,2048]{1,0:T(8,128)(2,1)S(1)}, bf16[48,2048]{1,0:T(8,128)(2,1)S(1)}, u32[]{:S(2)}, u32[]{:S(2)}) collective-permute-start(bf16[48,2048]{1,0:T(8,128)(2,1)S(1)} %maximum_select_fusion.after_ref.refs_0_), channel_id=1, source_target_pairs={{0,4},{1,5},{4,8},{5,9},{8,12},{9,13},{12,14},{13,15},{14,10},{15,... | collective-permute-start | bytes 589832 | tf_op jit(solution)/shard_map/ppermute | solution.py:31
  5.4 5.8 %fetch.1 = (bf16[4096,1024]{1,0:T(8,128)(2,1)S(1)}, bf16[4096,1024]{1,0:T(8,128)(2,1)S(1)}) custom-call(bf16[48,2048]{1,0:T(8,128)(2,1)S(1)} %maximum_select_fusion.after_ref.refs_0_, bf16[4096,1024]{1,0:T(8,128)(2,1)} %refs_0_.1, bf16[4096,1024]{1,0:T(8,128)(2,1)} %refs_1_.1), custom_call_target="tpu_custom_call" | custom-call | bytes 16777216 | tf_op jit(solution)/shard_map/fetch/pallas_call | solution.py:77
  11.2 0.9 collective-permute-done.2.refs_2_
  12.1 1.6 %collective-permute-start.3 = (bf16[48,2048]{1,0:T(8,128)(2,1)S(1)}, bf16[48,2048]{1,0:T(8,128)(2,1)S(1)}, u32[]{:S(2)}, u32[]{:S(2)}) collective-permute-start(bf16[48,2048]{1,0:T(8,128)(2,1)S(1)} %collective-permute-done.1.refs_1_), channel_id=1, source_target_pairs={{0,4},{1,5},{4,8},{5,9},{8,12},{9,13},{12,14},{13,15},{14,10},{15,... | collective-permute-start | bytes 589832 | tf_op jit(solution)/shard_map/ppermute | solution.py:31
  14.7 3.3 %collective-permute-done.3.refs_0_.refs_3_ = bf16[48,2048]{1,0:T(8,128)(2,1)S(1)} collective-permute-done((bf16[48,2048]{1,0:T(8,128)(2,1)S(1)}, bf16[48,2048]{1,0:T(8,128)(2,1)S(1)}, u32[]{:S(2)}, u32[]{:S(2)}) %collective-permute-start.3) | collective-permute-done | bytes 196640 | tf_op jit(solution)/shard_map/ppermute | solution.py:31
  18.0 1.5 %collective-permute-done.4.refs_1_.refs_4_ = bf16[48,2048]{1,0:T(8,128)(2,1)S(1)} collective-permute-done((bf16[48,2048]{1,0:T(8,128)(2,1)S(1)}, bf16[48,2048]{1,0:T(8,128)(2,1)S(1)}, u32[]{:S(2)}, u32[]{:S(2)}) %collective-permute-start.4) | collective-permute-done | bytes 196640 | tf_op jit(solution)/shard_map/ppermute | solution.py:31
  19.5 1.6 %collective-permute-start.5 = (bf16[48,2048]{1,0:T(8,128)(2,1)S(1)}, bf16[48,2048]{1,0:T(8,128)(2,1)S(1)}, u32[]{:S(2)}, u32[]{:S(2)}) collective-permute-start(bf16[48,2048]{1,0:T(8,128)(2,1)S(1)} %collective-permute-done.3.refs_0_.refs_3_), channel_id=1, source_target_pairs={{0,4},{1,5},{4,8},{5,9},{8,12},{9,13},{12,14},{13,15},{14,10},{15,... | collective-permute-start | bytes 589832 | tf_op jit(solution)/shard_map/ppermute | solution.py:31
  21.7 5.0 %forward.3 = (bf16[288,1024]{1,0:T(8,128)(2,1)S(1)}, f32[144,1024]{1,0:T(8,128)S(1)}, f32[144,1024]{1,0:T(8,128)S(1)}, bf16[4096,1024]{1,0:T(8,128)(2,1)S(1)}) custom-call(s32[1]{0:T(128)} %bitcast.core_ref, bf16[48,2048]{1,0:T(8,128)(2,1)S(1)} %maximum_select_fusion.after_ref.refs_0_, bf16[48,2048]{1,0:T(8,128)(2,1)S(1)} %collective-permute-done.1.refs_1_, ...), custom_call_target="tpu_custom_call" | custom-call | flops 3623878656 | bytes 17956864 | tf_op jit(solution)/shard_map/forward/pallas_call | solution.py:41
  26.8 1.6 %collective-permute-done.6.refs_1_.refs_6_ = bf16[48,2048]{1,0:T(8,128)(2,1)S(1)} collective-permute-done((bf16[48,2048]{1,0:T(8,128)(2,1)S(1)}, bf16[48,2048]{1,0:T(8,128)(2,1)S(1)}, u32[]{:S(2)}, u32[]{:S(2)}) %collective-permute-start.6) | collective-permute-done | bytes 196640 | tf_op jit(solution)/shard_map/ppermute | solution.py:31
  28.5 0.5 collective-permute-start.15
  29.0 1.6 %collective-permute-start.10 = (bf16[48,1024]{1,0:T(8,128)(2,1)S(1)}, bf16[48,1024]{1,0:T(8,128)(2,1)S(1)}, u32[]{:S(2)}, u32[]{:S(2)}) collective-permute-start(bf16[48,1024]{1,0:T(8,128)(2,1)S(1)} %slice.73), channel_id=1, source_target_pairs={{0,4},{1,5},{4,8},{5,9},{8,12},{9,13},{12,14},{13,15},{14,10},{15,... | collective-permute-start | bytes 294920 | tf_op jit(solution)/shard_map/ppermute | solution.py:31
  31.0 4.5 %forward.4 = (bf16[192,1024]{1,0:T(8,128)(2,1)S(1)}, f32[96,1024]{1,0:T(8,128)S(1)}, f32[96,1024]{1,0:T(8,128)S(1)}, bf16[1024,4096]{1,0:T(8,128)(2,1)S(1)}) custom-call(s32[1]{0:T(128)} %bitcast.core_ref, bf16[48,2048]{1,0:T(8,128)(2,1)S(1)} %collective-permute-done.3.refs_0_.refs_3_, bf16[48,2048]{1,0:T(8,128)(2,1)S(1)} %collective-permute-done.4.refs_1_.refs_4_, ...), custom_call_target="tpu_custom_call" | custom-call | flops 2415919104 | bytes 25952256 | tf_op jit(solution)/shard_map/forward/pallas_call | solution.py:41
  35.7 1.4 %collective-permute-done.16.refs_5_.refs_15_ = bf16[48,2048]{1,0:T(8,128)(2,1)S(1)} collective-permute-done((bf16[48,2048]{1,0:T(8,128)(2,1)S(1)}, bf16[48,2048]{1,0:T(8,128)(2,1)S(1)}, u32[]{:S(2)}, u32[]{:S(2)}) %collective-permute-start.16) | collective-permute-done | bytes 196640 | tf_op jit(solution)/shard_map/ppermute | solution.py:31
  37.1 4.3 %forward.5 = (bf16[288,1024]{1,0:T(8,128)(2,1)S(1)}, f32[144,1024]{1,0:T(8,128)S(1)}, f32[144,1024]{1,0:T(8,128)S(1)}) custom-call(s32[1]{0:T(128)} %bitcast.core_ref, bf16[48,2048]{1,0:T(8,128)(2,1)S(1)} %collective-permute-done.5.refs_0_.refs_5_, bf16[48,2048]{1,0:T(8,128)(2,1)S(1)} %collective-permute-done.6.refs_1_.refs_6_, ...), custom_call_target="tpu_custom_call" | custom-call | flops 3623878656 | bytes 26345472 | tf_op jit(solution)/shard_map/forward/pallas_call | solution.py:41
  41.4 1.4 %down.4 = bf16[288,2048]{1,0:T(8,128)(2,1)S(1)} custom-call(s32[1]{0:T(128)} %bitcast.core_ref, bf16[288,1024]{1,0:T(8,128)(2,1)S(1)} %get-tuple-element.65.refs_0_, bf16[1024,4096]{1,0:T(8,128)(2,1)S(1)} %get-tuple-element.66.refs_1_.refs_2_.refs_10_.refs_6_), custom_call_target="tpu_custom_call" | custom-call | flops 1207959552 | bytes 8978432 | tf_op jit(solution)/shard_map/down/pallas_call | solution.py:41
  43.6 1.4 %down.3 = bf16[288,2048]{1,0:T(8,128)(2,1)S(1)} custom-call(s32[1]{0:T(128)} %bitcast.core_ref, bf16[288,1024]{1,0:T(8,128)(2,1)S(1)} %get-tuple-element.65.refs_0_, bf16[1024,4096]{1,0:T(8,128)(2,1)S(1)} %get-tuple-element.66.refs_1_.refs_2_.refs_10_.refs_6_), custom_call_target="tpu_custom_call" | custom-call | flops 1207959552 | bytes 8978432 | tf_op jit(solution)/shard_map/down/pallas_call | solution.py:41
  45.1 1.6 %collective-permute-start.22 = (bf16[96,1024]{1,0:T(8,128)(2,1)S(1)}, bf16[96,1024]{1,0:T(8,128)(2,1)S(1)}, u32[]{:S(2)}, u32[]{:S(2)}) collective-permute-start(bf16[96,1024]{1,0:T(8,128)(2,1)S(1)} %get-tuple-element.114), channel_id=1, source_target_pairs={{0,4},{1,5},{4,8},{5,9},{8,12},{9,13},{12,14},{13,15},{14,10},{15,... | collective-permute-start | bytes 589832 | tf_op jit(solution)/shard_map/ppermute | solution.py:31
  47.2 4.2 %down.5 = (bf16[480,2048]{1,0:T(8,128)(2,1)S(1)}, bf16[480,2048]{1,0:T(8,128)(2,1)S(1)}) custom-call(s32[1]{0:T(128)} %bitcast.core_ref, bf16[288,1024]{1,0:T(8,128)(2,1)S(1)} %get-tuple-element.67.refs_0_, bf16[192,1024]{1,0:T(8,128)(2,1)S(1)} %get-tuple-element.68.refs_1_, bf16[1024,4096]{1,0:T(8,128)(2,1)S(1)} %get-tuple-element.66.refs_1_.refs_2_.refs_10_.refs_6_), custom_call_target="tpu_custom_call" | custom-call | flops 4026531840 | bytes 9371648 | tf_op jit(solution)/shard_map/down/pallas_call | solution.py:41
  51.7 0.7 collective-permute-done.22
  52.4 1.3 collective-permute-done.23
  54.0 1.6 %collective-permute-start.25 = (bf16[96,2048]{1,0:T(8,128)(2,1)S(1)}, bf16[96,2048]{1,0:T(8,128)(2,1)S(1)}, u32[]{:S(2)}, u32[]{:S(2)}) collective-permute-start(bf16[96,2048]{1,0:T(8,128)(2,1)S(1)} %get-tuple-element.73), channel_id=1, source_target_pairs={{0,4},{1,5},{4,8},{5,9},{8,12},{9,13},{12,14},{13,15},{14,10},{15,... | collective-permute-start | bytes 1179656 | tf_op jit(solution)/shard_map/ppermute | solution.py:31
  56.6 7.7 %collective-permute-done.25 = bf16[96,2048]{1,0:T(8,128)(2,1)S(1)} collective-permute-done((bf16[96,2048]{1,0:T(8,128)(2,1)S(1)}, bf16[96,2048]{1,0:T(8,128)(2,1)S(1)}, u32[]{:S(2)}, u32[]{:S(2)}) %collective-permute-start.25) | collective-permute-done | bytes 393248 | tf_op jit(solution)/shard_map/ppermute | solution.py:31
  64.3 1.3 collective-permute-done.26
  66.0 0.7 collective-permute-start.28
  66.7 1.3 collective-permute-start.29
  68.6 6.5 %collective-permute-done.28 = bf16[96,2048]{1,0:T(8,128)(2,1)S(1)} collective-permute-done((bf16[96,2048]{1,0:T(8,128)(2,1)S(1)}, bf16[96,2048]{1,0:T(8,128)(2,1)S(1)}, u32[]{:S(2)}, u32[]{:S(2)}) %collective-permute-start.28) | collective-permute-done | bytes 393248 | tf_op jit(solution)/shard_map/ppermute | solution.py:31
  76.1 0.6 collective-permute-start.31
  76.7 1.5 %collective-permute-start.32 = (bf16[96,2048]{1,0:T(8,128)(2,1)S(1)}, bf16[96,2048]{1,0:T(8,128)(2,1)S(1)}, u32[]{:S(2)}, u32[]{:S(2)}) collective-permute-start(bf16[96,2048]{1,0:T(8,128)(2,1)S(1)} %get-tuple-element.82), channel_id=1, source_target_pairs={{4,0},{5,1},{8,4},{9,5},{12,8},{13,9},{14,12},{15,13},{10,14},{11,... | collective-permute-start | bytes 1179656 | tf_op jit(solution)/shard_map/ppermute | solution.py:31
  78.2 0.6 collective-permute-start.33
  78.7 6.0 %collective-permute-done.31 = bf16[96,2048]{1,0:T(8,128)(2,1)S(1)} collective-permute-done((bf16[96,2048]{1,0:T(8,128)(2,1)S(1)}, bf16[96,2048]{1,0:T(8,128)(2,1)S(1)}, u32[]{:S(2)}, u32[]{:S(2)}) %collective-permute-start.31) | collective-permute-done | bytes 393248 | tf_op jit(solution)/shard_map/ppermute | solution.py:31
  85.5 0.6 collective-permute-start.34
  86.1 1.5 %collective-permute-start.35 = (bf16[96,2048]{1,0:T(8,128)(2,1)S(1)}, bf16[96,2048]{1,0:T(8,128)(2,1)S(1)}, u32[]{:S(2)}, u32[]{:S(2)}) collective-permute-start(bf16[96,2048]{1,0:T(8,128)(2,1)S(1)} %pad_maximum_fusion.refs_0_), channel_id=1, source_target_pairs={{4,0},{5,1},{8,4},{9,5},{12,8},{13,9},{14,12},{15,13},{10,14},{11,... | collective-permute-start | bytes 1179656 | tf_op jit(solution)/shard_map/ppermute | solution.py:31
  87.6 7.9 %collective-permute-done.34.refs_1_ = bf16[96,2048]{1,0:T(8,128)(2,1)S(1)} collective-permute-done((bf16[96,2048]{1,0:T(8,128)(2,1)S(1)}, bf16[96,2048]{1,0:T(8,128)(2,1)S(1)}, u32[]{:S(2)}, u32[]{:S(2)}) %collective-permute-start.34) | collective-permute-done | bytes 393248 | tf_op jit(solution)/shard_map/ppermute | solution.py:31
  95.5 0.9 collective-permute-done.35.refs_2_
  96.6 1.8 %collective-permute-start.37 = (bf16[96,2048]{1,0:T(8,128)(2,1)S(1)}, bf16[96,2048]{1,0:T(8,128)(2,1)S(1)}, u32[]{:S(2)}, u32[]{:S(2)}) collective-permute-start(bf16[96,2048]{1,0:T(8,128)(2,1)S(1)} %collective-permute-done.35.refs_2_), channel_id=1, source_target_pairs={{4,0},{5,1},{8,4},{9,5},{12,8},{13,9},{14,12},{15,13},{10,14},{11,... | collective-permute-start | bytes 1179656 | tf_op jit(solution)/shard_map/ppermute | solution.py:31
  98.9 5.2 %collective-permute-done.36.refs_3_ = bf16[96,2048]{1,0:T(8,128)(2,1)S(1)} collective-permute-done((bf16[96,2048]{1,0:T(8,128)(2,1)S(1)}, bf16[96,2048]{1,0:T(8,128)(2,1)S(1)}, u32[]{:S(2)}, u32[]{:S(2)}) %collective-permute-start.36) | collective-permute-done | bytes 393248 | tf_op jit(solution)/shard_map/ppermute | solution.py:31
  104.9 2.0 %collective-permute-start.44 = (bf16[96,2048]{1,0:T(8,128)(2,1)S(1)}, bf16[96,2048]{1,0:T(8,128)(2,1)S(1)}, u32[]{:S(2)}, u32[]{:S(2)}) collective-permute-start(bf16[96,2048]{1,0:T(8,128)(2,1)S(1)} %collective-permute-done.37.refs_4_), channel_id=1, source_target_pairs={{4,0},{5,1},{8,4},{9,5},{12,8},{13,9},{14,12},{15,13},{10,14},{11,... | collective-permute-start | bytes 1179656 | tf_op jit(solution)/shard_map/ppermute | solution.py:31
  107.0 4.3 %back.2.refs_16_ = bf16[240,1024]{1,0:T(8,128)(2,1)S(1)} custom-call(s32[1]{0:T(128)} %bitcast.core_ref, bf16[96,2048]{1,0:T(8,128)(2,1)S(1)} %pad_maximum_fusion.refs_0_, bf16[96,2048]{1,0:T(8,128)(2,1)S(1)} %collective-permute-done.34.refs_1_, bf16[96,2048]{1,0:T(8,128)(2,1)S(1)} %collective-permute-done.35.refs_2_, ...), custom_call_target="tpu_custom_call" | custom-call | flops 4026531840 | bytes 13303808 | tf_op jit(solution)/shard_map/back/pallas_call | solution.py:41
  111.2 4.7 %collective-permute-done.43.refs_0_ = bf16[96,2048]{1,0:T(8,128)(2,1)S(1)} collective-permute-done((bf16[96,2048]{1,0:T(8,128)(2,1)S(1)}, bf16[96,2048]{1,0:T(8,128)(2,1)S(1)}, u32[]{:S(2)}, u32[]{:S(2)}) %collective-permute-start.43) | collective-permute-done | bytes 393248 | tf_op jit(solution)/shard_map/ppermute | solution.py:31
  116.0 1.6 %collective-permute-start.45 = (bf16[96,1024]{1,0:T(8,128)(2,1)S(1)}, bf16[96,1024]{1,0:T(8,128)(2,1)S(1)}, u32[]{:S(2)}, u32[]{:S(2)}) collective-permute-start(bf16[96,1024]{1,0:T(8,128)(2,1)S(1)} %slice.95), channel_id=1, source_target_pairs={{0,4},{1,5},{4,8},{5,9},{8,12},{9,13},{12,14},{13,15},{14,10},{15,... | collective-permute-start | bytes 589832 | tf_op jit(solution)/shard_map/ppermute | solution.py:31
  117.6 0.8 collective-permute-start.46
  118.9 3.1 %collective-permute-done.45 = bf16[96,1024]{1,0:T(8,128)(2,1)S(1)} collective-permute-done((bf16[96,1024]{1,0:T(8,128)(2,1)S(1)}, bf16[96,1024]{1,0:T(8,128)(2,1)S(1)}, u32[]{:S(2)}, u32[]{:S(2)}) %collective-permute-start.45) | collective-permute-done | bytes 196640 | tf_op jit(solution)/shard_map/ppermute | solution.py:31
  122.0 1.8 %collective-permute-done.46 = bf16[96,1024]{1,0:T(8,128)(2,1)S(1)} collective-permute-done((bf16[96,1024]{1,0:T(8,128)(2,1)S(1)}, bf16[96,1024]{1,0:T(8,128)(2,1)S(1)}, u32[]{:S(2)}, u32[]{:S(2)}) %collective-permute-start.46) | collective-permute-done | bytes 196640 | tf_op jit(solution)/shard_map/ppermute | solution.py:31
  124.0 1.7 %collective-permute-done.49.refs_5_ = bf16[96,2048]{1,0:T(8,128)(2,1)S(1)} collective-permute-done((bf16[96,2048]{1,0:T(8,128)(2,1)S(1)}, bf16[96,2048]{1,0:T(8,128)(2,1)S(1)}, u32[]{:S(2)}, u32[]{:S(2)}) %collective-permute-start.49) | collective-permute-done | bytes 393248 | tf_op jit(solution)/shard_map/ppermute | solution.py:31
  125.7 2.6 %back.3.refs_17_ = bf16[144,1024]{1,0:T(8,128)(2,1)S(1)} custom-call(s32[1]{0:T(128)} %bitcast.core_ref, bf16[96,2048]{1,0:T(8,128)(2,1)S(1)} %collective-permute-done.43.refs_0_, bf16[96,2048]{1,0:T(8,128)(2,1)S(1)} %collective-permute-done.44.refs_1_, bf16[96,2048]{1,0:T(8,128)(2,1)S(1)} %constant_dynamic-update-slice_fusion.2.refs_2_, ...), custom_call_target="tpu_custom_call" | custom-call | flops 2415919104 | bytes 11337728 | tf_op jit(solution)/shard_map/back/pallas_call | solution.py:41
  128.4 5.6 %outer.1 = bf16[4096,1024]{1,0:T(8,128)(2,1)} custom-call(s32[1]{0:T(128)} %bitcast.core_ref, bf16[48,2048]{1,0:T(8,128)(2,1)S(1)} %maximum_select_fusion.after_ref.refs_0_, bf16[48,2048]{1,0:T(8,128)(2,1)S(1)} %collective-permute-done.1.refs_1_, bf16[48,2048]{1,0:T(8,128)(2,1)S(1)} %collective-permute-done.2.refs_2_, ...), custom_call_target="tpu_custom_call" | custom-call | flops 3221225472 | bytes 8388608 | tf_op jit(solution)/shard_map/outer/pallas_call | solution.py:255
  (86 shorter events, 10.7 us)
Async XLA Ops:
  2.5 8.8 %collective-permute-start.1 = (bf16[48,2048]{1,0:T(8,128)(2,1)S(1)}, bf16[48,2048]{1,0:T(8,128)(2,1)S(1)}, u32[]{:S(2)}, u32[]{:S(2)}) collective-permute-start(bf16[48,2048]{1,0:T(8,128)(2,1)S(1)} %maximum_select_fusion.after_ref.refs_0_), channel_id=1, source_target_pairs={{0,4},{1,5},{4,8},{5,9},{8,12},{9,13},{12,14},{13,15},{14,10},{15,... | collective-permute-start | bytes 589832 | tf_op jit(solution)/shard_map/ppermute | solution.py:31
  5.4 6.7 %collective-permute-start.2 = (bf16[48,2048]{1,0:T(8,128)(2,1)S(1)}, bf16[48,2048]{1,0:T(8,128)(2,1)S(1)}, u32[]{:S(2)}, u32[]{:S(2)}) collective-permute-start(bf16[48,2048]{1,0:T(8,128)(2,1)S(1)} %maximum_select_fusion.after_ref.refs_0_), channel_id=1, source_target_pairs={{4,0},{5,1},{8,4},{9,5},{12,8},{13,9},{14,12},{15,13},{10,14},{11,... | collective-permute-start | bytes 589832 | tf_op jit(solution)/shard_map/ppermute | solution.py:31
  12.1 5.9 %collective-permute-start.3 = (bf16[48,2048]{1,0:T(8,128)(2,1)S(1)}, bf16[48,2048]{1,0:T(8,128)(2,1)S(1)}, u32[]{:S(2)}, u32[]{:S(2)}) collective-permute-start(bf16[48,2048]{1,0:T(8,128)(2,1)S(1)} %collective-permute-done.1.refs_1_), channel_id=1, source_target_pairs={{0,4},{1,5},{4,8},{5,9},{8,12},{9,13},{12,14},{13,15},{14,10},{15,... | collective-permute-start | bytes 589832 | tf_op jit(solution)/shard_map/ppermute | solution.py:31
  13.7 5.8 %collective-permute-start.4 = (bf16[48,2048]{1,0:T(8,128)(2,1)S(1)}, bf16[48,2048]{1,0:T(8,128)(2,1)S(1)}, u32[]{:S(2)}, u32[]{:S(2)}) collective-permute-start(bf16[48,2048]{1,0:T(8,128)(2,1)S(1)} %collective-permute-done.2.refs_2_), channel_id=1, source_target_pairs={{4,0},{5,1},{8,4},{9,5},{12,8},{13,9},{14,12},{15,13},{10,14},{11,... | collective-permute-start | bytes 589832 | tf_op jit(solution)/shard_map/ppermute | solution.py:31
  14.1 6.9 %collective-permute-start.7 = (bf16[48,2048]{1,0:T(8,128)(2,1)S(1)}, bf16[48,2048]{1,0:T(8,128)(2,1)S(1)}, u32[]{:S(2)}, u32[]{:S(2)}) collective-permute-start(bf16[48,2048]{1,0:T(8,128)(2,1)S(1)} %maximum_select_fusion.after_ref.refs_0_), channel_id=1, source_target_pairs={{0,1},{1,0},{2,3},{3,2},{4,5},{5,4},{6,7},{7,6},{8,9},{9,8},{10,11... | collective-permute-start | bytes 589832 | tf_op jit(solution)/shard_map/ppermute | solution.py:31
  14.1 7.1 %collective-permute-start.8 = (bf16[48,2048]{1,0:T(8,128)(2,1)S(1)}, bf16[48,2048]{1,0:T(8,128)(2,1)S(1)}, u32[]{:S(2)}, u32[]{:S(2)}) collective-permute-start(bf16[48,2048]{1,0:T(8,128)(2,1)S(1)} %collective-permute-done.1.refs_1_), channel_id=1, source_target_pairs={{0,1},{1,0},{2,3},{3,2},{4,5},{5,4},{6,7},{7,6},{8,9},{9,8},{10,11... | collective-permute-start | bytes 589832 | tf_op jit(solution)/shard_map/ppermute | solution.py:31
  14.7 7.1 %collective-permute-start.9 = (bf16[48,2048]{1,0:T(8,128)(2,1)S(1)}, bf16[48,2048]{1,0:T(8,128)(2,1)S(1)}, u32[]{:S(2)}, u32[]{:S(2)}) collective-permute-start(bf16[48,2048]{1,0:T(8,128)(2,1)S(1)} %collective-permute-done.2.refs_2_), channel_id=1, source_target_pairs={{0,1},{1,0},{2,3},{3,2},{4,5},{5,4},{6,7},{7,6},{8,9},{9,8},{10,11... | collective-permute-start | bytes 589832 | tf_op jit(solution)/shard_map/ppermute | solution.py:31
  19.5 11.1 %collective-permute-start.12 = (bf16[48,2048]{1,0:T(8,128)(2,1)S(1)}, bf16[48,2048]{1,0:T(8,128)(2,1)S(1)}, u32[]{:S(2)}, u32[]{:S(2)}) collective-permute-start(bf16[48,2048]{1,0:T(8,128)(2,1)S(1)} %collective-permute-done.3.refs_0_.refs_3_), channel_id=1, source_target_pairs={{0,1},{1,0},{2,3},{3,2},{4,5},{5,4},{6,7},{7,6},{8,9},{9,8},{10,11... | collective-permute-start | bytes 589832 | tf_op jit(solution)/shard_map/ppermute | solution.py:31
  19.5 7.3 %collective-permute-start.5 = (bf16[48,2048]{1,0:T(8,128)(2,1)S(1)}, bf16[48,2048]{1,0:T(8,128)(2,1)S(1)}, u32[]{:S(2)}, u32[]{:S(2)}) collective-permute-start(bf16[48,2048]{1,0:T(8,128)(2,1)S(1)} %collective-permute-done.3.refs_0_.refs_3_), channel_id=1, source_target_pairs={{0,4},{1,5},{4,8},{5,9},{8,12},{9,13},{12,14},{13,15},{14,10},{15,... | collective-permute-start | bytes 589832 | tf_op jit(solution)/shard_map/ppermute | solution.py:31
  21.0 10.0 %collective-permute-start.13 = (bf16[48,2048]{1,0:T(8,128)(2,1)S(1)}, bf16[48,2048]{1,0:T(8,128)(2,1)S(1)}, u32[]{:S(2)}, u32[]{:S(2)}) collective-permute-start(bf16[48,2048]{1,0:T(8,128)(2,1)S(1)} %collective-permute-done.4.refs_1_.refs_4_), channel_id=1, source_target_pairs={{0,1},{1,0},{2,3},{3,2},{4,5},{5,4},{6,7},{7,6},{8,9},{9,8},{10,11... | collective-permute-start | bytes 589832 | tf_op jit(solution)/shard_map/ppermute | solution.py:31
  21.3 7.1 %collective-permute-start.6 = (bf16[48,2048]{1,0:T(8,128)(2,1)S(1)}, bf16[48,2048]{1,0:T(8,128)(2,1)S(1)}, u32[]{:S(2)}, u32[]{:S(2)}) collective-permute-start(bf16[48,2048]{1,0:T(8,128)(2,1)S(1)} %collective-permute-done.4.refs_1_.refs_4_), channel_id=1, source_target_pairs={{4,0},{5,1},{8,4},{9,5},{12,8},{13,9},{14,12},{15,13},{10,14},{11,... | collective-permute-start | bytes 589832 | tf_op jit(solution)/shard_map/ppermute | solution.py:31
  28.4 7.3 %collective-permute-start.14 = (bf16[48,2048]{1,0:T(8,128)(2,1)S(1)}, bf16[48,2048]{1,0:T(8,128)(2,1)S(1)}, u32[]{:S(2)}, u32[]{:S(2)}) collective-permute-start(bf16[48,2048]{1,0:T(8,128)(2,1)S(1)} %collective-permute-done.5.refs_0_.refs_5_), channel_id=1, source_target_pairs={{0,1},{1,0},{2,3},{3,2},{4,5},{5,4},{6,7},{7,6},{8,9},{9,8},{10,11... | collective-permute-start | bytes 589832 | tf_op jit(solution)/shard_map/ppermute | solution.py:31
  28.5 7.2 %collective-permute-start.15 = (bf16[48,2048]{1,0:T(8,128)(2,1)S(1)}, bf16[48,2048]{1,0:T(8,128)(2,1)S(1)}, u32[]{:S(2)}, u32[]{:S(2)}) collective-permute-start(bf16[48,2048]{1,0:T(8,128)(2,1)S(1)} %collective-permute-done.6.refs_1_.refs_6_), channel_id=1, source_target_pairs={{0,1},{1,0},{2,3},{3,2},{4,5},{5,4},{6,7},{7,6},{8,9},{9,8},{10,11... | collective-permute-start | bytes 589832 | tf_op jit(solution)/shard_map/ppermute | solution.py:31
  29.0 6.5 %collective-permute-start.10 = (bf16[48,1024]{1,0:T(8,128)(2,1)S(1)}, bf16[48,1024]{1,0:T(8,128)(2,1)S(1)}, u32[]{:S(2)}, u32[]{:S(2)}) collective-permute-start(bf16[48,1024]{1,0:T(8,128)(2,1)S(1)} %slice.73), channel_id=1, source_target_pairs={{0,4},{1,5},{4,8},{5,9},{8,12},{9,13},{12,14},{13,15},{14,10},{15,... | collective-permute-start | bytes 294920 | tf_op jit(solution)/shard_map/ppermute | solution.py:31
  30.6 5.0 %collective-permute-start.11 = (bf16[48,1024]{1,0:T(8,128)(2,1)S(1)}, bf16[48,1024]{1,0:T(8,128)(2,1)S(1)}, u32[]{:S(2)}, u32[]{:S(2)}) collective-permute-start(bf16[48,1024]{1,0:T(8,128)(2,1)S(1)} %slice.74), channel_id=1, source_target_pairs={{4,0},{5,1},{8,4},{9,5},{12,8},{13,9},{14,12},{15,13},{10,14},{11,... | collective-permute-start | bytes 294920 | tf_op jit(solution)/shard_map/ppermute | solution.py:31
  42.9 2.1 %collective-permute-start.17 = (bf16[96,2048]{1,0:T(8,128)(2,1)S(1)}, bf16[96,2048]{1,0:T(8,128)(2,1)S(1)}, u32[]{:S(2)}, u32[]{:S(2)}) collective-permute-start(bf16[96,2048]{1,0:T(8,128)(2,1)S(1)} %get-tuple-element.112), channel_id=1, source_target_pairs={{0,1},{1,0},{2,3},{3,2},{4,5},{5,4},{6,7},{7,6},{8,9},{9,8},{10,11... | collective-permute-start | bytes 1179656 | tf_op jit(solution)/shard_map/ppermute | solution.py:31
  43.1 10.6 %collective-permute-start.21 = (bf16[96,2048]{1,0:T(8,128)(2,1)S(1)}, bf16[96,2048]{1,0:T(8,128)(2,1)S(1)}, u32[]{:S(2)}, u32[]{:S(2)}) collective-permute-start(bf16[96,2048]{1,0:T(8,128)(2,1)S(1)} %get-tuple-element.111), channel_id=1, source_target_pairs={{0,1},{1,0},{2,3},{3,2},{4,5},{5,4},{6,7},{7,6},{8,9},{9,8},{10,11... | collective-permute-start | bytes 1179656 | tf_op jit(solution)/shard_map/ppermute | solution.py:31
  43.4 10.2 %collective-permute-start.24 = (bf16[96,2048]{1,0:T(8,128)(2,1)S(1)}, bf16[96,2048]{1,0:T(8,128)(2,1)S(1)}, u32[]{:S(2)}, u32[]{:S(2)}) collective-permute-start(bf16[96,2048]{1,0:T(8,128)(2,1)S(1)} %get-tuple-element.110), channel_id=1, source_target_pairs={{0,1},{1,0},{2,3},{3,2},{4,5},{5,4},{6,7},{7,6},{8,9},{9,8},{10,11... | collective-permute-start | bytes 1179656 | tf_op jit(solution)/shard_map/ppermute | solution.py:31
  45.1 7.2 %collective-permute-start.22 = (bf16[96,1024]{1,0:T(8,128)(2,1)S(1)}, bf16[96,1024]{1,0:T(8,128)(2,1)S(1)}, u32[]{:S(2)}, u32[]{:S(2)}) collective-permute-start(bf16[96,1024]{1,0:T(8,128)(2,1)S(1)} %get-tuple-element.114), channel_id=1, source_target_pairs={{0,4},{1,5},{4,8},{5,9},{8,12},{9,13},{12,14},{13,15},{14,10},{15,... | collective-permute-start | bytes 589832 | tf_op jit(solution)/shard_map/ppermute | solution.py:31
  46.8 6.9 %collective-permute-start.23 = (bf16[96,1024]{1,0:T(8,128)(2,1)S(1)}, bf16[96,1024]{1,0:T(8,128)(2,1)S(1)}, u32[]{:S(2)}, u32[]{:S(2)}) collective-permute-start(bf16[96,1024]{1,0:T(8,128)(2,1)S(1)} %get-tuple-element.113), channel_id=1, source_target_pairs={{4,0},{5,1},{8,4},{9,5},{12,8},{13,9},{14,12},{15,13},{10,14},{11,... | collective-permute-start | bytes 589832 | tf_op jit(solution)/shard_map/ppermute | solution.py:31
  54.0 10.3 %collective-permute-start.25 = (bf16[96,2048]{1,0:T(8,128)(2,1)S(1)}, bf16[96,2048]{1,0:T(8,128)(2,1)S(1)}, u32[]{:S(2)}, u32[]{:S(2)}) collective-permute-start(bf16[96,2048]{1,0:T(8,128)(2,1)S(1)} %get-tuple-element.73), channel_id=1, source_target_pairs={{0,4},{1,5},{4,8},{5,9},{8,12},{9,13},{12,14},{13,15},{14,10},{15,... | collective-permute-start | bytes 1179656 | tf_op jit(solution)/shard_map/ppermute | solution.py:31
  55.6 10.0 %collective-permute-start.26 = (bf16[96,2048]{1,0:T(8,128)(2,1)S(1)}, bf16[96,2048]{1,0:T(8,128)(2,1)S(1)}, u32[]{:S(2)}, u32[]{:S(2)}) collective-permute-start(bf16[96,2048]{1,0:T(8,128)(2,1)S(1)} %get-tuple-element.74), channel_id=1, source_target_pairs={{4,0},{5,1},{8,4},{9,5},{12,8},{13,9},{14,12},{15,13},{10,14},{11,... | collective-permute-start | bytes 1179656 | tf_op jit(solution)/shard_map/ppermute | solution.py:31
  56.1 9.5 %collective-permute-start.20 = (bf16[96,2048]{1,0:T(8,128)(2,1)S(1)}, bf16[96,2048]{1,0:T(8,128)(2,1)S(1)}, u32[]{:S(2)}, u32[]{:S(2)}) collective-permute-start(bf16[96,2048]{1,0:T(8,128)(2,1)S(1)} %get-tuple-element.102), channel_id=1, source_target_pairs={{0,1},{1,0},{2,3},{3,2},{4,5},{5,4},{6,7},{7,6},{8,9},{9,8},{10,11... | collective-permute-start | bytes 1179656 | tf_op jit(solution)/shard_map/ppermute | solution.py:31
  56.1 9.5 %collective-permute-start.27 = (bf16[96,2048]{1,0:T(8,128)(2,1)S(1)}, bf16[96,2048]{1,0:T(8,128)(2,1)S(1)}, u32[]{:S(2)}, u32[]{:S(2)}) collective-permute-start(bf16[96,2048]{1,0:T(8,128)(2,1)S(1)} %get-tuple-element.101), channel_id=1, source_target_pairs={{0,1},{1,0},{2,3},{3,2},{4,5},{5,4},{6,7},{7,6},{8,9},{9,8},{10,11... | collective-permute-start | bytes 1179656 | tf_op jit(solution)/shard_map/ppermute | solution.py:31
  66.0 9.1 %collective-permute-start.28 = (bf16[96,2048]{1,0:T(8,128)(2,1)S(1)}, bf16[96,2048]{1,0:T(8,128)(2,1)S(1)}, u32[]{:S(2)}, u32[]{:S(2)}) collective-permute-start(bf16[96,2048]{1,0:T(8,128)(2,1)S(1)} %get-tuple-element.77), channel_id=1, source_target_pairs={{0,4},{1,5},{4,8},{5,9},{8,12},{9,13},{12,14},{13,15},{14,10},{15,... | collective-permute-start | bytes 1179656 | tf_op jit(solution)/shard_map/ppermute | solution.py:31
  66.7 8.9 %collective-permute-start.29 = (bf16[96,2048]{1,0:T(8,128)(2,1)S(1)}, bf16[96,2048]{1,0:T(8,128)(2,1)S(1)}, u32[]{:S(2)}, u32[]{:S(2)}) collective-permute-start(bf16[96,2048]{1,0:T(8,128)(2,1)S(1)} %get-tuple-element.78), channel_id=1, source_target_pairs={{4,0},{5,1},{8,4},{9,5},{12,8},{13,9},{14,12},{15,13},{10,14},{11,... | collective-permute-start | bytes 1179656 | tf_op jit(solution)/shard_map/ppermute | solution.py:31
  68.1 7.6 %collective-permute-start.19 = (bf16[96,2048]{1,0:T(8,128)(2,1)S(1)}, bf16[96,2048]{1,0:T(8,128)(2,1)S(1)}, u32[]{:S(2)}, u32[]{:S(2)}) collective-permute-start(bf16[96,2048]{1,0:T(8,128)(2,1)S(1)} %get-tuple-element.103), channel_id=1, source_target_pairs={{0,1},{1,0},{2,3},{3,2},{4,5},{5,4},{6,7},{7,6},{8,9},{9,8},{10,11... | collective-permute-start | bytes 1179656 | tf_op jit(solution)/shard_map/ppermute | solution.py:31
  68.1 7.6 %collective-permute-start.30 = (bf16[96,2048]{1,0:T(8,128)(2,1)S(1)}, bf16[96,2048]{1,0:T(8,128)(2,1)S(1)}, u32[]{:S(2)}, u32[]{:S(2)}) collective-permute-start(bf16[96,2048]{1,0:T(8,128)(2,1)S(1)} %get-tuple-element.100), channel_id=1, source_target_pairs={{0,1},{1,0},{2,3},{3,2},{4,5},{5,4},{6,7},{7,6},{8,9},{9,8},{10,11... | collective-permute-start | bytes 1179656 | tf_op jit(solution)/shard_map/ppermute | solution.py:31
  76.1 8.7 %collective-permute-start.31 = (bf16[96,2048]{1,0:T(8,128)(2,1)S(1)}, bf16[96,2048]{1,0:T(8,128)(2,1)S(1)}, u32[]{:S(2)}, u32[]{:S(2)}) collective-permute-start(bf16[96,2048]{1,0:T(8,128)(2,1)S(1)} %get-tuple-element.81), channel_id=1, source_target_pairs={{0,4},{1,5},{4,8},{5,9},{8,12},{9,13},{12,14},{13,15},{14,10},{15,... | collective-permute-start | bytes 1179656 | tf_op jit(solution)/shard_map/ppermute | solution.py:31
  76.7 8.5 %collective-permute-start.32 = (bf16[96,2048]{1,0:T(8,128)(2,1)S(1)}, bf16[96,2048]{1,0:T(8,128)(2,1)S(1)}, u32[]{:S(2)}, u32[]{:S(2)}) collective-permute-start(bf16[96,2048]{1,0:T(8,128)(2,1)S(1)} %get-tuple-element.82), channel_id=1, source_target_pairs={{4,0},{5,1},{8,4},{9,5},{12,8},{13,9},{14,12},{15,13},{10,14},{11,... | collective-permute-start | bytes 1179656 | tf_op jit(solution)/shard_map/ppermute | solution.py:31
  78.1 7.0 %collective-permute-start.18 = (bf16[96,2048]{1,0:T(8,128)(2,1)S(1)}, bf16[96,2048]{1,0:T(8,128)(2,1)S(1)}, u32[]{:S(2)}, u32[]{:S(2)}) collective-permute-start(bf16[96,2048]{1,0:T(8,128)(2,1)S(1)} %get-tuple-element.99), channel_id=1, source_target_pairs={{0,1},{1,0},{2,3},{3,2},{4,5},{5,4},{6,7},{7,6},{8,9},{9,8},{10,11... | collective-permute-start | bytes 1179656 | tf_op jit(solution)/shard_map/ppermute | solution.py:31
  78.2 7.2 %collective-permute-start.33 = (bf16[24,2048]{1,0:T(8,128)(2,1)S(1)}, bf16[24,2048]{1,0:T(8,128)(2,1)S(1)}, u32[]{:S(2)}, u32[]{:S(2)}) collective-permute-start(bf16[24,2048]{1,0:T(8,128)(2,1)S(1)} %get-tuple-element.116), channel_id=1, source_target_pairs={{0,1},{1,0},{2,3},{3,2},{4,5},{5,4},{6,7},{7,6},{8,9},{9,8},{10,11... | collective-permute-start | bytes 294920 | tf_op jit(solution)/shard_map/ppermute | solution.py:31
  85.5 10.0 %collective-permute-start.34 = (bf16[96,2048]{1,0:T(8,128)(2,1)S(1)}, bf16[96,2048]{1,0:T(8,128)(2,1)S(1)}, u32[]{:S(2)}, u32[]{:S(2)}) collective-permute-start(bf16[96,2048]{1,0:T(8,128)(2,1)S(1)} %pad_maximum_fusion.refs_0_), channel_id=1, source_target_pairs={{0,4},{1,5},{4,8},{5,9},{8,12},{9,13},{12,14},{13,15},{14,10},{15,... | collective-permute-start | bytes 1179656 | tf_op jit(solution)/shard_map/ppermute | solution.py:31
  86.1 10.2 %collective-permute-start.35 = (bf16[96,2048]{1,0:T(8,128)(2,1)S(1)}, bf16[96,2048]{1,0:T(8,128)(2,1)S(1)}, u32[]{:S(2)}, u32[]{:S(2)}) collective-permute-start(bf16[96,2048]{1,0:T(8,128)(2,1)S(1)} %pad_maximum_fusion.refs_0_), channel_id=1, source_target_pairs={{4,0},{5,1},{8,4},{9,5},{12,8},{13,9},{14,12},{15,13},{10,14},{11,... | collective-permute-start | bytes 1179656 | tf_op jit(solution)/shard_map/ppermute | solution.py:31
  96.3 7.8 %collective-permute-start.36 = (bf16[96,2048]{1,0:T(8,128)(2,1)S(1)}, bf16[96,2048]{1,0:T(8,128)(2,1)S(1)}, u32[]{:S(2)}, u32[]{:S(2)}) collective-permute-start(bf16[96,2048]{1,0:T(8,128)(2,1)S(1)} %collective-permute-done.34.refs_1_), channel_id=1, source_target_pairs={{0,4},{1,5},{4,8},{5,9},{8,12},{9,13},{12,14},{13,15},{14,10},{15,... | collective-permute-start | bytes 1179656 | tf_op jit(solution)/shard_map/ppermute | solution.py:31
  96.6 7.8 %collective-permute-start.37 = (bf16[96,2048]{1,0:T(8,128)(2,1)S(1)}, bf16[96,2048]{1,0:T(8,128)(2,1)S(1)}, u32[]{:S(2)}, u32[]{:S(2)}) collective-permute-start(bf16[96,2048]{1,0:T(8,128)(2,1)S(1)} %collective-permute-done.35.refs_2_), channel_id=1, source_target_pairs={{4,0},{5,1},{8,4},{9,5},{12,8},{13,9},{14,12},{15,13},{10,14},{11,... | collective-permute-start | bytes 1179656 | tf_op jit(solution)/shard_map/ppermute | solution.py:31
  98.4 6.5 %collective-permute-start.38 = (bf16[96,2048]{1,0:T(8,128)(2,1)S(1)}, bf16[96,2048]{1,0:T(8,128)(2,1)S(1)}, u32[]{:S(2)}, u32[]{:S(2)}) collective-permute-start(bf16[96,2048]{1,0:T(8,128)(2,1)S(1)} %pad_maximum_fusion.refs_0_), channel_id=1, source_target_pairs={{0,1},{1,0},{2,3},{3,2},{4,5},{5,4},{6,7},{7,6},{8,9},{9,8},{10,11... | collective-permute-start | bytes 1179656 | tf_op jit(solution)/shard_map/ppermute | solution.py:31
  98.4 6.5 %collective-permute-start.39 = (bf16[96,2048]{1,0:T(8,128)(2,1)S(1)}, bf16[96,2048]{1,0:T(8,128)(2,1)S(1)}, u32[]{:S(2)}, u32[]{:S(2)}) collective-permute-start(bf16[96,2048]{1,0:T(8,128)(2,1)S(1)} %collective-permute-done.34.refs_1_), channel_id=1, source_target_pairs={{0,1},{1,0},{2,3},{3,2},{4,5},{5,4},{6,7},{7,6},{8,9},{9,8},{10,11... | collective-permute-start | bytes 1179656 | tf_op jit(solution)/shard_map/ppermute | solution.py:31
  98.9 8.1 %collective-permute-start.40 = (bf16[96,2048]{1,0:T(8,128)(2,1)S(1)}, bf16[96,2048]{1,0:T(8,128)(2,1)S(1)}, u32[]{:S(2)}, u32[]{:S(2)}) collective-permute-start(bf16[96,2048]{1,0:T(8,128)(2,1)S(1)} %collective-permute-done.35.refs_2_), channel_id=1, source_target_pairs={{0,1},{1,0},{2,3},{3,2},{4,5},{5,4},{6,7},{7,6},{8,9},{9,8},{10,11... | collective-permute-start | bytes 1179656 | tf_op jit(solution)/shard_map/ppermute | solution.py:31
  104.4 2.6 %collective-permute-start.41 = (bf16[96,2048]{1,0:T(8,128)(2,1)S(1)}, bf16[96,2048]{1,0:T(8,128)(2,1)S(1)}, u32[]{:S(2)}, u32[]{:S(2)}) collective-permute-start(bf16[96,2048]{1,0:T(8,128)(2,1)S(1)} %collective-permute-done.36.refs_3_), channel_id=1, source_target_pairs={{0,1},{1,0},{2,3},{3,2},{4,5},{5,4},{6,7},{7,6},{8,9},{9,8},{10,11... | collective-permute-start | bytes 1179656 | tf_op jit(solution)/shard_map/ppermute | solution.py:31
  104.4 2.6 %collective-permute-start.42 = (bf16[96,2048]{1,0:T(8,128)(2,1)S(1)}, bf16[96,2048]{1,0:T(8,128)(2,1)S(1)}, u32[]{:S(2)}, u32[]{:S(2)}) collective-permute-start(bf16[96,2048]{1,0:T(8,128)(2,1)S(1)} %collective-permute-done.37.refs_4_), channel_id=1, source_target_pairs={{0,1},{1,0},{2,3},{3,2},{4,5},{5,4},{6,7},{7,6},{8,9},{9,8},{10,11... | collective-permute-start | bytes 1179656 | tf_op jit(solution)/shard_map/ppermute | solution.py:31
  104.9 11.0 %collective-permute-start.43 = (bf16[96,2048]{1,0:T(8,128)(2,1)S(1)}, bf16[96,2048]{1,0:T(8,128)(2,1)S(1)}, u32[]{:S(2)}, u32[]{:S(2)}) collective-permute-start(bf16[96,2048]{1,0:T(8,128)(2,1)S(1)} %collective-permute-done.36.refs_3_), channel_id=1, source_target_pairs={{0,4},{1,5},{4,8},{5,9},{8,12},{9,13},{12,14},{13,15},{14,10},{15,... | collective-permute-start | bytes 1179656 | tf_op jit(solution)/shard_map/ppermute | solution.py:31
  104.9 11.1 %collective-permute-start.44 = (bf16[96,2048]{1,0:T(8,128)(2,1)S(1)}, bf16[96,2048]{1,0:T(8,128)(2,1)S(1)}, u32[]{:S(2)}, u32[]{:S(2)}) collective-permute-start(bf16[96,2048]{1,0:T(8,128)(2,1)S(1)} %collective-permute-done.37.refs_4_), channel_id=1, source_target_pairs={{4,0},{5,1},{8,4},{9,5},{12,8},{13,9},{14,12},{15,13},{10,14},{11,... | collective-permute-start | bytes 1179656 | tf_op jit(solution)/shard_map/ppermute | solution.py:31
  116.0 6.0 %collective-permute-start.45 = (bf16[96,1024]{1,0:T(8,128)(2,1)S(1)}, bf16[96,1024]{1,0:T(8,128)(2,1)S(1)}, u32[]{:S(2)}, u32[]{:S(2)}) collective-permute-start(bf16[96,1024]{1,0:T(8,128)(2,1)S(1)} %slice.95), channel_id=1, source_target_pairs={{0,4},{1,5},{4,8},{5,9},{8,12},{9,13},{12,14},{13,15},{14,10},{15,... | collective-permute-start | bytes 589832 | tf_op jit(solution)/shard_map/ppermute | solution.py:31
  117.6 6.3 %collective-permute-start.46 = (bf16[96,1024]{1,0:T(8,128)(2,1)S(1)}, bf16[96,1024]{1,0:T(8,128)(2,1)S(1)}, u32[]{:S(2)}, u32[]{:S(2)}) collective-permute-start(bf16[96,1024]{1,0:T(8,128)(2,1)S(1)} %slice.96), channel_id=1, source_target_pairs={{4,0},{5,1},{8,4},{9,5},{12,8},{13,9},{14,12},{15,13},{10,14},{11,... | collective-permute-start | bytes 589832 | tf_op jit(solution)/shard_map/ppermute | solution.py:31
  118.4 5.6 %collective-permute-start.47 = (bf16[96,2048]{1,0:T(8,128)(2,1)S(1)}, bf16[96,2048]{1,0:T(8,128)(2,1)S(1)}, u32[]{:S(2)}, u32[]{:S(2)}) collective-permute-start(bf16[96,2048]{1,0:T(8,128)(2,1)S(1)} %collective-permute-done.43.refs_0_), channel_id=1, source_target_pairs={{0,1},{1,0},{2,3},{3,2},{4,5},{5,4},{6,7},{7,6},{8,9},{9,8},{10,11... | collective-permute-start | bytes 1179656 | tf_op jit(solution)/shard_map/ppermute | solution.py:31
  118.4 5.6 %collective-permute-start.48 = (bf16[96,2048]{1,0:T(8,128)(2,1)S(1)}, bf16[96,2048]{1,0:T(8,128)(2,1)S(1)}, u32[]{:S(2)}, u32[]{:S(2)}) collective-permute-start(bf16[96,2048]{1,0:T(8,128)(2,1)S(1)} %collective-permute-done.44.refs_1_), channel_id=1, source_target_pairs={{0,1},{1,0},{2,3},{3,2},{4,5},{5,4},{6,7},{7,6},{8,9},{9,8},{10,11... | collective-permute-start | bytes 1179656 | tf_op jit(solution)/shard_map/ppermute | solution.py:31
  123.9 1.8 %collective-permute-start.49 = (bf16[96,2048]{1,0:T(8,128)(2,1)S(1)}, bf16[96,2048]{1,0:T(8,128)(2,1)S(1)}, u32[]{:S(2)}, u32[]{:S(2)}) collective-permute-start(bf16[96,2048]{1,0:T(8,128)(2,1)S(1)} %constant_dynamic-update-slice_fusion.2.refs_2_), channel_id=1, source_target_pairs={{0,1},{1,0},{2,3},{3,2},{4,5},{5,4},{6,7},{7,6},{8,9},{9,8},{10,11... | collective-permute-start | bytes 1179656 | tf_op jit(solution)/shard_map/ppermute | solution.py:31
  (3 other events, 15.1 us)

commit v3 on v2

--- a/solution.py
+++ b/solution.py
@@ -95,16 +95,47 @@
             yield own, slice(k, k + tile), pl.ds(pl.multiple_of(start + k, tile), tile)
 
 
-def forward(core, same, other, weights, late=None, beside=None):
-    count, rows = len(same), same[0].shape[0]
+def forward_own(core, same, weights):
+    count = len(same)
+    total = sum(b.shape[0] for b in same)
+    depth, columns = weights[0].shape
+
+    def kernel(core_ref, *refs):
+        blocks, weight_refs, sums = refs[:count], refs[count : count + 3], refs[count + 3 :]
+        for own, near, at in passes(core_ref[0], depth // 2, 1024):
+            if own:
+                left = jnp.concatenate([b[:, near] for b in blocks])
+                for s, w in zip(sums, weight_refs):
+                    product = jnp.dot(left, w[at, :], preferred_element_type=F32)
+                    if near.start == 0:
+                        s[...] = product
+                    else:
+                        s[...] += product
+
+    return call(
+        kernel,
+        "forward_own",
+        core,
+        [((total, columns), F32)] * 3,
+        [],
+        3 * total * depth * columns,
+        [*same, *weights],
+    )
+
+
+def forward(core, same, other, weights, late=None, beside=None, begun=()):
+    count, rows = len(other), other[0].shape[0]
+    same = [] if begun else same
+    first = len(same)
     total = count * rows
     depth, columns = weights[0].shape
     known = len(weights)
     coming = [w for w in (late, beside) if w is not None]
 
     def kernel(core_ref, *refs):
-        blocks, refs = refs[: 2 * count], refs[2 * count :]
+        blocks, refs = refs[: first + count], refs[first + count :]
         weight_refs, refs = list(refs[:known]), refs[known:]
+        begun_refs, refs = refs[: len(begun)], refs[len(begun) :]
         source, refs = refs[: len(coming)], refs[len(coming) :]
         (hidden_ref, by_dot_ref, by_error_ref), refs = refs[:3], refs[3:]
         arriving, refs = refs[: len(coming)], refs[len(coming) :]
@@ -117,11 +148,15 @@
 
         def add(some):
             for own, near, at in passes(core_ref[0], depth // 2, 1024):
-                part = blocks[:count] if own else blocks[count:]
+                part = blocks[:first] if own else blocks[first:]
+                if not part:
+                    continue
                 left = jnp.concatenate([b[:, near] for b in part])
-                for s, w in some:
+                for n, (s, w) in enumerate(some):
                     product = jnp.dot(left, w[at, :], preferred_element_type=F32)
-                    if own and near.start == 0:
+                    if begun and near.start == 0:
+                        s[...] = begun_refs[n][...] + product
+                    elif own and near.start == 0:
                         s[...] = product
                     else:
                         s[...] += product
@@ -152,8 +187,8 @@
         [((2 * total, columns), BF16), ((total, columns), F32), ((total, columns), F32)]
         + [(w.shape, w.dtype) for w in coming],
         [(total, columns)] * 3,
-        6 * total * depth * columns,
-        [*same, *other, *weights],
+        (3 if begun else 6) * total * depth * columns,
+        [*same, *other, *weights, *begun],
         coming,
     )
 
@@ -184,22 +219,58 @@
     )
 
 
-def back(core, same, other, down_weight, by_dot, by_error):
-    count, rows = len(same), same[0].shape[0]
+def back_own(core, same, down_weight):
+    total = sum(b.shape[0] for b in same)
+    columns, depth = down_weight.shape
+
+    def kernel(core_ref, *refs):
+        blocks, weight_ref, sum_ref = refs[:-2], refs[-2], refs[-1]
+        for own, near, at in passes(core_ref[0], depth // 2, 1024):
+            if own:
+                left = jnp.concatenate([b[:, near] for b in blocks])
+                product = lax.dot_general(
+                    left, weight_ref[:, at], (((1,), (1,)), ((), ())), preferred_element_type=F32
+                )
+                if near.start == 0:
+                    sum_ref[...] = product
+                else:
+                    sum_ref[...] += product
+
+    return call(
+        kernel,
+        "back_own",
+        core,
+        [((total, columns), F32)],
+        [],
+        total * depth * columns,
+        [*same, down_weight],
+    )
+
+
+def back(core, same, other, down_weight, by_dot, by_error, begun=()):
+    count, rows = len(other), other[0].shape[0]
     total = count * rows
+    same = [] if begun else same
+    first = len(same)
     columns, depth = down_weight.shape
     parts = len(by_dot)
 
     def kernel(core_ref, *refs):
-        blocks, refs = refs[: 2 * count], refs[2 * count :]
+        blocks, refs = refs[: first + count], refs[first + count :]
+        begun_refs, refs = refs[: len(begun)], refs[len(begun) :]
         weight_ref, by_dot_refs, by_error_refs = refs[0], refs[1 : 1 + parts], refs[1 + parts : -2]
         out_ref, sum_ref = refs[-2:]
         for own, near, at in passes(core_ref[0], depth // 2, 1024):
-            left = jnp.concatenate([b[:, near] for b in (blocks[:count] if own else blocks[count:])])
+            part = blocks[:first] if own else blocks[first:]
+            if not part:
+                continue
+            left = jnp.concatenate([b[:, near] for b in part])
             product = lax.dot_general(
                 left, weight_ref[:, at], (((1,), (1,)), ((), ())), preferred_element_type=F32
             )
-            if own and near.start == 0:
+            if begun and near.start == 0:
+                sum_ref[...] = begun_refs[0][...] + product
+            elif own and near.start == 0:
                 sum_ref[...] = product
             else:
                 sum_ref[...] += product
@@ -221,8 +292,8 @@
         core,
         [((total // 2, columns), BF16)],
         [(total, columns)],
-        2 * total * depth * columns,
-        [*same, *other, down_weight, *by_dot, *by_error],
+        (1 if begun else 2) * total * depth * columns,
+        [*same, *other, *begun, down_weight, *by_dot, *by_error],
     )[0]
 
 
@@ -334,7 +405,10 @@
             late = None if "probe" in weights else probe
             beside = down_weight if late is None and "down" not in weights else None
             known = [weights[n] for n in ("gate", "up", "probe") if n in weights]
-            h, d, e, *came = forward(core, same[at], other[at], known, late, beside)
+            begun = ()
+            if step > steps + 1 and late is None:
+                begun = forward_own(core, same[at], known)
+            h, d, e, *came = forward(core, same[at], other[at], known, late, beside, begun)
             hidden.append(h), by_dot.append(d), by_error.append(e)
             if came:
                 weights["down" if late is None else "probe"] = came[0]
@@ -407,6 +481,7 @@
             at = slice(gs[0][0], gs[-1][-1] + 1)
             first = sum(len(x) for x in back_groups[: len(weighted)])
             saved = slice(first, first + len(gs))
+            begun = back_own(core, same[0][at], weights["down"]) if step > steps + 1 else ()
             weighted.append(
                 back(
                     core,
@@ -415,6 +490,7 @@
                     weights["down"],
                     by_dot[saved],
                     by_error[saved],
+                    begun,
                 )
             )
             done.append(weighted[-1])

time: 134 us -> 132 us (0.985)
  waiting for transfers between devices: 59.7 us -> 56.5 us
    ppermute x50, waiting for transfers between devices: 59.7 us -> 56.5 us  [send(): return lax.ppermute(block, AXIS, route)]
    pallas_call x8 -> x10, Pallas kernels: 27.8 us -> 28.2 us  [call(): pl.pallas_call(kernel, in_specs=[IN_SMEM] + [IN_VMEM] * len(operands) + [...]
  transfers between devices with their start and end apart: 50 -> 50, of which waited for: 23 -> 20; matrix products, arithmetic and copies ran while one was open for 0% -> 0% of each run, Pallas kernels for 19% -> 22%
where the time goes in v3:
time: 132 us
  waiting for transfers between devices  56.5 us (43%)
  Pallas kernels  39.6 us (30%)
  starting transfers between devices  32.2 us (24%)
  other arithmetic  1.53 us (1%)
  local copies, waits for them, and re-layouts  1.41 us (1%)
    ppermute x50, waiting for transfers between devices, send(): return lax.ppermute(block, AXIS, route)  56.5 us
    ppermute x50, starting transfers between devices, send(): return lax.ppermute(block, AXIS, route)  32.2 us
    pallas_call x10, Pallas kernels, call(): pl.pallas_call(kernel, in_specs=[IN_SMEM] + [IN_VMEM] * len(operands) + [...  28.2 us
    pallas_call x1, Pallas kernels, fetch(): pl.pallas_call(kernel, in_specs=[pl.BlockSpec(memory_space=pl.ANY)] + [pl...  5.78 us
    pallas_call x1, Pallas kernels, outer(): pl.pallas_call(kernel, in_specs=[IN_SMEM] + [IN_VMEM] * len(operands), ou...  5.62 us
  transfers between devices with their start and end apart: 50, of which 20 were waited for; matrix products, arithmetic and copies ran while one was open for 0% of the time, Pallas kernels for 22%

profile of v3, /device:TPU:0, one launch (start us, length us, event | category | flops | bytes accessed | tf_op | source)
XLA Modules:
  0.0 131.8 jit_solution(2321525791723018285)
XLA Ops:
  0.0 1.0 constant_dynamic-slice_fusion.3
  1.5 0.9 collective-permute-done
  2.5 3.0 %collective-permute-start.1 = (bf16[48,2048]{1,0:T(8,128)(2,1)S(1)}, bf16[48,2048]{1,0:T(8,128)(2,1)S(1)}, u32[]{:S(2)}, u32[]{:S(2)}) collective-permute-start(bf16[48,2048]{1,0:T(8,128)(2,1)S(1)} %maximum_select_fusion.after_ref.refs_0_), channel_id=1, source_target_pairs={{0,4},{1,5},{4,8},{5,9},{8,12},{9,13},{12,14},{13,15},{14,10},{15,... | collective-permute-start | bytes 589832 | tf_op jit(solution)/shard_map/ppermute | solution.py:31
  5.4 5.8 %fetch.1 = (bf16[4096,1024]{1,0:T(8,128)(2,1)S(1)}, bf16[4096,1024]{1,0:T(8,128)(2,1)S(1)}) custom-call(bf16[48,2048]{1,0:T(8,128)(2,1)S(1)} %maximum_select_fusion.after_ref.refs_0_, bf16[4096,1024]{1,0:T(8,128)(2,1)} %refs_0_.1, bf16[4096,1024]{1,0:T(8,128)(2,1)} %refs_1_.1), custom_call_target="tpu_custom_call" | custom-call | bytes 16777216 | tf_op jit(solution)/shard_map/fetch/pallas_call | solution.py:77
  11.2 0.9 collective-permute-done.2.refs_2_
  12.1 1.6 %collective-permute-start.3 = (bf16[48,2048]{1,0:T(8,128)(2,1)S(1)}, bf16[48,2048]{1,0:T(8,128)(2,1)S(1)}, u32[]{:S(2)}, u32[]{:S(2)}) collective-permute-start(bf16[48,2048]{1,0:T(8,128)(2,1)S(1)} %collective-permute-done.1.refs_1_), channel_id=1, source_target_pairs={{0,4},{1,5},{4,8},{5,9},{8,12},{9,13},{12,14},{13,15},{14,10},{15,... | collective-permute-start | bytes 589832 | tf_op jit(solution)/shard_map/ppermute | solution.py:31
  14.7 3.3 %collective-permute-done.3.refs_0_.refs_3_ = bf16[48,2048]{1,0:T(8,128)(2,1)S(1)} collective-permute-done((bf16[48,2048]{1,0:T(8,128)(2,1)S(1)}, bf16[48,2048]{1,0:T(8,128)(2,1)S(1)}, u32[]{:S(2)}, u32[]{:S(2)}) %collective-permute-start.3) | collective-permute-done | bytes 196640 | tf_op jit(solution)/shard_map/ppermute | solution.py:31
  18.0 1.5 %collective-permute-done.4.refs_1_.refs_4_ = bf16[48,2048]{1,0:T(8,128)(2,1)S(1)} collective-permute-done((bf16[48,2048]{1,0:T(8,128)(2,1)S(1)}, bf16[48,2048]{1,0:T(8,128)(2,1)S(1)}, u32[]{:S(2)}, u32[]{:S(2)}) %collective-permute-start.4) | collective-permute-done | bytes 196640 | tf_op jit(solution)/shard_map/ppermute | solution.py:31
  19.5 1.6 %collective-permute-start.5 = (bf16[48,2048]{1,0:T(8,128)(2,1)S(1)}, bf16[48,2048]{1,0:T(8,128)(2,1)S(1)}, u32[]{:S(2)}, u32[]{:S(2)}) collective-permute-start(bf16[48,2048]{1,0:T(8,128)(2,1)S(1)} %collective-permute-done.3.refs_0_.refs_3_), channel_id=1, source_target_pairs={{0,4},{1,5},{4,8},{5,9},{8,12},{9,13},{12,14},{13,15},{14,10},{15,... | collective-permute-start | bytes 589832 | tf_op jit(solution)/shard_map/ppermute | solution.py:31
  21.7 5.0 %forward.3 = (bf16[288,1024]{1,0:T(8,128)(2,1)S(1)}, f32[144,1024]{1,0:T(8,128)S(1)}, f32[144,1024]{1,0:T(8,128)S(1)}, bf16[4096,1024]{1,0:T(8,128)(2,1)S(1)}) custom-call(s32[1]{0:T(128)} %bitcast.core_ref, bf16[48,2048]{1,0:T(8,128)(2,1)S(1)} %maximum_select_fusion.after_ref.refs_0_, bf16[48,2048]{1,0:T(8,128)(2,1)S(1)} %collective-permute-done.1.refs_1_, ...), custom_call_target="tpu_custom_call" | custom-call | flops 3623878656 | bytes 17956864 | tf_op jit(solution)/shard_map/forward/pallas_call | solution.py:41
  26.8 1.6 %collective-permute-done.6.refs_1_.refs_6_ = bf16[48,2048]{1,0:T(8,128)(2,1)S(1)} collective-permute-done((bf16[48,2048]{1,0:T(8,128)(2,1)S(1)}, bf16[48,2048]{1,0:T(8,128)(2,1)S(1)}, u32[]{:S(2)}, u32[]{:S(2)}) %collective-permute-start.6) | collective-permute-done | bytes 196640 | tf_op jit(solution)/shard_map/ppermute | solution.py:31
  29.0 1.6 %collective-permute-start.10 = (bf16[48,1024]{1,0:T(8,128)(2,1)S(1)}, bf16[48,1024]{1,0:T(8,128)(2,1)S(1)}, u32[]{:S(2)}, u32[]{:S(2)}) collective-permute-start(bf16[48,1024]{1,0:T(8,128)(2,1)S(1)} %slice.73), channel_id=1, source_target_pairs={{0,4},{1,5},{4,8},{5,9},{8,12},{9,13},{12,14},{13,15},{14,10},{15,... | collective-permute-start | bytes 294920 | tf_op jit(solution)/shard_map/ppermute | solution.py:31
  31.0 4.5 %forward.4 = (bf16[192,1024]{1,0:T(8,128)(2,1)S(1)}, f32[96,1024]{1,0:T(8,128)S(1)}, f32[96,1024]{1,0:T(8,128)S(1)}, bf16[1024,4096]{1,0:T(8,128)(2,1)S(1)}) custom-call(s32[1]{0:T(128)} %bitcast.core_ref, bf16[48,2048]{1,0:T(8,128)(2,1)S(1)} %collective-permute-done.3.refs_0_.refs_3_, bf16[48,2048]{1,0:T(8,128)(2,1)S(1)} %collective-permute-done.4.refs_1_.refs_4_, ...), custom_call_target="tpu_custom_call" | custom-call | flops 2415919104 | bytes 25952256 | tf_op jit(solution)/shard_map/forward/pallas_call | solution.py:41
  35.7 2.0 %forward_own.1 = (f32[144,1024]{1,0:T(8,128)S(1)}, f32[144,1024]{1,0:T(8,128)S(1)}, f32[144,1024]{1,0:T(8,128)S(1)}) custom-call(s32[1]{0:T(128)} %bitcast.core_ref, bf16[48,2048]{1,0:T(8,128)(2,1)S(1)} %collective-permute-done.5.refs_0_.refs_5_, bf16[48,2048]{1,0:T(8,128)(2,1)S(1)} %collective-permute-done.6.refs_1_.refs_6_, ...), custom_call_target="tpu_custom_call" | custom-call | flops 1811939328 | bytes 25755648 | tf_op jit(solution)/shard_map/forward_own/pallas_call | solution.py:41
  37.8 2.5 %forward.5 = (bf16[288,1024]{1,0:T(8,128)(2,1)S(1)}, f32[144,1024]{1,0:T(8,128)S(1)}, f32[144,1024]{1,0:T(8,128)S(1)}) custom-call(s32[1]{0:T(128)} %bitcast.core_ref, bf16[48,2048]{1,0:T(8,128)(2,1)S(1)} %collective-permute-done.14.refs_0_.refs_13_, bf16[48,2048]{1,0:T(8,128)(2,1)S(1)} %collective-permute-done.15.refs_1_.refs_14_, ...), custom_call_target="tpu_custom_call" | custom-call | flops 1811939328 | bytes 26640384 | tf_op jit(solution)/shard_map/forward/pallas_call | solution.py:41
  40.2 1.4 %down.4 = bf16[288,2048]{1,0:T(8,128)(2,1)S(1)} custom-call(s32[1]{0:T(128)} %bitcast.core_ref, bf16[288,1024]{1,0:T(8,128)(2,1)S(1)} %get-tuple-element.71.refs_0_, bf16[1024,4096]{1,0:T(8,128)(2,1)S(1)} %get-tuple-element.72.refs_1_.refs_2_.refs_10_.refs_3_.refs_4_), custom_call_target="tpu_custom_call" | custom-call | flops 1207959552 | bytes 8978432 | tf_op jit(solution)/shard_map/down/pallas_call | solution.py:41
  41.7 0.6 collective-permute-start.17
  42.8 1.4 %down.3 = bf16[288,2048]{1,0:T(8,128)(2,1)S(1)} custom-call(s32[1]{0:T(128)} %bitcast.core_ref, bf16[288,1024]{1,0:T(8,128)(2,1)S(1)} %get-tuple-element.71.refs_0_, bf16[1024,4096]{1,0:T(8,128)(2,1)S(1)} %get-tuple-element.72.refs_1_.refs_2_.refs_10_.refs_3_.refs_4_), custom_call_target="tpu_custom_call" | custom-call | flops 1207959552 | bytes 8978432 | tf_op jit(solution)/shard_map/down/pallas_call | solution.py:41
  44.3 1.6 %collective-permute-start.22 = (bf16[96,1024]{1,0:T(8,128)(2,1)S(1)}, bf16[96,1024]{1,0:T(8,128)(2,1)S(1)}, u32[]{:S(2)}, u32[]{:S(2)}) collective-permute-start(bf16[96,1024]{1,0:T(8,128)(2,1)S(1)} %get-tuple-element.120), channel_id=1, source_target_pairs={{0,4},{1,5},{4,8},{5,9},{8,12},{9,13},{12,14},{13,15},{14,10},{15,... | collective-permute-start | bytes 589832 | tf_op jit(solution)/shard_map/ppermute | solution.py:31
  46.4 4.3 %down.5 = (bf16[480,2048]{1,0:T(8,128)(2,1)S(1)}, bf16[480,2048]{1,0:T(8,128)(2,1)S(1)}) custom-call(s32[1]{0:T(128)} %bitcast.core_ref, bf16[288,1024]{1,0:T(8,128)(2,1)S(1)} %get-tuple-element.73.refs_0_, bf16[192,1024]{1,0:T(8,128)(2,1)S(1)} %get-tuple-element.74.refs_1_, bf16[1024,4096]{1,0:T(8,128)(2,1)S(1)} %get-tuple-element.72.refs_1_.refs_2_.refs_10_.refs_3_.refs_4_), custom_call_target="tpu_custom_call" | custom-call | flops 4026531840 | bytes 9371648 | tf_op jit(solution)/shard_map/down/pallas_call | solution.py:41
  51.3 1.3 collective-permute-done.23
  52.9 1.6 %collective-permute-start.25 = (bf16[96,2048]{1,0:T(8,128)(2,1)S(1)}, bf16[96,2048]{1,0:T(8,128)(2,1)S(1)}, u32[]{:S(2)}, u32[]{:S(2)}) collective-permute-start(bf16[96,2048]{1,0:T(8,128)(2,1)S(1)} %get-tuple-element.79), channel_id=1, source_target_pairs={{0,4},{1,5},{4,8},{5,9},{8,12},{9,13},{12,14},{13,15},{14,10},{15,... | collective-permute-start | bytes 1179656 | tf_op jit(solution)/shard_map/ppermute | solution.py:31
  55.5 7.4 %collective-permute-done.25 = bf16[96,2048]{1,0:T(8,128)(2,1)S(1)} collective-permute-done((bf16[96,2048]{1,0:T(8,128)(2,1)S(1)}, bf16[96,2048]{1,0:T(8,128)(2,1)S(1)}, u32[]{:S(2)}, u32[]{:S(2)}) %collective-permute-start.25) | collective-permute-done | bytes 393248 | tf_op jit(solution)/shard_map/ppermute | solution.py:31
  62.9 1.2 collective-permute-done.26
  64.6 0.8 collective-permute-start.28
  65.3 1.3 %collective-permute-start.29 = (bf16[96,2048]{1,0:T(8,128)(2,1)S(1)}, bf16[96,2048]{1,0:T(8,128)(2,1)S(1)}, u32[]{:S(2)}, u32[]{:S(2)}) collective-permute-start(bf16[96,2048]{1,0:T(8,128)(2,1)S(1)} %get-tuple-element.84), channel_id=1, source_target_pairs={{4,0},{5,1},{8,4},{9,5},{12,8},{13,9},{14,12},{15,13},{10,14},{11,... | collective-permute-start | bytes 1179656 | tf_op jit(solution)/shard_map/ppermute | solution.py:31
  67.2 6.2 %collective-permute-done.28 = bf16[96,2048]{1,0:T(8,128)(2,1)S(1)} collective-permute-done((bf16[96,2048]{1,0:T(8,128)(2,1)S(1)}, bf16[96,2048]{1,0:T(8,128)(2,1)S(1)}, u32[]{:S(2)}, u32[]{:S(2)}) %collective-permute-start.28) | collective-permute-done | bytes 393248 | tf_op jit(solution)/shard_map/ppermute | solution.py:31
  73.4 0.6 collective-permute-done.29
  74.3 0.6 collective-permute-start.31
  74.9 1.5 %collective-permute-start.32 = (bf16[96,2048]{1,0:T(8,128)(2,1)S(1)}, bf16[96,2048]{1,0:T(8,128)(2,1)S(1)}, u32[]{:S(2)}, u32[]{:S(2)}) collective-permute-start(bf16[96,2048]{1,0:T(8,128)(2,1)S(1)} %get-tuple-element.88), channel_id=1, source_target_pairs={{4,0},{5,1},{8,4},{9,5},{12,8},{13,9},{14,12},{15,13},{10,14},{11,... | collective-permute-start | bytes 1179656 | tf_op jit(solution)/shard_map/ppermute | solution.py:31
  76.4 0.6 collective-permute-start.33
  77.0 5.9 %collective-permute-done.31 = bf16[96,2048]{1,0:T(8,128)(2,1)S(1)} collective-permute-done((bf16[96,2048]{1,0:T(8,128)(2,1)S(1)}, bf16[96,2048]{1,0:T(8,128)(2,1)S(1)}, u32[]{:S(2)}, u32[]{:S(2)}) %collective-permute-start.31) | collective-permute-done | bytes 393248 | tf_op jit(solution)/shard_map/ppermute | solution.py:31
  82.9 0.8 collective-permute-done.32
  84.6 1.6 %collective-permute-start.35 = (bf16[96,2048]{1,0:T(8,128)(2,1)S(1)}, bf16[96,2048]{1,0:T(8,128)(2,1)S(1)}, u32[]{:S(2)}, u32[]{:S(2)}) collective-permute-start(bf16[96,2048]{1,0:T(8,128)(2,1)S(1)} %pad_maximum_fusion.refs_0_), channel_id=1, source_target_pairs={{4,0},{5,1},{8,4},{9,5},{12,8},{13,9},{14,12},{15,13},{10,14},{11,... | collective-permute-start | bytes 1179656 | tf_op jit(solution)/shard_map/ppermute | solution.py:31
  86.2 8.3 %collective-permute-done.34.refs_1_ = bf16[96,2048]{1,0:T(8,128)(2,1)S(1)} collective-permute-done((bf16[96,2048]{1,0:T(8,128)(2,1)S(1)}, bf16[96,2048]{1,0:T(8,128)(2,1)S(1)}, u32[]{:S(2)}, u32[]{:S(2)}) %collective-permute-start.34) | collective-permute-done | bytes 393248 | tf_op jit(solution)/shard_map/ppermute | solution.py:31
  94.4 0.7 collective-permute-done.35.refs_2_
  95.2 2.0 %collective-permute-start.37 = (bf16[96,2048]{1,0:T(8,128)(2,1)S(1)}, bf16[96,2048]{1,0:T(8,128)(2,1)S(1)}, u32[]{:S(2)}, u32[]{:S(2)}) collective-permute-start(bf16[96,2048]{1,0:T(8,128)(2,1)S(1)} %collective-permute-done.35.refs_2_), channel_id=1, source_target_pairs={{4,0},{5,1},{8,4},{9,5},{12,8},{13,9},{14,12},{15,13},{10,14},{11,... | collective-permute-start | bytes 1179656 | tf_op jit(solution)/shard_map/ppermute | solution.py:31
  97.7 5.2 %collective-permute-done.36.refs_3_ = bf16[96,2048]{1,0:T(8,128)(2,1)S(1)} collective-permute-done((bf16[96,2048]{1,0:T(8,128)(2,1)S(1)}, bf16[96,2048]{1,0:T(8,128)(2,1)S(1)}, u32[]{:S(2)}, u32[]{:S(2)}) %collective-permute-start.36) | collective-permute-done | bytes 393248 | tf_op jit(solution)/shard_map/ppermute | solution.py:31
  103.5 2.1 %collective-permute-start.44 = (bf16[96,2048]{1,0:T(8,128)(2,1)S(1)}, bf16[96,2048]{1,0:T(8,128)(2,1)S(1)}, u32[]{:S(2)}, u32[]{:S(2)}) collective-permute-start(bf16[96,2048]{1,0:T(8,128)(2,1)S(1)} %collective-permute-done.37.refs_4_), channel_id=1, source_target_pairs={{4,0},{5,1},{8,4},{9,5},{12,8},{13,9},{14,12},{15,13},{10,14},{11,... | collective-permute-start | bytes 1179656 | tf_op jit(solution)/shard_map/ppermute | solution.py:31
  105.5 4.3 %back.2.refs_16_ = bf16[240,1024]{1,0:T(8,128)(2,1)S(1)} custom-call(s32[1]{0:T(128)} %bitcast.core_ref, bf16[96,2048]{1,0:T(8,128)(2,1)S(1)} %pad_maximum_fusion.refs_0_, bf16[96,2048]{1,0:T(8,128)(2,1)S(1)} %collective-permute-done.34.refs_1_, bf16[96,2048]{1,0:T(8,128)(2,1)S(1)} %collective-permute-done.35.refs_2_, ...), custom_call_target="tpu_custom_call" | custom-call | flops 4026531840 | bytes 13303808 | tf_op jit(solution)/shard_map/back/pallas_call | solution.py:41
  109.8 4.9 %collective-permute-done.43.refs_0_ = bf16[96,2048]{1,0:T(8,128)(2,1)S(1)} collective-permute-done((bf16[96,2048]{1,0:T(8,128)(2,1)S(1)}, bf16[96,2048]{1,0:T(8,128)(2,1)S(1)}, u32[]{:S(2)}, u32[]{:S(2)}) %collective-permute-start.43) | collective-permute-done | bytes 393248 | tf_op jit(solution)/shard_map/ppermute | solution.py:31
  114.8 1.7 %collective-permute-start.47 = (bf16[96,1024]{1,0:T(8,128)(2,1)S(1)}, bf16[96,1024]{1,0:T(8,128)(2,1)S(1)}, u32[]{:S(2)}, u32[]{:S(2)}) collective-permute-start(bf16[96,1024]{1,0:T(8,128)(2,1)S(1)} %slice.95), channel_id=1, source_target_pairs={{0,4},{1,5},{4,8},{5,9},{8,12},{9,13},{12,14},{13,15},{14,10},{15,... | collective-permute-start | bytes 589832 | tf_op jit(solution)/shard_map/ppermute | solution.py:31
  116.5 0.7 collective-permute-start.48
  117.7 3.4 %collective-permute-done.47 = bf16[96,1024]{1,0:T(8,128)(2,1)S(1)} collective-permute-done((bf16[96,1024]{1,0:T(8,128)(2,1)S(1)}, bf16[96,1024]{1,0:T(8,128)(2,1)S(1)}, u32[]{:S(2)}, u32[]{:S(2)}) %collective-permute-start.47) | collective-permute-done | bytes 196640 | tf_op jit(solution)/shard_map/ppermute | solution.py:31
  121.1 1.6 %collective-permute-done.48 = bf16[96,1024]{1,0:T(8,128)(2,1)S(1)} collective-permute-done((bf16[96,1024]{1,0:T(8,128)(2,1)S(1)}, bf16[96,1024]{1,0:T(8,128)(2,1)S(1)}, u32[]{:S(2)}, u32[]{:S(2)}) %collective-permute-start.48) | collective-permute-done | bytes 196640 | tf_op jit(solution)/shard_map/ppermute | solution.py:31
  122.9 1.4 %back_own.1.refs_3_ = f32[288,1024]{1,0:T(8,128)S(1)} custom-call(s32[1]{0:T(128)} %bitcast.core_ref, bf16[96,2048]{1,0:T(8,128)(2,1)S(1)} %collective-permute-done.43.refs_0_, bf16[96,2048]{1,0:T(8,128)(2,1)S(1)} %collective-permute-done.44.refs_1_, bf16[96,2048]{1,0:T(8,128)(2,1)S(1)} %constant_dynamic-update-slice_fusion.2.refs_2_, ...), custom_call_target="tpu_custom_call" | custom-call | flops 1207959552 | bytes 9568256 | tf_op jit(solution)/shard_map/back_own/pallas_call | solution.py:41
  124.6 1.4 %back.3.refs_17_ = bf16[144,1024]{1,0:T(8,128)(2,1)S(1)} custom-call(s32[1]{0:T(128)} %bitcast.core_ref, bf16[96,2048]{1,0:T(8,128)(2,1)S(1)} %collective-permute-done.45.refs_0_, bf16[96,2048]{1,0:T(8,128)(2,1)S(1)} %collective-permute-done.46.refs_1_, bf16[96,2048]{1,0:T(8,128)(2,1)S(1)} %collective-permute-done.49.refs_2_, ...), custom_call_target="tpu_custom_call" | custom-call | flops 1207959552 | bytes 10747904 | tf_op jit(solution)/shard_map/back/pallas_call | solution.py:41
  126.0 5.6 %outer.1 = bf16[4096,1024]{1,0:T(8,128)(2,1)} custom-call(s32[1]{0:T(128)} %bitcast.core_ref, bf16[48,2048]{1,0:T(8,128)(2,1)S(1)} %maximum_select_fusion.after_ref.refs_0_, bf16[48,2048]{1,0:T(8,128)(2,1)S(1)} %collective-permute-done.1.refs_1_, bf16[48,2048]{1,0:T(8,128)(2,1)S(1)} %collective-permute-done.2.refs_2_, ...), custom_call_target="tpu_custom_call" | custom-call | flops 3221225472 | bytes 8388608 | tf_op jit(solution)/shard_map/outer/pallas_call | solution.py:326
  (88 shorter events, 10.6 us)
Async XLA Ops:
  2.5 8.8 %collective-permute-start.1 = (bf16[48,2048]{1,0:T(8,128)(2,1)S(1)}, bf16[48,2048]{1,0:T(8,128)(2,1)S(1)}, u32[]{:S(2)}, u32[]{:S(2)}) collective-permute-start(bf16[48,2048]{1,0:T(8,128)(2,1)S(1)} %maximum_select_fusion.after_ref.refs_0_), channel_id=1, source_target_pairs={{0,4},{1,5},{4,8},{5,9},{8,12},{9,13},{12,14},{13,15},{14,10},{15,... | collective-permute-start | bytes 589832 | tf_op jit(solution)/shard_map/ppermute | solution.py:31
  5.4 6.7 %collective-permute-start.2 = (bf16[48,2048]{1,0:T(8,128)(2,1)S(1)}, bf16[48,2048]{1,0:T(8,128)(2,1)S(1)}, u32[]{:S(2)}, u32[]{:S(2)}) collective-permute-start(bf16[48,2048]{1,0:T(8,128)(2,1)S(1)} %maximum_select_fusion.after_ref.refs_0_), channel_id=1, source_target_pairs={{4,0},{5,1},{8,4},{9,5},{12,8},{13,9},{14,12},{15,13},{10,14},{11,... | collective-permute-start | bytes 589832 | tf_op jit(solution)/shard_map/ppermute | solution.py:31
  12.1 5.9 %collective-permute-start.3 = (bf16[48,2048]{1,0:T(8,128)(2,1)S(1)}, bf16[48,2048]{1,0:T(8,128)(2,1)S(1)}, u32[]{:S(2)}, u32[]{:S(2)}) collective-permute-start(bf16[48,2048]{1,0:T(8,128)(2,1)S(1)} %collective-permute-done.1.refs_1_), channel_id=1, source_target_pairs={{0,4},{1,5},{4,8},{5,9},{8,12},{9,13},{12,14},{13,15},{14,10},{15,... | collective-permute-start | bytes 589832 | tf_op jit(solution)/shard_map/ppermute | solution.py:31
  13.7 5.8 %collective-permute-start.4 = (bf16[48,2048]{1,0:T(8,128)(2,1)S(1)}, bf16[48,2048]{1,0:T(8,128)(2,1)S(1)}, u32[]{:S(2)}, u32[]{:S(2)}) collective-permute-start(bf16[48,2048]{1,0:T(8,128)(2,1)S(1)} %collective-permute-done.2.refs_2_), channel_id=1, source_target_pairs={{4,0},{5,1},{8,4},{9,5},{12,8},{13,9},{14,12},{15,13},{10,14},{11,... | collective-permute-start | bytes 589832 | tf_op jit(solution)/shard_map/ppermute | solution.py:31
  14.1 6.9 %collective-permute-start.7 = (bf16[48,2048]{1,0:T(8,128)(2,1)S(1)}, bf16[48,2048]{1,0:T(8,128)(2,1)S(1)}, u32[]{:S(2)}, u32[]{:S(2)}) collective-permute-start(bf16[48,2048]{1,0:T(8,128)(2,1)S(1)} %maximum_select_fusion.after_ref.refs_0_), channel_id=1, source_target_pairs={{0,1},{1,0},{2,3},{3,2},{4,5},{5,4},{6,7},{7,6},{8,9},{9,8},{10,11... | collective-permute-start | bytes 589832 | tf_op jit(solution)/shard_map/ppermute | solution.py:31
  14.1 7.1 %collective-permute-start.8 = (bf16[48,2048]{1,0:T(8,128)(2,1)S(1)}, bf16[48,2048]{1,0:T(8,128)(2,1)S(1)}, u32[]{:S(2)}, u32[]{:S(2)}) collective-permute-start(bf16[48,2048]{1,0:T(8,128)(2,1)S(1)} %collective-permute-done.1.refs_1_), channel_id=1, source_target_pairs={{0,1},{1,0},{2,3},{3,2},{4,5},{5,4},{6,7},{7,6},{8,9},{9,8},{10,11... | collective-permute-start | bytes 589832 | tf_op jit(solution)/shard_map/ppermute | solution.py:31
  14.7 7.1 %collective-permute-start.9 = (bf16[48,2048]{1,0:T(8,128)(2,1)S(1)}, bf16[48,2048]{1,0:T(8,128)(2,1)S(1)}, u32[]{:S(2)}, u32[]{:S(2)}) collective-permute-start(bf16[48,2048]{1,0:T(8,128)(2,1)S(1)} %collective-permute-done.2.refs_2_), channel_id=1, source_target_pairs={{0,1},{1,0},{2,3},{3,2},{4,5},{5,4},{6,7},{7,6},{8,9},{9,8},{10,11... | collective-permute-start | bytes 589832 | tf_op jit(solution)/shard_map/ppermute | solution.py:31
  19.5 11.1 %collective-permute-start.12 = (bf16[48,2048]{1,0:T(8,128)(2,1)S(1)}, bf16[48,2048]{1,0:T(8,128)(2,1)S(1)}, u32[]{:S(2)}, u32[]{:S(2)}) collective-permute-start(bf16[48,2048]{1,0:T(8,128)(2,1)S(1)} %collective-permute-done.3.refs_0_.refs_3_), channel_id=1, source_target_pairs={{0,1},{1,0},{2,3},{3,2},{4,5},{5,4},{6,7},{7,6},{8,9},{9,8},{10,11... | collective-permute-start | bytes 589832 | tf_op jit(solution)/shard_map/ppermute | solution.py:31
  19.5 7.3 %collective-permute-start.5 = (bf16[48,2048]{1,0:T(8,128)(2,1)S(1)}, bf16[48,2048]{1,0:T(8,128)(2,1)S(1)}, u32[]{:S(2)}, u32[]{:S(2)}) collective-permute-start(bf16[48,2048]{1,0:T(8,128)(2,1)S(1)} %collective-permute-done.3.refs_0_.refs_3_), channel_id=1, source_target_pairs={{0,4},{1,5},{4,8},{5,9},{8,12},{9,13},{12,14},{13,15},{14,10},{15,... | collective-permute-start | bytes 589832 | tf_op jit(solution)/shard_map/ppermute | solution.py:31
  21.0 10.0 %collective-permute-start.13 = (bf16[48,2048]{1,0:T(8,128)(2,1)S(1)}, bf16[48,2048]{1,0:T(8,128)(2,1)S(1)}, u32[]{:S(2)}, u32[]{:S(2)}) collective-permute-start(bf16[48,2048]{1,0:T(8,128)(2,1)S(1)} %collective-permute-done.4.refs_1_.refs_4_), channel_id=1, source_target_pairs={{0,1},{1,0},{2,3},{3,2},{4,5},{5,4},{6,7},{7,6},{8,9},{9,8},{10,11... | collective-permute-start | bytes 589832 | tf_op jit(solution)/shard_map/ppermute | solution.py:31
  21.3 7.1 %collective-permute-start.6 = (bf16[48,2048]{1,0:T(8,128)(2,1)S(1)}, bf16[48,2048]{1,0:T(8,128)(2,1)S(1)}, u32[]{:S(2)}, u32[]{:S(2)}) collective-permute-start(bf16[48,2048]{1,0:T(8,128)(2,1)S(1)} %collective-permute-done.4.refs_1_.refs_4_), channel_id=1, source_target_pairs={{4,0},{5,1},{8,4},{9,5},{12,8},{13,9},{14,12},{15,13},{10,14},{11,... | collective-permute-start | bytes 589832 | tf_op jit(solution)/shard_map/ppermute | solution.py:31
  28.4 9.4 %collective-permute-start.14 = (bf16[48,2048]{1,0:T(8,128)(2,1)S(1)}, bf16[48,2048]{1,0:T(8,128)(2,1)S(1)}, u32[]{:S(2)}, u32[]{:S(2)}) collective-permute-start(bf16[48,2048]{1,0:T(8,128)(2,1)S(1)} %collective-permute-done.5.refs_0_.refs_5_), channel_id=1, source_target_pairs={{0,1},{1,0},{2,3},{3,2},{4,5},{5,4},{6,7},{7,6},{8,9},{9,8},{10,11... | collective-permute-start | bytes 589832 | tf_op jit(solution)/shard_map/ppermute | solution.py:31
  28.5 9.3 %collective-permute-start.15 = (bf16[48,2048]{1,0:T(8,128)(2,1)S(1)}, bf16[48,2048]{1,0:T(8,128)(2,1)S(1)}, u32[]{:S(2)}, u32[]{:S(2)}) collective-permute-start(bf16[48,2048]{1,0:T(8,128)(2,1)S(1)} %collective-permute-done.6.refs_1_.refs_6_), channel_id=1, source_target_pairs={{0,1},{1,0},{2,3},{3,2},{4,5},{5,4},{6,7},{7,6},{8,9},{9,8},{10,11... | collective-permute-start | bytes 589832 | tf_op jit(solution)/shard_map/ppermute | solution.py:31
  29.0 6.5 %collective-permute-start.10 = (bf16[48,1024]{1,0:T(8,128)(2,1)S(1)}, bf16[48,1024]{1,0:T(8,128)(2,1)S(1)}, u32[]{:S(2)}, u32[]{:S(2)}) collective-permute-start(bf16[48,1024]{1,0:T(8,128)(2,1)S(1)} %slice.73), channel_id=1, source_target_pairs={{0,4},{1,5},{4,8},{5,9},{8,12},{9,13},{12,14},{13,15},{14,10},{15,... | collective-permute-start | bytes 294920 | tf_op jit(solution)/shard_map/ppermute | solution.py:31
  30.6 5.0 %collective-permute-start.11 = (bf16[48,1024]{1,0:T(8,128)(2,1)S(1)}, bf16[48,1024]{1,0:T(8,128)(2,1)S(1)}, u32[]{:S(2)}, u32[]{:S(2)}) collective-permute-start(bf16[48,1024]{1,0:T(8,128)(2,1)S(1)} %slice.74), channel_id=1, source_target_pairs={{4,0},{5,1},{8,4},{9,5},{12,8},{13,9},{14,12},{15,13},{10,14},{11,... | collective-permute-start | bytes 294920 | tf_op jit(solution)/shard_map/ppermute | solution.py:31
  35.6 2.1 %collective-permute-start.16 = (bf16[48,2048]{1,0:T(8,128)(2,1)S(1)}, bf16[48,2048]{1,0:T(8,128)(2,1)S(1)}, u32[]{:S(2)}, u32[]{:S(2)}) collective-permute-start(bf16[48,2048]{1,0:T(8,128)(2,1)S(1)} %constant_dynamic-update-slice_fusion.refs_2_.refs_7_), channel_id=1, source_target_pairs={{0,1},{1,0},{2,3},{3,2},{4,5},{5,4},{6,7},{7,6},{8,9},{9,8},{10,11... | collective-permute-start | bytes 589832 | tf_op jit(solution)/shard_map/ppermute | solution.py:31
  41.7 2.5 %collective-permute-start.17 = (bf16[96,2048]{1,0:T(8,128)(2,1)S(1)}, bf16[96,2048]{1,0:T(8,128)(2,1)S(1)}, u32[]{:S(2)}, u32[]{:S(2)}) collective-permute-start(bf16[96,2048]{1,0:T(8,128)(2,1)S(1)} %get-tuple-element.118), channel_id=1, source_target_pairs={{0,1},{1,0},{2,3},{3,2},{4,5},{5,4},{6,7},{7,6},{8,9},{9,8},{10,11... | collective-permute-start | bytes 1179656 | tf_op jit(solution)/shard_map/ppermute | solution.py:31
  42.3 10.3 %collective-permute-start.21 = (bf16[96,2048]{1,0:T(8,128)(2,1)S(1)}, bf16[96,2048]{1,0:T(8,128)(2,1)S(1)}, u32[]{:S(2)}, u32[]{:S(2)}) collective-permute-start(bf16[96,2048]{1,0:T(8,128)(2,1)S(1)} %get-tuple-element.117), channel_id=1, source_target_pairs={{0,1},{1,0},{2,3},{3,2},{4,5},{5,4},{6,7},{7,6},{8,9},{9,8},{10,11... | collective-permute-start | bytes 1179656 | tf_op jit(solution)/shard_map/ppermute | solution.py:31
  42.3 10.2 %collective-permute-start.24 = (bf16[96,2048]{1,0:T(8,128)(2,1)S(1)}, bf16[96,2048]{1,0:T(8,128)(2,1)S(1)}, u32[]{:S(2)}, u32[]{:S(2)}) collective-permute-start(bf16[96,2048]{1,0:T(8,128)(2,1)S(1)} %get-tuple-element.116), channel_id=1, source_target_pairs={{0,1},{1,0},{2,3},{3,2},{4,5},{5,4},{6,7},{7,6},{8,9},{9,8},{10,11... | collective-permute-start | bytes 1179656 | tf_op jit(solution)/shard_map/ppermute | solution.py:31
  44.3 6.9 %collective-permute-start.22 = (bf16[96,1024]{1,0:T(8,128)(2,1)S(1)}, bf16[96,1024]{1,0:T(8,128)(2,1)S(1)}, u32[]{:S(2)}, u32[]{:S(2)}) collective-permute-start(bf16[96,1024]{1,0:T(8,128)(2,1)S(1)} %get-tuple-element.120), channel_id=1, source_target_pairs={{0,4},{1,5},{4,8},{5,9},{8,12},{9,13},{12,14},{13,15},{14,10},{15,... | collective-permute-start | bytes 589832 | tf_op jit(solution)/shard_map/ppermute | solution.py:31
  46.0 6.6 %collective-permute-start.23 = (bf16[96,1024]{1,0:T(8,128)(2,1)S(1)}, bf16[96,1024]{1,0:T(8,128)(2,1)S(1)}, u32[]{:S(2)}, u32[]{:S(2)}) collective-permute-start(bf16[96,1024]{1,0:T(8,128)(2,1)S(1)} %get-tuple-element.119), channel_id=1, source_target_pairs={{4,0},{5,1},{8,4},{9,5},{12,8},{13,9},{14,12},{15,13},{10,14},{11,... | collective-permute-start | bytes 589832 | tf_op jit(solution)/shard_map/ppermute | solution.py:31
  52.9 10.0 %collective-permute-start.25 = (bf16[96,2048]{1,0:T(8,128)(2,1)S(1)}, bf16[96,2048]{1,0:T(8,128)(2,1)S(1)}, u32[]{:S(2)}, u32[]{:S(2)}) collective-permute-start(bf16[96,2048]{1,0:T(8,128)(2,1)S(1)} %get-tuple-element.79), channel_id=1, source_target_pairs={{0,4},{1,5},{4,8},{5,9},{8,12},{9,13},{12,14},{13,15},{14,10},{15,... | collective-permute-start | bytes 1179656 | tf_op jit(solution)/shard_map/ppermute | solution.py:31
  54.5 9.7 %collective-permute-start.26 = (bf16[96,2048]{1,0:T(8,128)(2,1)S(1)}, bf16[96,2048]{1,0:T(8,128)(2,1)S(1)}, u32[]{:S(2)}, u32[]{:S(2)}) collective-permute-start(bf16[96,2048]{1,0:T(8,128)(2,1)S(1)} %get-tuple-element.80), channel_id=1, source_target_pairs={{4,0},{5,1},{8,4},{9,5},{12,8},{13,9},{14,12},{15,13},{10,14},{11,... | collective-permute-start | bytes 1179656 | tf_op jit(solution)/shard_map/ppermute | solution.py:31
  55.0 9.2 %collective-permute-start.20 = (bf16[96,2048]{1,0:T(8,128)(2,1)S(1)}, bf16[96,2048]{1,0:T(8,128)(2,1)S(1)}, u32[]{:S(2)}, u32[]{:S(2)}) collective-permute-start(bf16[96,2048]{1,0:T(8,128)(2,1)S(1)} %get-tuple-element.108), channel_id=1, source_target_pairs={{0,1},{1,0},{2,3},{3,2},{4,5},{5,4},{6,7},{7,6},{8,9},{9,8},{10,11... | collective-permute-start | bytes 1179656 | tf_op jit(solution)/shard_map/ppermute | solution.py:31
  55.0 9.2 %collective-permute-start.27 = (bf16[96,2048]{1,0:T(8,128)(2,1)S(1)}, bf16[96,2048]{1,0:T(8,128)(2,1)S(1)}, u32[]{:S(2)}, u32[]{:S(2)}) collective-permute-start(bf16[96,2048]{1,0:T(8,128)(2,1)S(1)} %get-tuple-element.107), channel_id=1, source_target_pairs={{0,1},{1,0},{2,3},{3,2},{4,5},{5,4},{6,7},{7,6},{8,9},{9,8},{10,11... | collective-permute-start | bytes 1179656 | tf_op jit(solution)/shard_map/ppermute | solution.py:31
  64.6 8.8 %collective-permute-start.28 = (bf16[96,2048]{1,0:T(8,128)(2,1)S(1)}, bf16[96,2048]{1,0:T(8,128)(2,1)S(1)}, u32[]{:S(2)}, u32[]{:S(2)}) collective-permute-start(bf16[96,2048]{1,0:T(8,128)(2,1)S(1)} %get-tuple-element.83), channel_id=1, source_target_pairs={{0,4},{1,5},{4,8},{5,9},{8,12},{9,13},{12,14},{13,15},{14,10},{15,... | collective-permute-start | bytes 1179656 | tf_op jit(solution)/shard_map/ppermute | solution.py:31
  65.3 8.6 %collective-permute-start.29 = (bf16[96,2048]{1,0:T(8,128)(2,1)S(1)}, bf16[96,2048]{1,0:T(8,128)(2,1)S(1)}, u32[]{:S(2)}, u32[]{:S(2)}) collective-permute-start(bf16[96,2048]{1,0:T(8,128)(2,1)S(1)} %get-tuple-element.84), channel_id=1, source_target_pairs={{4,0},{5,1},{8,4},{9,5},{12,8},{13,9},{14,12},{15,13},{10,14},{11,... | collective-permute-start | bytes 1179656 | tf_op jit(solution)/shard_map/ppermute | solution.py:31
  66.6 7.3 %collective-permute-start.19 = (bf16[96,2048]{1,0:T(8,128)(2,1)S(1)}, bf16[96,2048]{1,0:T(8,128)(2,1)S(1)}, u32[]{:S(2)}, u32[]{:S(2)}) collective-permute-start(bf16[96,2048]{1,0:T(8,128)(2,1)S(1)} %get-tuple-element.109), channel_id=1, source_target_pairs={{0,1},{1,0},{2,3},{3,2},{4,5},{5,4},{6,7},{7,6},{8,9},{9,8},{10,11... | collective-permute-start | bytes 1179656 | tf_op jit(solution)/shard_map/ppermute | solution.py:31
  66.6 7.3 %collective-permute-start.30 = (bf16[96,2048]{1,0:T(8,128)(2,1)S(1)}, bf16[96,2048]{1,0:T(8,128)(2,1)S(1)}, u32[]{:S(2)}, u32[]{:S(2)}) collective-permute-start(bf16[96,2048]{1,0:T(8,128)(2,1)S(1)} %get-tuple-element.106), channel_id=1, source_target_pairs={{0,1},{1,0},{2,3},{3,2},{4,5},{5,4},{6,7},{7,6},{8,9},{9,8},{10,11... | collective-permute-start | bytes 1179656 | tf_op jit(solution)/shard_map/ppermute | solution.py:31
  74.3 8.6 %collective-permute-start.31 = (bf16[96,2048]{1,0:T(8,128)(2,1)S(1)}, bf16[96,2048]{1,0:T(8,128)(2,1)S(1)}, u32[]{:S(2)}, u32[]{:S(2)}) collective-permute-start(bf16[96,2048]{1,0:T(8,128)(2,1)S(1)} %get-tuple-element.87), channel_id=1, source_target_pairs={{0,4},{1,5},{4,8},{5,9},{8,12},{9,13},{12,14},{13,15},{14,10},{15,... | collective-permute-start | bytes 1179656 | tf_op jit(solution)/shard_map/ppermute | solution.py:31
  74.9 8.8 %collective-permute-start.32 = (bf16[96,2048]{1,0:T(8,128)(2,1)S(1)}, bf16[96,2048]{1,0:T(8,128)(2,1)S(1)}, u32[]{:S(2)}, u32[]{:S(2)}) collective-permute-start(bf16[96,2048]{1,0:T(8,128)(2,1)S(1)} %get-tuple-element.88), channel_id=1, source_target_pairs={{4,0},{5,1},{8,4},{9,5},{12,8},{13,9},{14,12},{15,13},{10,14},{11,... | collective-permute-start | bytes 1179656 | tf_op jit(solution)/shard_map/ppermute | solution.py:31
  76.4 7.3 %collective-permute-start.18 = (bf16[96,2048]{1,0:T(8,128)(2,1)S(1)}, bf16[96,2048]{1,0:T(8,128)(2,1)S(1)}, u32[]{:S(2)}, u32[]{:S(2)}) collective-permute-start(bf16[96,2048]{1,0:T(8,128)(2,1)S(1)} %get-tuple-element.105), channel_id=1, source_target_pairs={{0,1},{1,0},{2,3},{3,2},{4,5},{5,4},{6,7},{7,6},{8,9},{9,8},{10,11... | collective-permute-start | bytes 1179656 | tf_op jit(solution)/shard_map/ppermute | solution.py:31
  76.4 7.6 %collective-permute-start.33 = (bf16[24,2048]{1,0:T(8,128)(2,1)S(1)}, bf16[24,2048]{1,0:T(8,128)(2,1)S(1)}, u32[]{:S(2)}, u32[]{:S(2)}) collective-permute-start(bf16[24,2048]{1,0:T(8,128)(2,1)S(1)} %get-tuple-element.122), channel_id=1, source_target_pairs={{0,1},{1,0},{2,3},{3,2},{4,5},{5,4},{6,7},{7,6},{8,9},{9,8},{10,11... | collective-permute-start | bytes 294920 | tf_op jit(solution)/shard_map/ppermute | solution.py:31
  84.1 10.3 %collective-permute-start.34 = (bf16[96,2048]{1,0:T(8,128)(2,1)S(1)}, bf16[96,2048]{1,0:T(8,128)(2,1)S(1)}, u32[]{:S(2)}, u32[]{:S(2)}) collective-permute-start(bf16[96,2048]{1,0:T(8,128)(2,1)S(1)} %pad_maximum_fusion.refs_0_), channel_id=1, source_target_pairs={{0,4},{1,5},{4,8},{5,9},{8,12},{9,13},{12,14},{13,15},{14,10},{15,... | collective-permute-start | bytes 1179656 | tf_op jit(solution)/shard_map/ppermute | solution.py:31
  84.6 10.6 %collective-permute-start.35 = (bf16[96,2048]{1,0:T(8,128)(2,1)S(1)}, bf16[96,2048]{1,0:T(8,128)(2,1)S(1)}, u32[]{:S(2)}, u32[]{:S(2)}) collective-permute-start(bf16[96,2048]{1,0:T(8,128)(2,1)S(1)} %pad_maximum_fusion.refs_0_), channel_id=1, source_target_pairs={{4,0},{5,1},{8,4},{9,5},{12,8},{13,9},{14,12},{15,13},{10,14},{11,... | collective-permute-start | bytes 1179656 | tf_op jit(solution)/shard_map/ppermute | solution.py:31
  95.2 7.8 %collective-permute-start.36 = (bf16[96,2048]{1,0:T(8,128)(2,1)S(1)}, bf16[96,2048]{1,0:T(8,128)(2,1)S(1)}, u32[]{:S(2)}, u32[]{:S(2)}) collective-permute-start(bf16[96,2048]{1,0:T(8,128)(2,1)S(1)} %collective-permute-done.34.refs_1_), channel_id=1, source_target_pairs={{0,4},{1,5},{4,8},{5,9},{8,12},{9,13},{12,14},{13,15},{14,10},{15,... | collective-permute-start | bytes 1179656 | tf_op jit(solution)/shard_map/ppermute | solution.py:31
  95.2 7.8 %collective-permute-start.37 = (bf16[96,2048]{1,0:T(8,128)(2,1)S(1)}, bf16[96,2048]{1,0:T(8,128)(2,1)S(1)}, u32[]{:S(2)}, u32[]{:S(2)}) collective-permute-start(bf16[96,2048]{1,0:T(8,128)(2,1)S(1)} %collective-permute-done.35.refs_2_), channel_id=1, source_target_pairs={{4,0},{5,1},{8,4},{9,5},{12,8},{13,9},{14,12},{15,13},{10,14},{11,... | collective-permute-start | bytes 1179656 | tf_op jit(solution)/shard_map/ppermute | solution.py:31
  97.2 6.3 %collective-permute-start.38 = (bf16[96,2048]{1,0:T(8,128)(2,1)S(1)}, bf16[96,2048]{1,0:T(8,128)(2,1)S(1)}, u32[]{:S(2)}, u32[]{:S(2)}) collective-permute-start(bf16[96,2048]{1,0:T(8,128)(2,1)S(1)} %pad_maximum_fusion.refs_0_), channel_id=1, source_target_pairs={{0,1},{1,0},{2,3},{3,2},{4,5},{5,4},{6,7},{7,6},{8,9},{9,8},{10,11... | collective-permute-start | bytes 1179656 | tf_op jit(solution)/shard_map/ppermute | solution.py:31
  97.2 6.3 %collective-permute-start.39 = (bf16[96,2048]{1,0:T(8,128)(2,1)S(1)}, bf16[96,2048]{1,0:T(8,128)(2,1)S(1)}, u32[]{:S(2)}, u32[]{:S(2)}) collective-permute-start(bf16[96,2048]{1,0:T(8,128)(2,1)S(1)} %collective-permute-done.34.refs_1_), channel_id=1, source_target_pairs={{0,1},{1,0},{2,3},{3,2},{4,5},{5,4},{6,7},{7,6},{8,9},{9,8},{10,11... | collective-permute-start | bytes 1179656 | tf_op jit(solution)/shard_map/ppermute | solution.py:31
  97.7 7.8 %collective-permute-start.40 = (bf16[96,2048]{1,0:T(8,128)(2,1)S(1)}, bf16[96,2048]{1,0:T(8,128)(2,1)S(1)}, u32[]{:S(2)}, u32[]{:S(2)}) collective-permute-start(bf16[96,2048]{1,0:T(8,128)(2,1)S(1)} %collective-permute-done.35.refs_2_), channel_id=1, source_target_pairs={{0,1},{1,0},{2,3},{3,2},{4,5},{5,4},{6,7},{7,6},{8,9},{9,8},{10,11... | collective-permute-start | bytes 1179656 | tf_op jit(solution)/shard_map/ppermute | solution.py:31
  102.9 2.6 %collective-permute-start.41 = (bf16[96,2048]{1,0:T(8,128)(2,1)S(1)}, bf16[96,2048]{1,0:T(8,128)(2,1)S(1)}, u32[]{:S(2)}, u32[]{:S(2)}) collective-permute-start(bf16[96,2048]{1,0:T(8,128)(2,1)S(1)} %collective-permute-done.36.refs_3_), channel_id=1, source_target_pairs={{0,1},{1,0},{2,3},{3,2},{4,5},{5,4},{6,7},{7,6},{8,9},{9,8},{10,11... | collective-permute-start | bytes 1179656 | tf_op jit(solution)/shard_map/ppermute | solution.py:31
  102.9 2.6 %collective-permute-start.42 = (bf16[96,2048]{1,0:T(8,128)(2,1)S(1)}, bf16[96,2048]{1,0:T(8,128)(2,1)S(1)}, u32[]{:S(2)}, u32[]{:S(2)}) collective-permute-start(bf16[96,2048]{1,0:T(8,128)(2,1)S(1)} %collective-permute-done.37.refs_4_), channel_id=1, source_target_pairs={{0,1},{1,0},{2,3},{3,2},{4,5},{5,4},{6,7},{7,6},{8,9},{9,8},{10,11... | collective-permute-start | bytes 1179656 | tf_op jit(solution)/shard_map/ppermute | solution.py:31
  103.5 11.3 %collective-permute-start.43 = (bf16[96,2048]{1,0:T(8,128)(2,1)S(1)}, bf16[96,2048]{1,0:T(8,128)(2,1)S(1)}, u32[]{:S(2)}, u32[]{:S(2)}) collective-permute-start(bf16[96,2048]{1,0:T(8,128)(2,1)S(1)} %collective-permute-done.36.refs_3_), channel_id=1, source_target_pairs={{0,4},{1,5},{4,8},{5,9},{8,12},{9,13},{12,14},{13,15},{14,10},{15,... | collective-permute-start | bytes 1179656 | tf_op jit(solution)/shard_map/ppermute | solution.py:31
  103.5 11.3 %collective-permute-start.44 = (bf16[96,2048]{1,0:T(8,128)(2,1)S(1)}, bf16[96,2048]{1,0:T(8,128)(2,1)S(1)}, u32[]{:S(2)}, u32[]{:S(2)}) collective-permute-start(bf16[96,2048]{1,0:T(8,128)(2,1)S(1)} %collective-permute-done.37.refs_4_), channel_id=1, source_target_pairs={{4,0},{5,1},{8,4},{9,5},{12,8},{13,9},{14,12},{15,13},{10,14},{11,... | collective-permute-start | bytes 1179656 | tf_op jit(solution)/shard_map/ppermute | solution.py:31
  114.8 6.3 %collective-permute-start.47 = (bf16[96,1024]{1,0:T(8,128)(2,1)S(1)}, bf16[96,1024]{1,0:T(8,128)(2,1)S(1)}, u32[]{:S(2)}, u32[]{:S(2)}) collective-permute-start(bf16[96,1024]{1,0:T(8,128)(2,1)S(1)} %slice.95), channel_id=1, source_target_pairs={{0,4},{1,5},{4,8},{5,9},{8,12},{9,13},{12,14},{13,15},{14,10},{15,... | collective-permute-start | bytes 589832 | tf_op jit(solution)/shard_map/ppermute | solution.py:31
  116.5 6.3 %collective-permute-start.48 = (bf16[96,1024]{1,0:T(8,128)(2,1)S(1)}, bf16[96,1024]{1,0:T(8,128)(2,1)S(1)}, u32[]{:S(2)}, u32[]{:S(2)}) collective-permute-start(bf16[96,1024]{1,0:T(8,128)(2,1)S(1)} %slice.96), channel_id=1, source_target_pairs={{4,0},{5,1},{8,4},{9,5},{12,8},{13,9},{14,12},{15,13},{10,14},{11,... | collective-permute-start | bytes 589832 | tf_op jit(solution)/shard_map/ppermute | solution.py:31
  117.2 7.1 %collective-permute-start.45 = (bf16[96,2048]{1,0:T(8,128)(2,1)S(1)}, bf16[96,2048]{1,0:T(8,128)(2,1)S(1)}, u32[]{:S(2)}, u32[]{:S(2)}) collective-permute-start(bf16[96,2048]{1,0:T(8,128)(2,1)S(1)} %collective-permute-done.43.refs_0_), channel_id=1, source_target_pairs={{0,1},{1,0},{2,3},{3,2},{4,5},{5,4},{6,7},{7,6},{8,9},{9,8},{10,11... | collective-permute-start | bytes 1179656 | tf_op jit(solution)/shard_map/ppermute | solution.py:31
  117.2 7.1 %collective-permute-start.46 = (bf16[96,2048]{1,0:T(8,128)(2,1)S(1)}, bf16[96,2048]{1,0:T(8,128)(2,1)S(1)}, u32[]{:S(2)}, u32[]{:S(2)}) collective-permute-start(bf16[96,2048]{1,0:T(8,128)(2,1)S(1)} %collective-permute-done.44.refs_1_), channel_id=1, source_target_pairs={{0,1},{1,0},{2,3},{3,2},{4,5},{5,4},{6,7},{7,6},{8,9},{9,8},{10,11... | collective-permute-start | bytes 1179656 | tf_op jit(solution)/shard_map/ppermute | solution.py:31
  (3 other events, 15.1 us)

commit v4 on v3

--- a/solution.py
+++ b/solution.py
@@ -217,6 +217,48 @@
         places * total * depth * columns,
         [*hidden, down_weight],
     )
+
+
+def merge(core, sums, shape, splits=1, under=False):
+    rows, columns = shape
+    arrays = []
+    plan = []
+    for terms in sums:
+        places = []
+        for array, *rest in terms:
+            known = [n for n, x in enumerate(arrays) if x is array]
+            if not known:
+                arrays.append(array)
+            places.append((known[0] if known else len(arrays) - 1, *rest))
+        plan.append(places)
+    piece = columns // splits
+
+    def kernel(core_ref, *refs):
+        out_refs = refs[len(arrays) :]
+        for n, places in enumerate(plan):
+            for start in range(0, columns, columns // 4):
+                width = columns // 4
+                value = None
+                for at, row, column, *sign in places:
+                    if start < column or start >= column + arrays[at].shape[1]:
+                        continue
+                    term = refs[at][row : row + rows, start - column : start - column + width].astype(F32)
+                    if value is None:
+                        value = term
+                    else:
+                        value = value - term if sign else value + term
+                out = out_refs[0 if under else n * splits + start // piece]
+                at = n * rows if under else 0
+                out[at : at + rows, start % piece : start % piece + width] = value.astype(BF16)
+
+    outs = [((len(sums) * rows, columns), BF16)]
+    if not under:
+        outs = [((rows, piece), BF16)] * (len(sums) * splits)
+    return call(kernel, "merge", core, outs, [], 0, arrays)
+
+
+def stack(core, sums, shape):
+    return merge(core, sums, (shape[0] // len(sums), shape[1]), under=True)[0]
 
 
 def back_own(core, same, down_weight):
@@ -372,7 +414,9 @@
             swap()
             done = work(step, same, other)
             for c in chains:
-                before, after, *_ = tie(*moved[c], *(done if c == 0 else ()))
+                before, after = moved[c]
+                if done:
+                    before, after = tie(before, *done)[0], tie(after, *done)[0]
                 ends[c] = before, after
                 same[c] += [before, after]
         if even:
@@ -383,7 +427,9 @@
             swap()
             done = work(steps + 1, same, other)
             for c in chains:
-                near, far, *_ = tie(*moved[c], *(done if c == 0 else ()))
+                near, far = moved[c]
+                if done:
+                    near, far = tie(near, *done)[0], tie(far, *done)[0]
                 same[c].append(jnp.concatenate([near, far], axis=1))
         swap()
         work(steps + 2, same, other)
@@ -420,7 +466,7 @@
     (same,), (other,) = gather([chip_rows(tokens)], run_forward)
     if "down" not in weights:
         (weights["down"],) = fetch([down_weight], hidden[-1])
-    goals = chip_rows(targets).astype(F32)
+    goals = chip_rows(targets)
 
     split = max(len(groups) - 1, 1)
     near_blocks = [b for g in groups[:split] for b in g]
@@ -430,11 +476,12 @@
     def keep(blocks, own, others):
         for at, b in enumerate(blocks):
             at = slice(2 * rows * at, 2 * rows * (at + 1))
-            partial[b] = own[at]
+            partial[b] = (own, at.start)
             swapped[b] = send(others[at], partner)
 
-    def block_of(b):
-        return partial[b].astype(F32) + swapped[b].astype(F32)
+    def terms_of(b, row=0):
+        own, start = partial[b]
+        return [(own, start + row, 0), (swapped[b], row, 0)]
 
     def near_work(after):
         hidden_near = tie(*hidden[:split], after)[:-1]
@@ -449,26 +496,32 @@
     else:
         near_work(hidden[-1])
 
+    shape = (2 * rows, half)
     from_before = from_after = None
     if even:
-        far = block_of(count - 1).astype(BF16)
-        from_before, from_after = send(far[:, :quarter], onward), send(far[:, quarter:], backward)
+        to_after, to_before = merge(core, [terms_of(count - 1)], shape, splits=2)
+        from_before, from_after = send(to_after, onward), send(to_before, backward)
         if far_blocks:
-            from_before, from_after, _ = tie(from_before, from_after, near_work(far))
-        from_before = jnp.pad(from_before.astype(F32), [(0, 0), (0, quarter)])
-        from_after = jnp.pad(from_after.astype(F32), [(0, 0), (quarter, 0)])
+            from_before, from_after, _ = tie(from_before, from_after, near_work(to_after))
     for distance in range(steps, 0, -1):
-        to_after, to_before = block_of(2 * distance), block_of(2 * distance - 1)
+        to_after, to_before = terms_of(2 * distance), terms_of(2 * distance - 1)
         if from_before is not None:
-            to_after, to_before = to_after + from_before, to_before + from_after
-        to_after, to_before = tie(to_after.astype(BF16), to_before.astype(BF16))
+            to_after.append((from_before, 0, 0))
+            to_before.append((from_after, 0, half - from_after.shape[1]))
+        if False:
+            to_after, to_before = merge(core, [to_after, to_before], shape)
+        else:
+            (to_after,), (to_before,) = merge(core, [to_after], shape), merge(core, [to_before], shape)
         from_before, from_after = send(to_after, onward), send(to_before, backward)
         if distance == steps and not even and far_blocks:
             from_before, from_after, _ = tie(from_before, from_after, near_work(to_after))
-        from_before, from_after = tie(from_before, from_after)
-        from_before, from_after = from_before.astype(F32), from_after.astype(F32)
-    total = block_of(0) + from_before + from_after
-    message = jnp.concatenate([total[:rows] - goals, total[rows:]]).astype(BF16)
+    parts = []
+    for row in (0, rows):
+        terms = terms_of(0, row) + [(from_before, row, 0), (from_after, row, 0)]
+        if row == 0:
+            terms.append((goals, 0, 0, -1))
+        parts.append(terms)
+    message = stack(core, parts, shape)
 
     weighted = []
     back_groups = [groups[:split], *[[g] for g in groups[split:]]]

time: 132 us -> 129 us (0.977)
  other arithmetic: 1.53 us -> 0.07 us
  starting transfers between devices: 32.2 us -> 30.8 us
    ppermute x50, starting transfers between devices: 32.2 us -> 30.8 us  [send(): return lax.ppermute(block, AXIS, route)]
    pallas_call x10 -> x18, Pallas kernels: 28.2 us -> 29.3 us  [call(): pl.pallas_call(kernel, in_specs=[IN_SMEM] + [IN_VMEM] * len(operands) + [...]
  transfers between devices with their start and end apart: 50 -> 50, of which waited for: 20 -> 17; matrix products, arithmetic and copies ran while one was open for 0% -> 0% of each run, Pallas kernels for 22% -> 23%
where the time goes in v4:
time: 129 us
  waiting for transfers between devices  55.7 us (43%)
  Pallas kernels  40.7 us (32%)
  starting transfers between devices  30.8 us (24%)
    ppermute x50, waiting for transfers between devices, send(): return lax.ppermute(block, AXIS, route)  55.7 us
    ppermute x50, starting transfers between devices, send(): return lax.ppermute(block, AXIS, route)  30.8 us
    pallas_call x18, Pallas kernels, call(): pl.pallas_call(kernel, in_specs=[IN_SMEM] + [IN_VMEM] * len(operands) + [...  29.3 us
    pallas_call x1, Pallas kernels, fetch(): pl.pallas_call(kernel, in_specs=[pl.BlockSpec(memory_space=pl.ANY)] + [pl...  5.78 us
    pallas_call x1, Pallas kernels, outer(): pl.pallas_call(kernel, in_specs=[IN_SMEM] + [IN_VMEM] * len(operands), ou...  5.62 us
  transfers between devices with their start and end apart: 50, of which 17 were waited for; matrix products, arithmetic and copies ran while one was open for 0% of the time, Pallas kernels for 23%

profile of v4, /device:TPU:0, one launch (start us, length us, event | category | flops | bytes accessed | tf_op | source)
XLA Modules:
  0.0 129.1 jit_solution(6328198803481139824)
XLA Ops:
  0.0 1.0 constant_dynamic-slice_fusion.3
  1.0 0.5 collective-permute-start
  1.5 0.9 collective-permute-done
  2.5 2.9 %collective-permute-start.2 = (bf16[48,2048]{1,0:T(8,128)(2,1)S(1)}, bf16[48,2048]{1,0:T(8,128)(2,1)S(1)}, u32[]{:S(2)}, u32[]{:S(2)}) collective-permute-start(bf16[48,2048]{1,0:T(8,128)(2,1)S(1)} %maximum_select_fusion.after_ref.refs_0_), channel_id=1, source_target_pairs={{4,0},{5,1},{8,4},{9,5},{12,8},{13,9},{14,12},{15,13},{10,14},{11,... | collective-permute-start | bytes 589832 | tf_op jit(solution)/shard_map/ppermute | solution.py:31
  5.5 5.8 %fetch.1 = (bf16[4096,1024]{1,0:T(8,128)(2,1)S(1)}, bf16[4096,1024]{1,0:T(8,128)(2,1)S(1)}) custom-call(bf16[48,2048]{1,0:T(8,128)(2,1)S(1)} %maximum_select_fusion.after_ref.refs_0_, bf16[4096,1024]{1,0:T(8,128)(2,1)} %refs_0_.1, bf16[4096,1024]{1,0:T(8,128)(2,1)} %refs_1_.1), custom_call_target="tpu_custom_call" | custom-call | bytes 16777216 | tf_op jit(solution)/shard_map/fetch/pallas_call | solution.py:77
  11.3 2.0 %collective-permute-start.4 = (bf16[48,2048]{1,0:T(8,128)(2,1)S(1)}, bf16[48,2048]{1,0:T(8,128)(2,1)S(1)}, u32[]{:S(2)}, u32[]{:S(2)}) collective-permute-start(bf16[48,2048]{1,0:T(8,128)(2,1)S(1)} %collective-permute-done.2.refs_2_), channel_id=1, source_target_pairs={{4,0},{5,1},{8,4},{9,5},{12,8},{13,9},{14,12},{15,13},{10,14},{11,... | collective-permute-start | bytes 589832 | tf_op jit(solution)/shard_map/ppermute | solution.py:31
  13.9 5.0 %collective-permute-done.4.refs_1_.refs_4_ = bf16[48,2048]{1,0:T(8,128)(2,1)S(1)} collective-permute-done((bf16[48,2048]{1,0:T(8,128)(2,1)S(1)}, bf16[48,2048]{1,0:T(8,128)(2,1)S(1)}, u32[]{:S(2)}, u32[]{:S(2)}) %collective-permute-start.4) | collective-permute-done | bytes 196640 | tf_op jit(solution)/shard_map/ppermute | solution.py:31
  18.9 1.7 %collective-permute-start.9 = (bf16[48,2048]{1,0:T(8,128)(2,1)S(1)}, bf16[48,2048]{1,0:T(8,128)(2,1)S(1)}, u32[]{:S(2)}, u32[]{:S(2)}) collective-permute-start(bf16[48,2048]{1,0:T(8,128)(2,1)S(1)} %collective-permute-done.4.refs_1_.refs_4_), channel_id=1, source_target_pairs={{4,0},{5,1},{8,4},{9,5},{12,8},{13,9},{14,12},{15,13},{10,14},{11,... | collective-permute-start | bytes 589832 | tf_op jit(solution)/shard_map/ppermute | solution.py:31
  21.2 5.0 %forward.3 = (bf16[288,1024]{1,0:T(8,128)(2,1)S(1)}, f32[144,1024]{1,0:T(8,128)S(1)}, f32[144,1024]{1,0:T(8,128)S(1)}, bf16[4096,1024]{1,0:T(8,128)(2,1)S(1)}) custom-call(s32[1]{0:T(128)} %bitcast.core_ref, bf16[48,2048]{1,0:T(8,128)(2,1)S(1)} %maximum_select_fusion.after_ref.refs_0_, bf16[48,2048]{1,0:T(8,128)(2,1)S(1)} %collective-permute-done.1.refs_1_, ...), custom_call_target="tpu_custom_call" | custom-call | flops 3623878656 | bytes 17956864 | tf_op jit(solution)/shard_map/forward/pallas_call | solution.py:41
  26.4 1.5 %collective-permute-done.5.refs_0_.refs_5_ = bf16[48,2048]{1,0:T(8,128)(2,1)S(1)} collective-permute-done((bf16[48,2048]{1,0:T(8,128)(2,1)S(1)}, bf16[48,2048]{1,0:T(8,128)(2,1)S(1)}, u32[]{:S(2)}, u32[]{:S(2)}) %collective-permute-start.5) | collective-permute-done | bytes 196640 | tf_op jit(solution)/shard_map/ppermute | solution.py:31
  28.0 1.6 %collective-permute-start.13 = (bf16[48,1024]{1,0:T(8,128)(2,1)S(1)}, bf16[48,1024]{1,0:T(8,128)(2,1)S(1)}, u32[]{:S(2)}, u32[]{:S(2)}) collective-permute-start(bf16[48,1024]{1,0:T(8,128)(2,1)S(1)} %slice.37), channel_id=1, source_target_pairs={{4,0},{5,1},{8,4},{9,5},{12,8},{13,9},{14,12},{15,13},{10,14},{11,... | collective-permute-start | bytes 294920 | tf_op jit(solution)/shard_map/ppermute | solution.py:31
  29.6 0.5 collective-permute-start.10
  30.1 4.5 %forward.4 = (bf16[192,1024]{1,0:T(8,128)(2,1)S(1)}, f32[96,1024]{1,0:T(8,128)S(1)}, f32[96,1024]{1,0:T(8,128)S(1)}, bf16[1024,4096]{1,0:T(8,128)(2,1)S(1)}) custom-call(s32[1]{0:T(128)} %bitcast.core_ref, bf16[48,2048]{1,0:T(8,128)(2,1)S(1)} %collective-permute-done.3.refs_0_.refs_3_, bf16[48,2048]{1,0:T(8,128)(2,1)S(1)} %collective-permute-done.4.refs_1_.refs_4_, ...), custom_call_target="tpu_custom_call" | custom-call | flops 2415919104 | bytes 25952256 | tf_op jit(solution)/shard_map/forward/pallas_call | solution.py:41
  34.7 2.0 %forward_own.1 = (f32[144,1024]{1,0:T(8,128)S(1)}, f32[144,1024]{1,0:T(8,128)S(1)}, f32[144,1024]{1,0:T(8,128)S(1)}) custom-call(s32[1]{0:T(128)} %bitcast.core_ref, bf16[48,2048]{1,0:T(8,128)(2,1)S(1)} %collective-permute-done.5.refs_0_.refs_5_, bf16[48,2048]{1,0:T(8,128)(2,1)S(1)} %collective-permute-done.9.refs_1_.refs_6_, ...), custom_call_target="tpu_custom_call" | custom-call | flops 1811939328 | bytes 25755648 | tf_op jit(solution)/shard_map/forward_own/pallas_call | solution.py:41
  36.8 2.5 %forward.5 = (bf16[288,1024]{1,0:T(8,128)(2,1)S(1)}, f32[144,1024]{1,0:T(8,128)S(1)}, f32[144,1024]{1,0:T(8,128)S(1)}) custom-call(s32[1]{0:T(128)} %bitcast.core_ref, bf16[48,2048]{1,0:T(8,128)(2,1)S(1)} %collective-permute-done.14.refs_0_.refs_13_, bf16[48,2048]{1,0:T(8,128)(2,1)S(1)} %collective-permute-done.15.refs_1_.refs_14_, ...), custom_call_target="tpu_custom_call" | custom-call | flops 1811939328 | bytes 26640384 | tf_op jit(solution)/shard_map/forward/pallas_call | solution.py:41
  39.3 1.4 %down.4 = bf16[288,2048]{1,0:T(8,128)(2,1)S(1)} custom-call(s32[1]{0:T(128)} %bitcast.core_ref, bf16[288,1024]{1,0:T(8,128)(2,1)S(1)} %get-tuple-element.51.refs_0_, bf16[1024,4096]{1,0:T(8,128)(2,1)S(1)} %get-tuple-element.52.refs_1_.refs_2_.refs_10_.refs_3_.refs_4_), custom_call_target="tpu_custom_call" | custom-call | flops 1207959552 | bytes 8978432 | tf_op jit(solution)/shard_map/down/pallas_call | solution.py:41
  40.8 0.6 collective-permute-start.17
  41.8 1.4 %down.3.refs_0_ = bf16[288,2048]{1,0:T(8,128)(2,1)S(1)} custom-call(s32[1]{0:T(128)} %bitcast.core_ref, bf16[288,1024]{1,0:T(8,128)(2,1)S(1)} %get-tuple-element.51.refs_0_, bf16[1024,4096]{1,0:T(8,128)(2,1)S(1)} %get-tuple-element.52.refs_1_.refs_2_.refs_10_.refs_3_.refs_4_), custom_call_target="tpu_custom_call" | custom-call | flops 1207959552 | bytes 8978432 | tf_op jit(solution)/shard_map/down/pallas_call | solution.py:41
  43.3 0.6 collective-permute-start.22
  44.0 1.4 %collective-permute-start.23 = (bf16[96,1024]{1,0:T(8,128)(2,1)S(1)}, bf16[96,1024]{1,0:T(8,128)(2,1)S(1)}, u32[]{:S(2)}, u32[]{:S(2)}) collective-permute-start(bf16[96,1024]{1,0:T(8,128)(2,1)S(1)} %get-tuple-element.58), channel_id=1, source_target_pairs={{4,0},{5,1},{8,4},{9,5},{12,8},{13,9},{14,12},{15,13},{10,14},{11,... | collective-permute-start | bytes 589832 | tf_op jit(solution)/shard_map/ppermute | solution.py:31
  45.4 4.2 %down.5 = (bf16[480,2048]{1,0:T(8,128)(2,1)S(1)}, bf16[480,2048]{1,0:T(8,128)(2,1)S(1)}) custom-call(s32[1]{0:T(128)} %bitcast.core_ref, bf16[288,1024]{1,0:T(8,128)(2,1)S(1)} %get-tuple-element.54.refs_0_, bf16[192,1024]{1,0:T(8,128)(2,1)S(1)} %get-tuple-element.55.refs_1_, bf16[1024,4096]{1,0:T(8,128)(2,1)S(1)} %get-tuple-element.52.refs_1_.refs_2_.refs_10_.refs_3_.refs_4_), custom_call_target="tpu_custom_call" | custom-call | flops 4026531840 | bytes 9371648 | tf_op jit(solution)/shard_map/down/pallas_call | solution.py:41
  50.7 1.6 %collective-permute-start.30 = (bf16[96,2048]{1,0:T(8,128)(2,1)S(1)}, bf16[96,2048]{1,0:T(8,128)(2,1)S(1)}, u32[]{:S(2)}, u32[]{:S(2)}) collective-permute-start(bf16[96,2048]{1,0:T(8,128)(2,1)S(1)} %merge.12), channel_id=1, source_target_pairs={{4,0},{5,1},{8,4},{9,5},{12,8},{13,9},{14,12},{15,13},{10,14},{11,... | collective-permute-start | bytes 1179656 | tf_op jit(solution)/shard_map/ppermute | solution.py:31
  52.4 0.5 collective-permute-start.24
  53.0 0.5 collective-permute-start.19
  53.5 8.5 %collective-permute-done.30.refs_2_ = bf16[96,2048]{1,0:T(8,128)(2,1)S(1)} collective-permute-done((bf16[96,2048]{1,0:T(8,128)(2,1)S(1)}, bf16[96,2048]{1,0:T(8,128)(2,1)S(1)}, u32[]{:S(2)}, u32[]{:S(2)}) %collective-permute-start.30) | collective-permute-done | bytes 393248 | tf_op jit(solution)/shard_map/ppermute | solution.py:31
  62.1 1.6 %collective-permute-start.31 = (bf16[96,2048]{1,0:T(8,128)(2,1)S(1)}, bf16[96,2048]{1,0:T(8,128)(2,1)S(1)}, u32[]{:S(2)}, u32[]{:S(2)}) collective-permute-start(bf16[96,2048]{1,0:T(8,128)(2,1)S(1)} %merge.13), channel_id=1, source_target_pairs={{4,0},{5,1},{8,4},{9,5},{12,8},{13,9},{14,12},{15,13},{10,14},{11,... | collective-permute-start | bytes 1179656 | tf_op jit(solution)/shard_map/ppermute | solution.py:31
  63.9 0.5 collective-permute-start.25
  64.4 8.2 %collective-permute-done.31.refs_2_ = bf16[96,2048]{1,0:T(8,128)(2,1)S(1)} collective-permute-done((bf16[96,2048]{1,0:T(8,128)(2,1)S(1)}, bf16[96,2048]{1,0:T(8,128)(2,1)S(1)}, u32[]{:S(2)}, u32[]{:S(2)}) %collective-permute-start.31) | collective-permute-done | bytes 393248 | tf_op jit(solution)/shard_map/ppermute | solution.py:31
  72.7 1.7 %collective-permute-start.32 = (bf16[96,2048]{1,0:T(8,128)(2,1)S(1)}, bf16[96,2048]{1,0:T(8,128)(2,1)S(1)}, u32[]{:S(2)}, u32[]{:S(2)}) collective-permute-start(bf16[96,2048]{1,0:T(8,128)(2,1)S(1)} %merge.14), channel_id=1, source_target_pairs={{4,0},{5,1},{8,4},{9,5},{12,8},{13,9},{14,12},{15,13},{10,14},{11,... | collective-permute-start | bytes 1179656 | tf_op jit(solution)/shard_map/ppermute | solution.py:31
  74.6 0.5 collective-permute-start.26
  75.1 1.3 collective-permute-done.33
  76.5 5.8 %collective-permute-done.32.refs_3_ = bf16[96,2048]{1,0:T(8,128)(2,1)S(1)} collective-permute-done((bf16[96,2048]{1,0:T(8,128)(2,1)S(1)}, bf16[96,2048]{1,0:T(8,128)(2,1)S(1)}, u32[]{:S(2)}, u32[]{:S(2)}) %collective-permute-start.32) | collective-permute-done | bytes 393248 | tf_op jit(solution)/shard_map/ppermute | solution.py:31
  82.3 1.6 %collective-permute-done.26.refs_2_ = bf16[96,2048]{1,0:T(8,128)(2,1)S(1)} collective-permute-done((bf16[96,2048]{1,0:T(8,128)(2,1)S(1)}, bf16[96,2048]{1,0:T(8,128)(2,1)S(1)}, u32[]{:S(2)}, u32[]{:S(2)}) %collective-permute-start.26) | collective-permute-done | bytes 393248 | tf_op jit(solution)/shard_map/ppermute | solution.py:31
  84.1 0.5 collective-permute-start.34
  84.5 1.6 %collective-permute-start.35 = (bf16[96,2048]{1,0:T(8,128)(2,1)S(1)}, bf16[96,2048]{1,0:T(8,128)(2,1)S(1)}, u32[]{:S(2)}, u32[]{:S(2)}) collective-permute-start(bf16[96,2048]{1,0:T(8,128)(2,1)S(1)} %merge.15.refs_0_), channel_id=1, source_target_pairs={{4,0},{5,1},{8,4},{9,5},{12,8},{13,9},{14,12},{15,13},{10,14},{11,... | collective-permute-start | bytes 1179656 | tf_op jit(solution)/shard_map/ppermute | solution.py:31
  86.1 7.3 %collective-permute-done.34.refs_1_ = bf16[96,2048]{1,0:T(8,128)(2,1)S(1)} collective-permute-done((bf16[96,2048]{1,0:T(8,128)(2,1)S(1)}, bf16[96,2048]{1,0:T(8,128)(2,1)S(1)}, u32[]{:S(2)}, u32[]{:S(2)}) %collective-permute-start.34) | collective-permute-done | bytes 393248 | tf_op jit(solution)/shard_map/ppermute | solution.py:31
  93.8 1.6 %collective-permute-start.37 = (bf16[96,2048]{1,0:T(8,128)(2,1)S(1)}, bf16[96,2048]{1,0:T(8,128)(2,1)S(1)}, u32[]{:S(2)}, u32[]{:S(2)}) collective-permute-start(bf16[96,2048]{1,0:T(8,128)(2,1)S(1)} %collective-permute-done.35.refs_2_), channel_id=1, source_target_pairs={{4,0},{5,1},{8,4},{9,5},{12,8},{13,9},{14,12},{15,13},{10,14},{11,... | collective-permute-start | bytes 1179656 | tf_op jit(solution)/shard_map/ppermute | solution.py:31
  95.4 0.5 collective-permute-start.39
  95.9 5.2 %collective-permute-done.36.refs_3_ = bf16[96,2048]{1,0:T(8,128)(2,1)S(1)} collective-permute-done((bf16[96,2048]{1,0:T(8,128)(2,1)S(1)}, bf16[96,2048]{1,0:T(8,128)(2,1)S(1)}, u32[]{:S(2)}, u32[]{:S(2)}) %collective-permute-start.36) | collective-permute-done | bytes 393248 | tf_op jit(solution)/shard_map/ppermute | solution.py:31
  102.1 1.6 %collective-permute-start.45 = (bf16[96,2048]{1,0:T(8,128)(2,1)S(1)}, bf16[96,2048]{1,0:T(8,128)(2,1)S(1)}, u32[]{:S(2)}, u32[]{:S(2)}) collective-permute-start(bf16[96,2048]{1,0:T(8,128)(2,1)S(1)} %collective-permute-done.37.refs_4_), channel_id=1, source_target_pairs={{4,0},{5,1},{8,4},{9,5},{12,8},{13,9},{14,12},{15,13},{10,14},{11,... | collective-permute-start | bytes 1179656 | tf_op jit(solution)/shard_map/ppermute | solution.py:31
  103.7 4.3 %back.2.refs_16_ = bf16[240,1024]{1,0:T(8,128)(2,1)S(1)} custom-call(s32[1]{0:T(128)} %bitcast.core_ref, bf16[96,2048]{1,0:T(8,128)(2,1)S(1)} %merge.15.refs_0_, bf16[96,2048]{1,0:T(8,128)(2,1)S(1)} %collective-permute-done.34.refs_1_, bf16[96,2048]{1,0:T(8,128)(2,1)S(1)} %collective-permute-done.35.refs_2_, ...), custom_call_target="tpu_custom_call" | custom-call | flops 4026531840 | bytes 13303808 | tf_op jit(solution)/shard_map/back/pallas_call | solution.py:41
  108.0 5.1 %collective-permute-done.43.refs_0_ = bf16[96,2048]{1,0:T(8,128)(2,1)S(1)} collective-permute-done((bf16[96,2048]{1,0:T(8,128)(2,1)S(1)}, bf16[96,2048]{1,0:T(8,128)(2,1)S(1)}, u32[]{:S(2)}, u32[]{:S(2)}) %collective-permute-start.43) | collective-permute-done | bytes 393248 | tf_op jit(solution)/shard_map/ppermute | solution.py:31
  113.5 2.1 %collective-permute-start.48 = (bf16[96,1024]{1,0:T(8,128)(2,1)S(1)}, bf16[96,1024]{1,0:T(8,128)(2,1)S(1)}, u32[]{:S(2)}, u32[]{:S(2)}) collective-permute-start(bf16[96,1024]{1,0:T(8,128)(2,1)S(1)} %slice.47), channel_id=1, source_target_pairs={{4,0},{5,1},{8,4},{9,5},{12,8},{13,9},{14,12},{15,13},{10,14},{11,... | collective-permute-start | bytes 589832 | tf_op jit(solution)/shard_map/ppermute | solution.py:31
  115.6 0.5 collective-permute-start.44
  116.1 3.6 %collective-permute-done.47 = bf16[96,1024]{1,0:T(8,128)(2,1)S(1)} collective-permute-done((bf16[96,1024]{1,0:T(8,128)(2,1)S(1)}, bf16[96,1024]{1,0:T(8,128)(2,1)S(1)}, u32[]{:S(2)}, u32[]{:S(2)}) %collective-permute-start.47) | collective-permute-done | bytes 196640 | tf_op jit(solution)/shard_map/ppermute | solution.py:31
  120.1 1.4 %back_own.1.refs_3_ = f32[288,1024]{1,0:T(8,128)S(1)} custom-call(s32[1]{0:T(128)} %bitcast.core_ref, bf16[96,2048]{1,0:T(8,128)(2,1)S(1)} %collective-permute-done.43.refs_0_, bf16[96,2048]{1,0:T(8,128)(2,1)S(1)} %collective-permute-done.45.refs_1_, bf16[96,2048]{1,0:T(8,128)(2,1)S(1)} %constant_dynamic-update-slice_fusion.2.refs_2_, ...), custom_call_target="tpu_custom_call" | custom-call | flops 1207959552 | bytes 9568256 | tf_op jit(solution)/shard_map/back_own/pallas_call | solution.py:41
  121.8 1.4 %back.3.refs_17_ = bf16[144,1024]{1,0:T(8,128)(2,1)S(1)} custom-call(s32[1]{0:T(128)} %bitcast.core_ref, bf16[96,2048]{1,0:T(8,128)(2,1)S(1)} %collective-permute-done.44.refs_0_, bf16[96,2048]{1,0:T(8,128)(2,1)S(1)} %collective-permute-done.46.refs_1_, bf16[96,2048]{1,0:T(8,128)(2,1)S(1)} %collective-permute-done.49.refs_2_, ...), custom_call_target="tpu_custom_call" | custom-call | flops 1207959552 | bytes 10747904 | tf_op jit(solution)/shard_map/back/pallas_call | solution.py:41
  123.3 5.6 %outer.1 = bf16[4096,1024]{1,0:T(8,128)(2,1)} custom-call(s32[1]{0:T(128)} %bitcast.core_ref, bf16[48,2048]{1,0:T(8,128)(2,1)S(1)} %maximum_select_fusion.after_ref.refs_0_, bf16[48,2048]{1,0:T(8,128)(2,1)S(1)} %collective-permute-done.1.refs_1_, bf16[48,2048]{1,0:T(8,128)(2,1)S(1)} %collective-permute-done.2.refs_2_, ...), custom_call_target="tpu_custom_call" | custom-call | flops 3221225472 | bytes 8388608 | tf_op jit(solution)/shard_map/outer/pallas_call | solution.py:368
  (88 shorter events, 6.9 us)
Async XLA Ops:
  2.5 8.8 %collective-permute-start.2 = (bf16[48,2048]{1,0:T(8,128)(2,1)S(1)}, bf16[48,2048]{1,0:T(8,128)(2,1)S(1)}, u32[]{:S(2)}, u32[]{:S(2)}) collective-permute-start(bf16[48,2048]{1,0:T(8,128)(2,1)S(1)} %maximum_select_fusion.after_ref.refs_0_), channel_id=1, source_target_pairs={{4,0},{5,1},{8,4},{9,5},{12,8},{13,9},{14,12},{15,13},{10,14},{11,... | collective-permute-start | bytes 589832 | tf_op jit(solution)/shard_map/ppermute | solution.py:31
  5.4 7.9 %collective-permute-start.1 = (bf16[48,2048]{1,0:T(8,128)(2,1)S(1)}, bf16[48,2048]{1,0:T(8,128)(2,1)S(1)}, u32[]{:S(2)}, u32[]{:S(2)}) collective-permute-start(bf16[48,2048]{1,0:T(8,128)(2,1)S(1)} %maximum_select_fusion.after_ref.refs_0_), channel_id=1, source_target_pairs={{0,4},{1,5},{4,8},{5,9},{8,12},{9,13},{12,14},{13,15},{14,10},{15,... | collective-permute-start | bytes 589832 | tf_op jit(solution)/shard_map/ppermute | solution.py:31
  5.5 13.4 %collective-permute-start.6 = (bf16[48,2048]{1,0:T(8,128)(2,1)S(1)}, bf16[48,2048]{1,0:T(8,128)(2,1)S(1)}, u32[]{:S(2)}, u32[]{:S(2)}) collective-permute-start(bf16[48,2048]{1,0:T(8,128)(2,1)S(1)} %maximum_select_fusion.after_ref.refs_0_), channel_id=1, source_target_pairs={{0,1},{1,0},{2,3},{3,2},{4,5},{5,4},{6,7},{7,6},{8,9},{9,8},{10,11... | collective-permute-start | bytes 589832 | tf_op jit(solution)/shard_map/ppermute | solution.py:31
  11.3 7.6 %collective-permute-start.4 = (bf16[48,2048]{1,0:T(8,128)(2,1)S(1)}, bf16[48,2048]{1,0:T(8,128)(2,1)S(1)}, u32[]{:S(2)}, u32[]{:S(2)}) collective-permute-start(bf16[48,2048]{1,0:T(8,128)(2,1)S(1)} %collective-permute-done.2.refs_2_), channel_id=1, source_target_pairs={{4,0},{5,1},{8,4},{9,5},{12,8},{13,9},{14,12},{15,13},{10,14},{11,... | collective-permute-start | bytes 589832 | tf_op jit(solution)/shard_map/ppermute | solution.py:31
  13.3 7.3 %collective-permute-start.3 = (bf16[48,2048]{1,0:T(8,128)(2,1)S(1)}, bf16[48,2048]{1,0:T(8,128)(2,1)S(1)}, u32[]{:S(2)}, u32[]{:S(2)}) collective-permute-start(bf16[48,2048]{1,0:T(8,128)(2,1)S(1)} %collective-permute-done.1.refs_1_), channel_id=1, source_target_pairs={{0,4},{1,5},{4,8},{5,9},{8,12},{9,13},{12,14},{13,15},{14,10},{15,... | collective-permute-start | bytes 589832 | tf_op jit(solution)/shard_map/ppermute | solution.py:31
  13.4 7.4 %collective-permute-start.8 = (bf16[48,2048]{1,0:T(8,128)(2,1)S(1)}, bf16[48,2048]{1,0:T(8,128)(2,1)S(1)}, u32[]{:S(2)}, u32[]{:S(2)}) collective-permute-start(bf16[48,2048]{1,0:T(8,128)(2,1)S(1)} %collective-permute-done.2.refs_2_), channel_id=1, source_target_pairs={{0,1},{1,0},{2,3},{3,2},{4,5},{5,4},{6,7},{7,6},{8,9},{9,8},{10,11... | collective-permute-start | bytes 589832 | tf_op jit(solution)/shard_map/ppermute | solution.py:31
  13.6 7.6 %collective-permute-start.7 = (bf16[48,2048]{1,0:T(8,128)(2,1)S(1)}, bf16[48,2048]{1,0:T(8,128)(2,1)S(1)}, u32[]{:S(2)}, u32[]{:S(2)}) collective-permute-start(bf16[48,2048]{1,0:T(8,128)(2,1)S(1)} %collective-permute-done.1.refs_1_), channel_id=1, source_target_pairs={{0,1},{1,0},{2,3},{3,2},{4,5},{5,4},{6,7},{7,6},{8,9},{9,8},{10,11... | collective-permute-start | bytes 589832 | tf_op jit(solution)/shard_map/ppermute | solution.py:31
  18.9 10.7 %collective-permute-start.12 = (bf16[48,2048]{1,0:T(8,128)(2,1)S(1)}, bf16[48,2048]{1,0:T(8,128)(2,1)S(1)}, u32[]{:S(2)}, u32[]{:S(2)}) collective-permute-start(bf16[48,2048]{1,0:T(8,128)(2,1)S(1)} %collective-permute-done.4.refs_1_.refs_4_), channel_id=1, source_target_pairs={{0,1},{1,0},{2,3},{3,2},{4,5},{5,4},{6,7},{7,6},{8,9},{9,8},{10,11... | collective-permute-start | bytes 589832 | tf_op jit(solution)/shard_map/ppermute | solution.py:31
  18.9 7.4 %collective-permute-start.9 = (bf16[48,2048]{1,0:T(8,128)(2,1)S(1)}, bf16[48,2048]{1,0:T(8,128)(2,1)S(1)}, u32[]{:S(2)}, u32[]{:S(2)}) collective-permute-start(bf16[48,2048]{1,0:T(8,128)(2,1)S(1)} %collective-permute-done.4.refs_1_.refs_4_), channel_id=1, source_target_pairs={{4,0},{5,1},{8,4},{9,5},{12,8},{13,9},{14,12},{15,13},{10,14},{11,... | collective-permute-start | bytes 589832 | tf_op jit(solution)/shard_map/ppermute | solution.py:31
  20.6 9.5 %collective-permute-start.11 = (bf16[48,2048]{1,0:T(8,128)(2,1)S(1)}, bf16[48,2048]{1,0:T(8,128)(2,1)S(1)}, u32[]{:S(2)}, u32[]{:S(2)}) collective-permute-start(bf16[48,2048]{1,0:T(8,128)(2,1)S(1)} %collective-permute-done.3.refs_0_.refs_3_), channel_id=1, source_target_pairs={{0,1},{1,0},{2,3},{3,2},{4,5},{5,4},{6,7},{7,6},{8,9},{9,8},{10,11... | collective-permute-start | bytes 589832 | tf_op jit(solution)/shard_map/ppermute | solution.py:31
  20.8 7.1 %collective-permute-start.5 = (bf16[48,2048]{1,0:T(8,128)(2,1)S(1)}, bf16[48,2048]{1,0:T(8,128)(2,1)S(1)}, u32[]{:S(2)}, u32[]{:S(2)}) collective-permute-start(bf16[48,2048]{1,0:T(8,128)(2,1)S(1)} %collective-permute-done.3.refs_0_.refs_3_), channel_id=1, source_target_pairs={{0,4},{1,5},{4,8},{5,9},{8,12},{9,13},{12,14},{13,15},{14,10},{15,... | collective-permute-start | bytes 589832 | tf_op jit(solution)/shard_map/ppermute | solution.py:31
  26.3 10.5 %collective-permute-start.15 = (bf16[48,2048]{1,0:T(8,128)(2,1)S(1)}, bf16[48,2048]{1,0:T(8,128)(2,1)S(1)}, u32[]{:S(2)}, u32[]{:S(2)}) collective-permute-start(bf16[48,2048]{1,0:T(8,128)(2,1)S(1)} %collective-permute-done.9.refs_1_.refs_6_), channel_id=1, source_target_pairs={{0,1},{1,0},{2,3},{3,2},{4,5},{5,4},{6,7},{7,6},{8,9},{9,8},{10,11... | collective-permute-start | bytes 589832 | tf_op jit(solution)/shard_map/ppermute | solution.py:31
  27.9 8.9 %collective-permute-start.14 = (bf16[48,2048]{1,0:T(8,128)(2,1)S(1)}, bf16[48,2048]{1,0:T(8,128)(2,1)S(1)}, u32[]{:S(2)}, u32[]{:S(2)}) collective-permute-start(bf16[48,2048]{1,0:T(8,128)(2,1)S(1)} %collective-permute-done.5.refs_0_.refs_5_), channel_id=1, source_target_pairs={{0,1},{1,0},{2,3},{3,2},{4,5},{5,4},{6,7},{7,6},{8,9},{9,8},{10,11... | collective-permute-start | bytes 589832 | tf_op jit(solution)/shard_map/ppermute | solution.py:31
  28.0 6.6 %collective-permute-start.13 = (bf16[48,1024]{1,0:T(8,128)(2,1)S(1)}, bf16[48,1024]{1,0:T(8,128)(2,1)S(1)}, u32[]{:S(2)}, u32[]{:S(2)}) collective-permute-start(bf16[48,1024]{1,0:T(8,128)(2,1)S(1)} %slice.37), channel_id=1, source_target_pairs={{4,0},{5,1},{8,4},{9,5},{12,8},{13,9},{14,12},{15,13},{10,14},{11,... | collective-permute-start | bytes 294920 | tf_op jit(solution)/shard_map/ppermute | solution.py:31
  29.6 5.0 %collective-permute-start.10 = (bf16[48,1024]{1,0:T(8,128)(2,1)S(1)}, bf16[48,1024]{1,0:T(8,128)(2,1)S(1)}, u32[]{:S(2)}, u32[]{:S(2)}) collective-permute-start(bf16[48,1024]{1,0:T(8,128)(2,1)S(1)} %slice.36), channel_id=1, source_target_pairs={{0,4},{1,5},{4,8},{5,9},{8,12},{9,13},{12,14},{13,15},{14,10},{15,... | collective-permute-start | bytes 294920 | tf_op jit(solution)/shard_map/ppermute | solution.py:31
  34.6 2.1 %collective-permute-start.16 = (bf16[48,2048]{1,0:T(8,128)(2,1)S(1)}, bf16[48,2048]{1,0:T(8,128)(2,1)S(1)}, u32[]{:S(2)}, u32[]{:S(2)}) collective-permute-start(bf16[48,2048]{1,0:T(8,128)(2,1)S(1)} %constant_dynamic-update-slice_fusion.refs_2_.refs_7_), channel_id=1, source_target_pairs={{0,1},{1,0},{2,3},{3,2},{4,5},{5,4},{6,7},{7,6},{8,9},{9,8},{10,11... | collective-permute-start | bytes 589832 | tf_op jit(solution)/shard_map/ppermute | solution.py:31
  40.8 2.5 %collective-permute-start.17 = (bf16[96,2048]{1,0:T(8,128)(2,1)S(1)}, bf16[96,2048]{1,0:T(8,128)(2,1)S(1)}, u32[]{:S(2)}, u32[]{:S(2)}) collective-permute-start(bf16[96,2048]{1,0:T(8,128)(2,1)S(1)} %get-tuple-element.76), channel_id=1, source_target_pairs={{0,1},{1,0},{2,3},{3,2},{4,5},{5,4},{6,7},{7,6},{8,9},{9,8},{10,11... | collective-permute-start | bytes 1179656 | tf_op jit(solution)/shard_map/ppermute | solution.py:31
  41.3 9.3 %collective-permute-start.29 = (bf16[96,2048]{1,0:T(8,128)(2,1)S(1)}, bf16[96,2048]{1,0:T(8,128)(2,1)S(1)}, u32[]{:S(2)}, u32[]{:S(2)}) collective-permute-start(bf16[96,2048]{1,0:T(8,128)(2,1)S(1)} %get-tuple-element.74), channel_id=1, source_target_pairs={{0,1},{1,0},{2,3},{3,2},{4,5},{5,4},{6,7},{7,6},{8,9},{9,8},{10,11... | collective-permute-start | bytes 1179656 | tf_op jit(solution)/shard_map/ppermute | solution.py:31
  41.4 10.9 %collective-permute-start.21 = (bf16[96,2048]{1,0:T(8,128)(2,1)S(1)}, bf16[96,2048]{1,0:T(8,128)(2,1)S(1)}, u32[]{:S(2)}, u32[]{:S(2)}) collective-permute-start(bf16[96,2048]{1,0:T(8,128)(2,1)S(1)} %get-tuple-element.75), channel_id=1, source_target_pairs={{0,1},{1,0},{2,3},{3,2},{4,5},{5,4},{6,7},{7,6},{8,9},{9,8},{10,11... | collective-permute-start | bytes 1179656 | tf_op jit(solution)/shard_map/ppermute | solution.py:31
  43.3 6.9 %collective-permute-start.22 = (bf16[96,1024]{1,0:T(8,128)(2,1)S(1)}, bf16[96,1024]{1,0:T(8,128)(2,1)S(1)}, u32[]{:S(2)}, u32[]{:S(2)}) collective-permute-start(bf16[96,1024]{1,0:T(8,128)(2,1)S(1)} %get-tuple-element.53), channel_id=1, source_target_pairs={{0,4},{1,5},{4,8},{5,9},{8,12},{9,13},{12,14},{13,15},{14,10},{15,... | collective-permute-start | bytes 589832 | tf_op jit(solution)/shard_map/ppermute | solution.py:31
  44.0 6.6 %collective-permute-start.23 = (bf16[96,1024]{1,0:T(8,128)(2,1)S(1)}, bf16[96,1024]{1,0:T(8,128)(2,1)S(1)}, u32[]{:S(2)}, u32[]{:S(2)}) collective-permute-start(bf16[96,1024]{1,0:T(8,128)(2,1)S(1)} %get-tuple-element.58), channel_id=1, source_target_pairs={{4,0},{5,1},{8,4},{9,5},{12,8},{13,9},{14,12},{15,13},{10,14},{11,... | collective-permute-start | bytes 589832 | tf_op jit(solution)/shard_map/ppermute | solution.py:31
  49.8 3.2 %collective-permute-start.28 = (bf16[96,2048]{1,0:T(8,128)(2,1)S(1)}, bf16[96,2048]{1,0:T(8,128)(2,1)S(1)}, u32[]{:S(2)}, u32[]{:S(2)}) collective-permute-start(bf16[96,2048]{1,0:T(8,128)(2,1)S(1)} %get-tuple-element.69), channel_id=1, source_target_pairs={{0,1},{1,0},{2,3},{3,2},{4,5},{5,4},{6,7},{7,6},{8,9},{9,8},{10,11... | collective-permute-start | bytes 1179656 | tf_op jit(solution)/shard_map/ppermute | solution.py:31
  50.3 13.5 %collective-permute-start.20 = (bf16[96,2048]{1,0:T(8,128)(2,1)S(1)}, bf16[96,2048]{1,0:T(8,128)(2,1)S(1)}, u32[]{:S(2)}, u32[]{:S(2)}) collective-permute-start(bf16[96,2048]{1,0:T(8,128)(2,1)S(1)} %get-tuple-element.71), channel_id=1, source_target_pairs={{0,1},{1,0},{2,3},{3,2},{4,5},{5,4},{6,7},{7,6},{8,9},{9,8},{10,11... | collective-permute-start | bytes 1179656 | tf_op jit(solution)/shard_map/ppermute | solution.py:31
  50.7 11.3 %collective-permute-start.30 = (bf16[96,2048]{1,0:T(8,128)(2,1)S(1)}, bf16[96,2048]{1,0:T(8,128)(2,1)S(1)}, u32[]{:S(2)}, u32[]{:S(2)}) collective-permute-start(bf16[96,2048]{1,0:T(8,128)(2,1)S(1)} %merge.12), channel_id=1, source_target_pairs={{4,0},{5,1},{8,4},{9,5},{12,8},{13,9},{14,12},{15,13},{10,14},{11,... | collective-permute-start | bytes 1179656 | tf_op jit(solution)/shard_map/ppermute | solution.py:31
  52.4 11.3 %collective-permute-start.24 = (bf16[96,2048]{1,0:T(8,128)(2,1)S(1)}, bf16[96,2048]{1,0:T(8,128)(2,1)S(1)}, u32[]{:S(2)}, u32[]{:S(2)}) collective-permute-start(bf16[96,2048]{1,0:T(8,128)(2,1)S(1)} %merge.9), channel_id=1, source_target_pairs={{0,4},{1,5},{4,8},{5,9},{8,12},{9,13},{12,14},{13,15},{14,10},{15,... | collective-permute-start | bytes 1179656 | tf_op jit(solution)/shard_map/ppermute | solution.py:31
  53.0 11.5 %collective-permute-start.27 = (bf16[96,2048]{1,0:T(8,128)(2,1)S(1)}, bf16[96,2048]{1,0:T(8,128)(2,1)S(1)}, u32[]{:S(2)}, u32[]{:S(2)}) collective-permute-start(bf16[96,2048]{1,0:T(8,128)(2,1)S(1)} %get-tuple-element.70), channel_id=1, source_target_pairs={{0,1},{1,0},{2,3},{3,2},{4,5},{5,4},{6,7},{7,6},{8,9},{9,8},{10,11... | collective-permute-start | bytes 1179656 | tf_op jit(solution)/shard_map/ppermute | solution.py:31
  53.0 21.4 %collective-permute-start.19 = (bf16[96,2048]{1,0:T(8,128)(2,1)S(1)}, bf16[96,2048]{1,0:T(8,128)(2,1)S(1)}, u32[]{:S(2)}, u32[]{:S(2)}) collective-permute-start(bf16[96,2048]{1,0:T(8,128)(2,1)S(1)} %get-tuple-element.72), channel_id=1, source_target_pairs={{0,1},{1,0},{2,3},{3,2},{4,5},{5,4},{6,7},{7,6},{8,9},{9,8},{10,11... | collective-permute-start | bytes 1179656 | tf_op jit(solution)/shard_map/ppermute | solution.py:31
  62.1 10.5 %collective-permute-start.31 = (bf16[96,2048]{1,0:T(8,128)(2,1)S(1)}, bf16[96,2048]{1,0:T(8,128)(2,1)S(1)}, u32[]{:S(2)}, u32[]{:S(2)}) collective-permute-start(bf16[96,2048]{1,0:T(8,128)(2,1)S(1)} %merge.13), channel_id=1, source_target_pairs={{4,0},{5,1},{8,4},{9,5},{12,8},{13,9},{14,12},{15,13},{10,14},{11,... | collective-permute-start | bytes 1179656 | tf_op jit(solution)/shard_map/ppermute | solution.py:31
  63.9 10.5 %collective-permute-start.25 = (bf16[96,2048]{1,0:T(8,128)(2,1)S(1)}, bf16[96,2048]{1,0:T(8,128)(2,1)S(1)}, u32[]{:S(2)}, u32[]{:S(2)}) collective-permute-start(bf16[96,2048]{1,0:T(8,128)(2,1)S(1)} %merge.10), channel_id=1, source_target_pairs={{0,4},{1,5},{4,8},{5,9},{8,12},{9,13},{12,14},{13,15},{14,10},{15,... | collective-permute-start | bytes 1179656 | tf_op jit(solution)/shard_map/ppermute | solution.py:31
  64.4 12.0 %collective-permute-start.18 = (bf16[96,2048]{1,0:T(8,128)(2,1)S(1)}, bf16[96,2048]{1,0:T(8,128)(2,1)S(1)}, u32[]{:S(2)}, u32[]{:S(2)}) collective-permute-start(bf16[96,2048]{1,0:T(8,128)(2,1)S(1)} %get-tuple-element.73), channel_id=1, source_target_pairs={{0,1},{1,0},{2,3},{3,2},{4,5},{5,4},{6,7},{7,6},{8,9},{9,8},{10,11... | collective-permute-start | bytes 1179656 | tf_op jit(solution)/shard_map/ppermute | solution.py:31
  72.7 9.5 %collective-permute-start.32 = (bf16[96,2048]{1,0:T(8,128)(2,1)S(1)}, bf16[96,2048]{1,0:T(8,128)(2,1)S(1)}, u32[]{:S(2)}, u32[]{:S(2)}) collective-permute-start(bf16[96,2048]{1,0:T(8,128)(2,1)S(1)} %merge.14), channel_id=1, source_target_pairs={{4,0},{5,1},{8,4},{9,5},{12,8},{13,9},{14,12},{15,13},{10,14},{11,... | collective-permute-start | bytes 1179656 | tf_op jit(solution)/shard_map/ppermute | solution.py:31
  74.6 9.3 %collective-permute-start.26 = (bf16[96,2048]{1,0:T(8,128)(2,1)S(1)}, bf16[96,2048]{1,0:T(8,128)(2,1)S(1)}, u32[]{:S(2)}, u32[]{:S(2)}) collective-permute-start(bf16[96,2048]{1,0:T(8,128)(2,1)S(1)} %merge.11), channel_id=1, source_target_pairs={{0,4},{1,5},{4,8},{5,9},{8,12},{9,13},{12,14},{13,15},{14,10},{15,... | collective-permute-start | bytes 1179656 | tf_op jit(solution)/shard_map/ppermute | solution.py:31
  84.1 9.3 %collective-permute-start.34 = (bf16[96,2048]{1,0:T(8,128)(2,1)S(1)}, bf16[96,2048]{1,0:T(8,128)(2,1)S(1)}, u32[]{:S(2)}, u32[]{:S(2)}) collective-permute-start(bf16[96,2048]{1,0:T(8,128)(2,1)S(1)} %merge.15.refs_0_), channel_id=1, source_target_pairs={{0,4},{1,5},{4,8},{5,9},{8,12},{9,13},{12,14},{13,15},{14,10},{15,... | collective-permute-start | bytes 1179656 | tf_op jit(solution)/shard_map/ppermute | solution.py:31
  84.5 9.3 %collective-permute-start.35 = (bf16[96,2048]{1,0:T(8,128)(2,1)S(1)}, bf16[96,2048]{1,0:T(8,128)(2,1)S(1)}, u32[]{:S(2)}, u32[]{:S(2)}) collective-permute-start(bf16[96,2048]{1,0:T(8,128)(2,1)S(1)} %merge.15.refs_0_), channel_id=1, source_target_pairs={{4,0},{5,1},{8,4},{9,5},{12,8},{13,9},{14,12},{15,13},{10,14},{11,... | collective-permute-start | bytes 1179656 | tf_op jit(solution)/shard_map/ppermute | solution.py:31
  93.4 7.8 %collective-permute-start.36 = (bf16[96,2048]{1,0:T(8,128)(2,1)S(1)}, bf16[96,2048]{1,0:T(8,128)(2,1)S(1)}, u32[]{:S(2)}, u32[]{:S(2)}) collective-permute-start(bf16[96,2048]{1,0:T(8,128)(2,1)S(1)} %collective-permute-done.34.refs_1_), channel_id=1, source_target_pairs={{0,4},{1,5},{4,8},{5,9},{8,12},{9,13},{12,14},{13,15},{14,10},{15,... | collective-permute-start | bytes 1179656 | tf_op jit(solution)/shard_map/ppermute | solution.py:31
  93.8 7.8 %collective-permute-start.37 = (bf16[96,2048]{1,0:T(8,128)(2,1)S(1)}, bf16[96,2048]{1,0:T(8,128)(2,1)S(1)}, u32[]{:S(2)}, u32[]{:S(2)}) collective-permute-start(bf16[96,2048]{1,0:T(8,128)(2,1)S(1)} %collective-permute-done.35.refs_2_), channel_id=1, source_target_pairs={{4,0},{5,1},{8,4},{9,5},{12,8},{13,9},{14,12},{15,13},{10,14},{11,... | collective-permute-start | bytes 1179656 | tf_op jit(solution)/shard_map/ppermute | solution.py:31
  95.4 6.3 %collective-permute-start.38 = (bf16[96,2048]{1,0:T(8,128)(2,1)S(1)}, bf16[96,2048]{1,0:T(8,128)(2,1)S(1)}, u32[]{:S(2)}, u32[]{:S(2)}) collective-permute-start(bf16[96,2048]{1,0:T(8,128)(2,1)S(1)} %merge.15.refs_0_), channel_id=1, source_target_pairs={{0,1},{1,0},{2,3},{3,2},{4,5},{5,4},{6,7},{7,6},{8,9},{9,8},{10,11... | collective-permute-start | bytes 1179656 | tf_op jit(solution)/shard_map/ppermute | solution.py:31
  95.4 6.7 %collective-permute-start.39 = (bf16[96,2048]{1,0:T(8,128)(2,1)S(1)}, bf16[96,2048]{1,0:T(8,128)(2,1)S(1)}, u32[]{:S(2)}, u32[]{:S(2)}) collective-permute-start(bf16[96,2048]{1,0:T(8,128)(2,1)S(1)} %collective-permute-done.34.refs_1_), channel_id=1, source_target_pairs={{0,1},{1,0},{2,3},{3,2},{4,5},{5,4},{6,7},{7,6},{8,9},{9,8},{10,11... | collective-permute-start | bytes 1179656 | tf_op jit(solution)/shard_map/ppermute | solution.py:31
  95.9 7.8 %collective-permute-start.40 = (bf16[96,2048]{1,0:T(8,128)(2,1)S(1)}, bf16[96,2048]{1,0:T(8,128)(2,1)S(1)}, u32[]{:S(2)}, u32[]{:S(2)}) collective-permute-start(bf16[96,2048]{1,0:T(8,128)(2,1)S(1)} %collective-permute-done.35.refs_2_), channel_id=1, source_target_pairs={{0,1},{1,0},{2,3},{3,2},{4,5},{5,4},{6,7},{7,6},{8,9},{9,8},{10,11... | collective-permute-start | bytes 1179656 | tf_op jit(solution)/shard_map/ppermute | solution.py:31
  101.2 2.6 %collective-permute-start.41 = (bf16[96,2048]{1,0:T(8,128)(2,1)S(1)}, bf16[96,2048]{1,0:T(8,128)(2,1)S(1)}, u32[]{:S(2)}, u32[]{:S(2)}) collective-permute-start(bf16[96,2048]{1,0:T(8,128)(2,1)S(1)} %collective-permute-done.36.refs_3_), channel_id=1, source_target_pairs={{0,1},{1,0},{2,3},{3,2},{4,5},{5,4},{6,7},{7,6},{8,9},{9,8},{10,11... | collective-permute-start | bytes 1179656 | tf_op jit(solution)/shard_map/ppermute | solution.py:31
  101.6 2.2 %collective-permute-start.42 = (bf16[96,2048]{1,0:T(8,128)(2,1)S(1)}, bf16[96,2048]{1,0:T(8,128)(2,1)S(1)}, u32[]{:S(2)}, u32[]{:S(2)}) collective-permute-start(bf16[96,2048]{1,0:T(8,128)(2,1)S(1)} %collective-permute-done.37.refs_4_), channel_id=1, source_target_pairs={{0,1},{1,0},{2,3},{3,2},{4,5},{5,4},{6,7},{7,6},{8,9},{9,8},{10,11... | collective-permute-start | bytes 1179656 | tf_op jit(solution)/shard_map/ppermute | solution.py:31
  101.7 11.4 %collective-permute-start.43 = (bf16[96,2048]{1,0:T(8,128)(2,1)S(1)}, bf16[96,2048]{1,0:T(8,128)(2,1)S(1)}, u32[]{:S(2)}, u32[]{:S(2)}) collective-permute-start(bf16[96,2048]{1,0:T(8,128)(2,1)S(1)} %collective-permute-done.36.refs_3_), channel_id=1, source_target_pairs={{0,4},{1,5},{4,8},{5,9},{8,12},{9,13},{12,14},{13,15},{14,10},{15,... | collective-permute-start | bytes 1179656 | tf_op jit(solution)/shard_map/ppermute | solution.py:31
  102.1 11.4 %collective-permute-start.45 = (bf16[96,2048]{1,0:T(8,128)(2,1)S(1)}, bf16[96,2048]{1,0:T(8,128)(2,1)S(1)}, u32[]{:S(2)}, u32[]{:S(2)}) collective-permute-start(bf16[96,2048]{1,0:T(8,128)(2,1)S(1)} %collective-permute-done.37.refs_4_), channel_id=1, source_target_pairs={{4,0},{5,1},{8,4},{9,5},{12,8},{13,9},{14,12},{15,13},{10,14},{11,... | collective-permute-start | bytes 1179656 | tf_op jit(solution)/shard_map/ppermute | solution.py:31
  113.2 6.5 %collective-permute-start.47 = (bf16[96,1024]{1,0:T(8,128)(2,1)S(1)}, bf16[96,1024]{1,0:T(8,128)(2,1)S(1)}, u32[]{:S(2)}, u32[]{:S(2)}) collective-permute-start(bf16[96,1024]{1,0:T(8,128)(2,1)S(1)} %slice.46), channel_id=1, source_target_pairs={{0,4},{1,5},{4,8},{5,9},{8,12},{9,13},{12,14},{13,15},{14,10},{15,... | collective-permute-start | bytes 589832 | tf_op jit(solution)/shard_map/ppermute | solution.py:31
  113.5 6.5 %collective-permute-start.48 = (bf16[96,1024]{1,0:T(8,128)(2,1)S(1)}, bf16[96,1024]{1,0:T(8,128)(2,1)S(1)}, u32[]{:S(2)}, u32[]{:S(2)}) collective-permute-start(bf16[96,1024]{1,0:T(8,128)(2,1)S(1)} %slice.47), channel_id=1, source_target_pairs={{4,0},{5,1},{8,4},{9,5},{12,8},{13,9},{14,12},{15,13},{10,14},{11,... | collective-permute-start | bytes 589832 | tf_op jit(solution)/shard_map/ppermute | solution.py:31
  115.6 6.0 %collective-permute-start.46 = (bf16[96,2048]{1,0:T(8,128)(2,1)S(1)}, bf16[96,2048]{1,0:T(8,128)(2,1)S(1)}, u32[]{:S(2)}, u32[]{:S(2)}) collective-permute-start(bf16[96,2048]{1,0:T(8,128)(2,1)S(1)} %collective-permute-done.45.refs_1_), channel_id=1, source_target_pairs={{0,1},{1,0},{2,3},{3,2},{4,5},{5,4},{6,7},{7,6},{8,9},{9,8},{10,11... | collective-permute-start | bytes 1179656 | tf_op jit(solution)/shard_map/ppermute | solution.py:31
  115.6 6.0 %collective-permute-start.44 = (bf16[96,2048]{1,0:T(8,128)(2,1)S(1)}, bf16[96,2048]{1,0:T(8,128)(2,1)S(1)}, u32[]{:S(2)}, u32[]{:S(2)}) collective-permute-start(bf16[96,2048]{1,0:T(8,128)(2,1)S(1)} %collective-permute-done.43.refs_0_), channel_id=1, source_target_pairs={{0,1},{1,0},{2,3},{3,2},{4,5},{5,4},{6,7},{7,6},{8,9},{9,8},{10,11... | collective-permute-start | bytes 1179656 | tf_op jit(solution)/shard_map/ppermute | solution.py:31
  120.0 1.8 %collective-permute-start.49 = (bf16[96,2048]{1,0:T(8,128)(2,1)S(1)}, bf16[96,2048]{1,0:T(8,128)(2,1)S(1)}, u32[]{:S(2)}, u32[]{:S(2)}) collective-permute-start(bf16[96,2048]{1,0:T(8,128)(2,1)S(1)} %constant_dynamic-update-slice_fusion.2.refs_2_), channel_id=1, source_target_pairs={{0,1},{1,0},{2,3},{3,2},{4,5},{5,4},{6,7},{7,6},{8,9},{9,8},{10,11... | collective-permute-start | bytes 1179656 | tf_op jit(solution)/shard_map/ppermute | solution.py:31
  (3 other events, 27.3 us)

commit v5 on v4

--- a/solution.py
+++ b/solution.py
@@ -339,23 +339,33 @@
     )[0]
 
 
-def outer(core, same, other, weighted, scale):
-    count, rows = len(same), same[0].shape[0]
+def turn(core, same, other):
     half = same[0].shape[1]
-    total, depth = count * rows, 2 * half
+    total = sum(b.shape[0] for b in same)
+
+    def kernel(core_ref, *refs):
+        blocks, out_ref = refs[:-1], refs[-1]
+        for n, part in enumerate((blocks[: len(same)], blocks[len(same) :])):
+            for start in range(0, half, 512):
+                left = jnp.concatenate([b[:, start : start + 512] for b in part])
+                out_ref[n * half + start : n * half + start + 512, :] = left.T
+
+    return call(kernel, "turn", core, [((2 * half, total), BF16)], [], 0, [*same, *other])[0]
+
+
+def outer(core, turned, weighted, scale):
+    depth, total = turned.shape
+    half = depth // 2
     columns = weighted[0].shape[1]
     tile = 512
 
     def kernel(core_ref, *refs):
-        blocks, refs = refs[: 2 * count], refs[2 * count :]
-        weighted_refs, (out_ref, held, sems) = refs[:-3], refs[-3:]
+        turned_ref, weighted_refs, (out_ref, held, sems) = refs[0], refs[1:-3], refs[-3:]
         right = jnp.concatenate([w[...] for w in weighted_refs])
         copies = []
         for own, near, at in passes(core_ref[0], half, tile):
-            left = jnp.concatenate([b[:, near] for b in (blocks[:count] if own else blocks[count:])])
-            product = lax.dot_general(
-                left, right, (((0,), (0,)), ((), ())), preferred_element_type=F32
-            )
+            first = near.start + (0 if own else half)
+            product = jnp.dot(turned_ref[first : first + tile, :], right, preferred_element_type=F32)
             slot = len(copies)
             held[slot] = (product * scale).astype(BF16)
             copies.append(pltpu.make_async_copy(held.at[slot], out_ref.at[at], sems.at[slot]))
@@ -363,7 +373,7 @@
         for copy in copies:
             copy.wait()
 
-    operands = [*same, *other, *weighted]
+    operands = [turned, *weighted]
     tiles = depth // tile
     return pl.pallas_call(
         kernel,
@@ -513,6 +523,9 @@
         else:
             (to_after,), (to_before,) = merge(core, [to_after], shape), merge(core, [to_before], shape)
         from_before, from_after = send(to_after, onward), send(to_before, backward)
+        if distance == 1:
+            turned = turn(core, [tie(same[0], to_after)[0], *same[1:]], other)
+            from_before, from_after = tie(from_before, turned)[0], tie(from_after, turned)[0]
         if distance == steps and not even and far_blocks:
             from_before, from_after, _ = tie(from_before, from_after, near_work(to_after))
     parts = []
@@ -550,7 +563,7 @@
         return done
 
     gather([message], run_back)
-    return outer(core, same, other, weighted, (mine * devices) ** (-0.5))
+    return outer(core, turned, weighted, (mine * devices) ** (-0.5))
 
 
 def solution(mesh):

time: 129 us -> 129 us (level)
  waiting for transfers between devices: 55.7 us -> 54.2 us
    ppermute x50, waiting for transfers between devices: 55.7 us -> 54.2 us  [send(): return lax.ppermute(block, AXIS, route)]
    pallas_call x18 -> x19, Pallas kernels: 29.3 us -> 30.2 us  [call(): pl.pallas_call(kernel, in_specs=[IN_SMEM] + [IN_VMEM] * len(operands) + [...]
  transfers between devices with their start and end apart: 50 -> 50, of which waited for: 17 -> 17; matrix products, arithmetic and copies ran while one was open for 0% -> 0% of each run, Pallas kernels for 23% -> 24%
where the time goes in v5:
time: 129 us
  waiting for transfers between devices  54.2 us (42%)
  Pallas kernels  41.6 us (32%)
  starting transfers between devices  31.1 us (24%)
  local copies, waits for them, and re-layouts  1.33 us (1%)
    ppermute x50, waiting for transfers between devices, send(): return lax.ppermute(block, AXIS, route)  54.2 us
    ppermute x50, starting transfers between devices, send(): return lax.ppermute(block, AXIS, route)  31.1 us
    pallas_call x19, Pallas kernels, call(): pl.pallas_call(kernel, in_specs=[IN_SMEM] + [IN_VMEM] * len(operands) + [...  30.2 us
    pallas_call x1, Pallas kernels, fetch(): pl.pallas_call(kernel, in_specs=[pl.BlockSpec(memory_space=pl.ANY)] + [pl...  5.78 us
    pallas_call x1, Pallas kernels, outer(): pl.pallas_call(kernel, in_specs=[IN_SMEM] + [IN_VMEM] * len(operands), ou...  5.59 us
  transfers between devices with their start and end apart: 50, of which 17 were waited for; matrix products, arithmetic and copies ran while one was open for 0% of the time, Pallas kernels for 24%

profile of v5, /device:TPU:0, one launch (start us, length us, event | category | flops | bytes accessed | tf_op | source)
XLA Modules:
  0.0 128.9 jit_solution(9221588952743423243)
XLA Ops:
  0.0 1.0 constant_dynamic-slice_fusion.3
  1.0 0.5 collective-permute-start
  1.5 0.9 collective-permute-done
  2.5 2.9 %collective-permute-start.2 = (bf16[48,2048]{1,0:T(8,128)(2,1)S(1)}, bf16[48,2048]{1,0:T(8,128)(2,1)S(1)}, u32[]{:S(2)}, u32[]{:S(2)}) collective-permute-start(bf16[48,2048]{1,0:T(8,128)(2,1)S(1)} %maximum_select_fusion.after_ref.refs_0_), channel_id=1, source_target_pairs={{4,0},{5,1},{8,4},{9,5},{12,8},{13,9},{14,12},{15,13},{10,14},{11,... | collective-permute-start | bytes 589832 | tf_op jit(solution)/shard_map/ppermute | solution.py:31
  5.5 5.8 %fetch.1 = (bf16[4096,1024]{1,0:T(8,128)(2,1)S(1)}, bf16[4096,1024]{1,0:T(8,128)(2,1)S(1)}) custom-call(bf16[48,2048]{1,0:T(8,128)(2,1)S(1)} %maximum_select_fusion.after_ref.refs_0_, bf16[4096,1024]{1,0:T(8,128)(2,1)} %refs_0_.1, bf16[4096,1024]{1,0:T(8,128)(2,1)} %refs_1_.1), custom_call_target="tpu_custom_call" | custom-call | bytes 16777216 | tf_op jit(solution)/shard_map/fetch/pallas_call | solution.py:77
  11.3 2.0 %collective-permute-start.7 = (bf16[48,2048]{1,0:T(8,128)(2,1)S(1)}, bf16[48,2048]{1,0:T(8,128)(2,1)S(1)}, u32[]{:S(2)}, u32[]{:S(2)}) collective-permute-start(bf16[48,2048]{1,0:T(8,128)(2,1)S(1)} %collective-permute-done.2.refs_2_), channel_id=1, source_target_pairs={{4,0},{5,1},{8,4},{9,5},{12,8},{13,9},{14,12},{15,13},{10,14},{11,... | collective-permute-start | bytes 589832 | tf_op jit(solution)/shard_map/ppermute | solution.py:31
  13.9 5.0 %collective-permute-done.7.refs_1_.refs_4_ = bf16[48,2048]{1,0:T(8,128)(2,1)S(1)} collective-permute-done((bf16[48,2048]{1,0:T(8,128)(2,1)S(1)}, bf16[48,2048]{1,0:T(8,128)(2,1)S(1)}, u32[]{:S(2)}, u32[]{:S(2)}) %collective-permute-start.7) | collective-permute-done | bytes 196640 | tf_op jit(solution)/shard_map/ppermute | solution.py:31
  18.9 1.7 %collective-permute-start.12 = (bf16[48,2048]{1,0:T(8,128)(2,1)S(1)}, bf16[48,2048]{1,0:T(8,128)(2,1)S(1)}, u32[]{:S(2)}, u32[]{:S(2)}) collective-permute-start(bf16[48,2048]{1,0:T(8,128)(2,1)S(1)} %collective-permute-done.7.refs_1_.refs_4_), channel_id=1, source_target_pairs={{4,0},{5,1},{8,4},{9,5},{12,8},{13,9},{14,12},{15,13},{10,14},{11,... | collective-permute-start | bytes 589832 | tf_op jit(solution)/shard_map/ppermute | solution.py:31
  20.6 0.5 collective-permute-start.8
  21.4 5.1 %forward.3 = (bf16[288,1024]{1,0:T(8,128)(2,1)S(1)}, f32[144,1024]{1,0:T(8,128)S(1)}, f32[144,1024]{1,0:T(8,128)S(1)}, bf16[4096,1024]{1,0:T(8,128)(2,1)S(1)}) custom-call(s32[1]{0:T(128)} %bitcast.core_ref, bf16[48,2048]{1,0:T(8,128)(2,1)S(1)} %maximum_select_fusion.after_ref.refs_0_, bf16[48,2048]{1,0:T(8,128)(2,1)S(1)} %collective-permute-done.1.refs_1_, ...), custom_call_target="tpu_custom_call" | custom-call | flops 3623878656 | bytes 17956864 | tf_op jit(solution)/shard_map/forward/pallas_call | solution.py:41
  26.6 1.4 %collective-permute-done.10.refs_0_.refs_5_ = bf16[48,2048]{1,0:T(8,128)(2,1)S(1)} collective-permute-done((bf16[48,2048]{1,0:T(8,128)(2,1)S(1)}, bf16[48,2048]{1,0:T(8,128)(2,1)S(1)}, u32[]{:S(2)}, u32[]{:S(2)}) %collective-permute-start.10) | collective-permute-done | bytes 196640 | tf_op jit(solution)/shard_map/ppermute | solution.py:31
  28.1 1.6 %collective-permute-start.15 = (bf16[48,1024]{1,0:T(8,128)(2,1)S(1)}, bf16[48,1024]{1,0:T(8,128)(2,1)S(1)}, u32[]{:S(2)}, u32[]{:S(2)}) collective-permute-start(bf16[48,1024]{1,0:T(8,128)(2,1)S(1)} %slice.37), channel_id=1, source_target_pairs={{4,0},{5,1},{8,4},{9,5},{12,8},{13,9},{14,12},{15,13},{10,14},{11,... | collective-permute-start | bytes 294920 | tf_op jit(solution)/shard_map/ppermute | solution.py:31
  29.7 0.5 collective-permute-start.14
  30.2 4.5 %forward.4 = (bf16[192,1024]{1,0:T(8,128)(2,1)S(1)}, f32[96,1024]{1,0:T(8,128)S(1)}, f32[96,1024]{1,0:T(8,128)S(1)}, bf16[1024,4096]{1,0:T(8,128)(2,1)S(1)}) custom-call(s32[1]{0:T(128)} %bitcast.core_ref, bf16[48,2048]{1,0:T(8,128)(2,1)S(1)} %collective-permute-done.6.refs_0_.refs_3_, bf16[48,2048]{1,0:T(8,128)(2,1)S(1)} %collective-permute-done.7.refs_1_.refs_4_, ...), custom_call_target="tpu_custom_call" | custom-call | flops 2415919104 | bytes 25952256 | tf_op jit(solution)/shard_map/forward/pallas_call | solution.py:41
  34.8 2.0 %forward_own.1 = (f32[144,1024]{1,0:T(8,128)S(1)}, f32[144,1024]{1,0:T(8,128)S(1)}, f32[144,1024]{1,0:T(8,128)S(1)}) custom-call(s32[1]{0:T(128)} %bitcast.core_ref, bf16[48,2048]{1,0:T(8,128)(2,1)S(1)} %collective-permute-done.10.refs_0_.refs_5_, bf16[48,2048]{1,0:T(8,128)(2,1)S(1)} %collective-permute-done.12.refs_1_.refs_6_, ...), custom_call_target="tpu_custom_call" | custom-call | flops 1811939328 | bytes 25755648 | tf_op jit(solution)/shard_map/forward_own/pallas_call | solution.py:41
  36.9 2.4 %forward.5 = (bf16[288,1024]{1,0:T(8,128)(2,1)S(1)}, f32[144,1024]{1,0:T(8,128)S(1)}, f32[144,1024]{1,0:T(8,128)S(1)}) custom-call(s32[1]{0:T(128)} %bitcast.core_ref, bf16[48,2048]{1,0:T(8,128)(2,1)S(1)} %collective-permute-done.11.refs_0_.refs_13_, bf16[48,2048]{1,0:T(8,128)(2,1)S(1)} %collective-permute-done.13.refs_1_.refs_14_, ...), custom_call_target="tpu_custom_call" | custom-call | flops 1811939328 | bytes 26640384 | tf_op jit(solution)/shard_map/forward/pallas_call | solution.py:41
  39.3 1.4 %down.4 = bf16[288,2048]{1,0:T(8,128)(2,1)S(1)} custom-call(s32[1]{0:T(128)} %bitcast.core_ref, bf16[288,1024]{1,0:T(8,128)(2,1)S(1)} %get-tuple-element.54.refs_0_, bf16[1024,4096]{1,0:T(8,128)(2,1)S(1)} %get-tuple-element.55.refs_1_.refs_2_.refs_10_.refs_3_.refs_4_), custom_call_target="tpu_custom_call" | custom-call | flops 1207959552 | bytes 8978432 | tf_op jit(solution)/shard_map/down/pallas_call | solution.py:41
  40.9 0.5 collective-permute-start.17
  41.9 1.4 %down.3.refs_0_ = bf16[288,2048]{1,0:T(8,128)(2,1)S(1)} custom-call(s32[1]{0:T(128)} %bitcast.core_ref, bf16[288,1024]{1,0:T(8,128)(2,1)S(1)} %get-tuple-element.54.refs_0_, bf16[1024,4096]{1,0:T(8,128)(2,1)S(1)} %get-tuple-element.55.refs_1_.refs_2_.refs_10_.refs_3_.refs_4_), custom_call_target="tpu_custom_call" | custom-call | flops 1207959552 | bytes 8978432 | tf_op jit(solution)/shard_map/down/pallas_call | solution.py:41
  43.4 0.9 collective-permute-start.21
  44.3 1.2 collective-permute-start.22
  45.5 4.2 %down.5 = (bf16[480,2048]{1,0:T(8,128)(2,1)S(1)}, bf16[480,2048]{1,0:T(8,128)(2,1)S(1)}) custom-call(s32[1]{0:T(128)} %bitcast.core_ref, bf16[288,1024]{1,0:T(8,128)(2,1)S(1)} %get-tuple-element.57.refs_0_, bf16[192,1024]{1,0:T(8,128)(2,1)S(1)} %get-tuple-element.58.refs_1_, bf16[1024,4096]{1,0:T(8,128)(2,1)S(1)} %get-tuple-element.55.refs_1_.refs_2_.refs_10_.refs_3_.refs_4_), custom_call_target="tpu_custom_call" | custom-call | flops 4026531840 | bytes 9371648 | tf_op jit(solution)/shard_map/down/pallas_call | solution.py:41
  51.0 1.4 %collective-permute-start.30 = (bf16[96,2048]{1,0:T(8,128)(2,1)S(1)}, bf16[96,2048]{1,0:T(8,128)(2,1)S(1)}, u32[]{:S(2)}, u32[]{:S(2)}) collective-permute-start(bf16[96,2048]{1,0:T(8,128)(2,1)S(1)} %merge.12), channel_id=1, source_target_pairs={{4,0},{5,1},{8,4},{9,5},{12,8},{13,9},{14,12},{15,13},{10,14},{11,... | collective-permute-start | bytes 1179656 | tf_op jit(solution)/shard_map/ppermute | solution.py:31
  52.6 0.7 collective-permute-start.23
  53.3 0.5 collective-permute-start.18
  53.8 8.3 %collective-permute-done.30.refs_2_ = bf16[96,2048]{1,0:T(8,128)(2,1)S(1)} collective-permute-done((bf16[96,2048]{1,0:T(8,128)(2,1)S(1)}, bf16[96,2048]{1,0:T(8,128)(2,1)S(1)}, u32[]{:S(2)}, u32[]{:S(2)}) %collective-permute-start.30) | collective-permute-done | bytes 393248 | tf_op jit(solution)/shard_map/ppermute | solution.py:31
  62.2 1.6 %collective-permute-start.31 = (bf16[96,2048]{1,0:T(8,128)(2,1)S(1)}, bf16[96,2048]{1,0:T(8,128)(2,1)S(1)}, u32[]{:S(2)}, u32[]{:S(2)}) collective-permute-start(bf16[96,2048]{1,0:T(8,128)(2,1)S(1)} %merge.13), channel_id=1, source_target_pairs={{4,0},{5,1},{8,4},{9,5},{12,8},{13,9},{14,12},{15,13},{10,14},{11,... | collective-permute-start | bytes 1179656 | tf_op jit(solution)/shard_map/ppermute | solution.py:31
  64.0 0.5 collective-permute-start.24
  64.5 7.9 %collective-permute-done.31.refs_2_ = bf16[96,2048]{1,0:T(8,128)(2,1)S(1)} collective-permute-done((bf16[96,2048]{1,0:T(8,128)(2,1)S(1)}, bf16[96,2048]{1,0:T(8,128)(2,1)S(1)}, u32[]{:S(2)}, u32[]{:S(2)}) %collective-permute-start.31) | collective-permute-done | bytes 393248 | tf_op jit(solution)/shard_map/ppermute | solution.py:31
  72.6 1.9 %collective-permute-start.32 = (bf16[96,2048]{1,0:T(8,128)(2,1)S(1)}, bf16[96,2048]{1,0:T(8,128)(2,1)S(1)}, u32[]{:S(2)}, u32[]{:S(2)}) collective-permute-start(bf16[96,2048]{1,0:T(8,128)(2,1)S(1)} %merge.14), channel_id=1, source_target_pairs={{4,0},{5,1},{8,4},{9,5},{12,8},{13,9},{14,12},{15,13},{10,14},{11,... | collective-permute-start | bytes 1179656 | tf_op jit(solution)/shard_map/ppermute | solution.py:31
  75.0 1.3 collective-permute-done.33
  76.3 0.9 turn.1.refs_0_
  77.2 4.7 %collective-permute-done.32.refs_3_ = bf16[96,2048]{1,0:T(8,128)(2,1)S(1)} collective-permute-done((bf16[96,2048]{1,0:T(8,128)(2,1)S(1)}, bf16[96,2048]{1,0:T(8,128)(2,1)S(1)}, u32[]{:S(2)}, u32[]{:S(2)}) %collective-permute-start.32) | collective-permute-done | bytes 393248 | tf_op jit(solution)/shard_map/ppermute | solution.py:31
  81.9 2.1 %collective-permute-done.26.refs_2_ = bf16[96,2048]{1,0:T(8,128)(2,1)S(1)} collective-permute-done((bf16[96,2048]{1,0:T(8,128)(2,1)S(1)}, bf16[96,2048]{1,0:T(8,128)(2,1)S(1)}, u32[]{:S(2)}, u32[]{:S(2)}) %collective-permute-start.26) | collective-permute-done | bytes 393248 | tf_op jit(solution)/shard_map/ppermute | solution.py:31
  84.5 1.7 %collective-permute-start.35 = (bf16[96,2048]{1,0:T(8,128)(2,1)S(1)}, bf16[96,2048]{1,0:T(8,128)(2,1)S(1)}, u32[]{:S(2)}, u32[]{:S(2)}) collective-permute-start(bf16[96,2048]{1,0:T(8,128)(2,1)S(1)} %merge.15.refs_0_), channel_id=1, source_target_pairs={{4,0},{5,1},{8,4},{9,5},{12,8},{13,9},{14,12},{15,13},{10,14},{11,... | collective-permute-start | bytes 1179656 | tf_op jit(solution)/shard_map/ppermute | solution.py:31
  86.3 7.3 %collective-permute-done.34.refs_1_ = bf16[96,2048]{1,0:T(8,128)(2,1)S(1)} collective-permute-done((bf16[96,2048]{1,0:T(8,128)(2,1)S(1)}, bf16[96,2048]{1,0:T(8,128)(2,1)S(1)}, u32[]{:S(2)}, u32[]{:S(2)}) %collective-permute-start.34) | collective-permute-done | bytes 393248 | tf_op jit(solution)/shard_map/ppermute | solution.py:31
  93.8 1.7 %collective-permute-start.37 = (bf16[96,2048]{1,0:T(8,128)(2,1)S(1)}, bf16[96,2048]{1,0:T(8,128)(2,1)S(1)}, u32[]{:S(2)}, u32[]{:S(2)}) collective-permute-start(bf16[96,2048]{1,0:T(8,128)(2,1)S(1)} %collective-permute-done.35.refs_2_), channel_id=1, source_target_pairs={{4,0},{5,1},{8,4},{9,5},{12,8},{13,9},{14,12},{15,13},{10,14},{11,... | collective-permute-start | bytes 1179656 | tf_op jit(solution)/shard_map/ppermute | solution.py:31
  95.6 0.5 collective-permute-start.39
  96.1 5.2 %collective-permute-done.36.refs_3_ = bf16[96,2048]{1,0:T(8,128)(2,1)S(1)} collective-permute-done((bf16[96,2048]{1,0:T(8,128)(2,1)S(1)}, bf16[96,2048]{1,0:T(8,128)(2,1)S(1)}, u32[]{:S(2)}, u32[]{:S(2)}) %collective-permute-start.36) | collective-permute-done | bytes 393248 | tf_op jit(solution)/shard_map/ppermute | solution.py:31
  102.1 1.7 %collective-permute-start.45 = (bf16[96,2048]{1,0:T(8,128)(2,1)S(1)}, bf16[96,2048]{1,0:T(8,128)(2,1)S(1)}, u32[]{:S(2)}, u32[]{:S(2)}) collective-permute-start(bf16[96,2048]{1,0:T(8,128)(2,1)S(1)} %collective-permute-done.37.refs_4_), channel_id=1, source_target_pairs={{4,0},{5,1},{8,4},{9,5},{12,8},{13,9},{14,12},{15,13},{10,14},{11,... | collective-permute-start | bytes 1179656 | tf_op jit(solution)/shard_map/ppermute | solution.py:31
  103.9 4.3 %back.2.refs_1_ = bf16[240,1024]{1,0:T(8,128)(2,1)S(1)} custom-call(s32[1]{0:T(128)} %bitcast.core_ref, bf16[96,2048]{1,0:T(8,128)(2,1)S(1)} %merge.15.refs_0_, bf16[96,2048]{1,0:T(8,128)(2,1)S(1)} %collective-permute-done.34.refs_1_, bf16[96,2048]{1,0:T(8,128)(2,1)S(1)} %collective-permute-done.35.refs_2_, ...), custom_call_target="tpu_custom_call" | custom-call | flops 4026531840 | bytes 13303808 | tf_op jit(solution)/shard_map/back/pallas_call | solution.py:41
  108.1 5.0 %collective-permute-done.43.refs_0_ = bf16[96,2048]{1,0:T(8,128)(2,1)S(1)} collective-permute-done((bf16[96,2048]{1,0:T(8,128)(2,1)S(1)}, bf16[96,2048]{1,0:T(8,128)(2,1)S(1)}, u32[]{:S(2)}, u32[]{:S(2)}) %collective-permute-start.43) | collective-permute-done | bytes 393248 | tf_op jit(solution)/shard_map/ppermute | solution.py:31
  113.5 2.1 %collective-permute-start.48 = (bf16[96,1024]{1,0:T(8,128)(2,1)S(1)}, bf16[96,1024]{1,0:T(8,128)(2,1)S(1)}, u32[]{:S(2)}, u32[]{:S(2)}) collective-permute-start(bf16[96,1024]{1,0:T(8,128)(2,1)S(1)} %slice.47), channel_id=1, source_target_pairs={{4,0},{5,1},{8,4},{9,5},{12,8},{13,9},{14,12},{15,13},{10,14},{11,... | collective-permute-start | bytes 589832 | tf_op jit(solution)/shard_map/ppermute | solution.py:31
  115.6 0.5 collective-permute-start.44
  116.1 3.6 %collective-permute-done.47 = bf16[96,1024]{1,0:T(8,128)(2,1)S(1)} collective-permute-done((bf16[96,1024]{1,0:T(8,128)(2,1)S(1)}, bf16[96,1024]{1,0:T(8,128)(2,1)S(1)}, u32[]{:S(2)}, u32[]{:S(2)}) %collective-permute-start.47) | collective-permute-done | bytes 196640 | tf_op jit(solution)/shard_map/ppermute | solution.py:31
  119.9 1.4 %back_own.1.refs_3_ = f32[288,1024]{1,0:T(8,128)S(1)} custom-call(s32[1]{0:T(128)} %bitcast.core_ref, bf16[96,2048]{1,0:T(8,128)(2,1)S(1)} %collective-permute-done.43.refs_0_, bf16[96,2048]{1,0:T(8,128)(2,1)S(1)} %collective-permute-done.45.refs_1_, bf16[96,2048]{1,0:T(8,128)(2,1)S(1)} %constant_dynamic-update-slice_fusion.2.refs_2_, ...), custom_call_target="tpu_custom_call" | custom-call | flops 1207959552 | bytes 9568256 | tf_op jit(solution)/shard_map/back_own/pallas_call | solution.py:41
  121.6 1.4 %back.3.refs_2_ = bf16[144,1024]{1,0:T(8,128)(2,1)S(1)} custom-call(s32[1]{0:T(128)} %bitcast.core_ref, bf16[96,2048]{1,0:T(8,128)(2,1)S(1)} %collective-permute-done.44.refs_0_, bf16[96,2048]{1,0:T(8,128)(2,1)S(1)} %collective-permute-done.46.refs_1_, bf16[96,2048]{1,0:T(8,128)(2,1)S(1)} %collective-permute-done.49.refs_2_, ...), custom_call_target="tpu_custom_call" | custom-call | flops 1207959552 | bytes 10747904 | tf_op jit(solution)/shard_map/back/pallas_call | solution.py:41
  123.1 5.6 %outer.1 = bf16[4096,1024]{1,0:T(8,128)(2,1)} custom-call(s32[1]{0:T(128)} %bitcast.core_ref, bf16[4096,384]{1,0:T(8,128)(2,1)S(1)} %turn.1.refs_0_, bf16[240,1024]{1,0:T(8,128)(2,1)S(1)} %back.2.refs_1_, bf16[144,1024]{1,0:T(8,128)(2,1)S(1)} %back.3.refs_2_), custom_call_target="tpu_custom_call" | custom-call | flops 3221225472 | bytes 8388608 | tf_op jit(solution)/shard_map/outer/pallas_call | solution.py:378
  (89 shorter events, 7.0 us)
Async XLA Ops:
  2.5 8.8 %collective-permute-start.2 = (bf16[48,2048]{1,0:T(8,128)(2,1)S(1)}, bf16[48,2048]{1,0:T(8,128)(2,1)S(1)}, u32[]{:S(2)}, u32[]{:S(2)}) collective-permute-start(bf16[48,2048]{1,0:T(8,128)(2,1)S(1)} %maximum_select_fusion.after_ref.refs_0_), channel_id=1, source_target_pairs={{4,0},{5,1},{8,4},{9,5},{12,8},{13,9},{14,12},{15,13},{10,14},{11,... | collective-permute-start | bytes 589832 | tf_op jit(solution)/shard_map/ppermute | solution.py:31
  5.4 7.9 %collective-permute-start.1 = (bf16[48,2048]{1,0:T(8,128)(2,1)S(1)}, bf16[48,2048]{1,0:T(8,128)(2,1)S(1)}, u32[]{:S(2)}, u32[]{:S(2)}) collective-permute-start(bf16[48,2048]{1,0:T(8,128)(2,1)S(1)} %maximum_select_fusion.after_ref.refs_0_), channel_id=1, source_target_pairs={{0,4},{1,5},{4,8},{5,9},{8,12},{9,13},{12,14},{13,15},{14,10},{15,... | collective-permute-start | bytes 589832 | tf_op jit(solution)/shard_map/ppermute | solution.py:31
  5.5 15.1 %collective-permute-start.3 = (bf16[48,2048]{1,0:T(8,128)(2,1)S(1)}, bf16[48,2048]{1,0:T(8,128)(2,1)S(1)}, u32[]{:S(2)}, u32[]{:S(2)}) collective-permute-start(bf16[48,2048]{1,0:T(8,128)(2,1)S(1)} %maximum_select_fusion.after_ref.refs_0_), channel_id=1, source_target_pairs={{0,1},{1,0},{2,3},{3,2},{4,5},{5,4},{6,7},{7,6},{8,9},{9,8},{10,11... | collective-permute-start | bytes 589832 | tf_op jit(solution)/shard_map/ppermute | solution.py:31
  11.3 7.6 %collective-permute-start.7 = (bf16[48,2048]{1,0:T(8,128)(2,1)S(1)}, bf16[48,2048]{1,0:T(8,128)(2,1)S(1)}, u32[]{:S(2)}, u32[]{:S(2)}) collective-permute-start(bf16[48,2048]{1,0:T(8,128)(2,1)S(1)} %collective-permute-done.2.refs_2_), channel_id=1, source_target_pairs={{4,0},{5,1},{8,4},{9,5},{12,8},{13,9},{14,12},{15,13},{10,14},{11,... | collective-permute-start | bytes 589832 | tf_op jit(solution)/shard_map/ppermute | solution.py:31
  13.3 7.3 %collective-permute-start.6 = (bf16[48,2048]{1,0:T(8,128)(2,1)S(1)}, bf16[48,2048]{1,0:T(8,128)(2,1)S(1)}, u32[]{:S(2)}, u32[]{:S(2)}) collective-permute-start(bf16[48,2048]{1,0:T(8,128)(2,1)S(1)} %collective-permute-done.1.refs_1_), channel_id=1, source_target_pairs={{0,4},{1,5},{4,8},{5,9},{8,12},{9,13},{12,14},{13,15},{14,10},{15,... | collective-permute-start | bytes 589832 | tf_op jit(solution)/shard_map/ppermute | solution.py:31
  13.4 7.7 %collective-permute-start.5 = (bf16[48,2048]{1,0:T(8,128)(2,1)S(1)}, bf16[48,2048]{1,0:T(8,128)(2,1)S(1)}, u32[]{:S(2)}, u32[]{:S(2)}) collective-permute-start(bf16[48,2048]{1,0:T(8,128)(2,1)S(1)} %collective-permute-done.2.refs_2_), channel_id=1, source_target_pairs={{0,1},{1,0},{2,3},{3,2},{4,5},{5,4},{6,7},{7,6},{8,9},{9,8},{10,11... | collective-permute-start | bytes 589832 | tf_op jit(solution)/shard_map/ppermute | solution.py:31
  13.6 7.8 %collective-permute-start.4 = (bf16[48,2048]{1,0:T(8,128)(2,1)S(1)}, bf16[48,2048]{1,0:T(8,128)(2,1)S(1)}, u32[]{:S(2)}, u32[]{:S(2)}) collective-permute-start(bf16[48,2048]{1,0:T(8,128)(2,1)S(1)} %collective-permute-done.1.refs_1_), channel_id=1, source_target_pairs={{0,1},{1,0},{2,3},{3,2},{4,5},{5,4},{6,7},{7,6},{8,9},{9,8},{10,11... | collective-permute-start | bytes 589832 | tf_op jit(solution)/shard_map/ppermute | solution.py:31
  18.9 7.6 %collective-permute-start.12 = (bf16[48,2048]{1,0:T(8,128)(2,1)S(1)}, bf16[48,2048]{1,0:T(8,128)(2,1)S(1)}, u32[]{:S(2)}, u32[]{:S(2)}) collective-permute-start(bf16[48,2048]{1,0:T(8,128)(2,1)S(1)} %collective-permute-done.7.refs_1_.refs_4_), channel_id=1, source_target_pairs={{4,0},{5,1},{8,4},{9,5},{12,8},{13,9},{14,12},{15,13},{10,14},{11,... | collective-permute-start | bytes 589832 | tf_op jit(solution)/shard_map/ppermute | solution.py:31
  20.6 9.1 %collective-permute-start.9 = (bf16[48,2048]{1,0:T(8,128)(2,1)S(1)}, bf16[48,2048]{1,0:T(8,128)(2,1)S(1)}, u32[]{:S(2)}, u32[]{:S(2)}) collective-permute-start(bf16[48,2048]{1,0:T(8,128)(2,1)S(1)} %collective-permute-done.7.refs_1_.refs_4_), channel_id=1, source_target_pairs={{0,1},{1,0},{2,3},{3,2},{4,5},{5,4},{6,7},{7,6},{8,9},{9,8},{10,11... | collective-permute-start | bytes 589832 | tf_op jit(solution)/shard_map/ppermute | solution.py:31
  20.6 9.6 %collective-permute-start.8 = (bf16[48,2048]{1,0:T(8,128)(2,1)S(1)}, bf16[48,2048]{1,0:T(8,128)(2,1)S(1)}, u32[]{:S(2)}, u32[]{:S(2)}) collective-permute-start(bf16[48,2048]{1,0:T(8,128)(2,1)S(1)} %collective-permute-done.6.refs_0_.refs_3_), channel_id=1, source_target_pairs={{0,1},{1,0},{2,3},{3,2},{4,5},{5,4},{6,7},{7,6},{8,9},{9,8},{10,11... | collective-permute-start | bytes 589832 | tf_op jit(solution)/shard_map/ppermute | solution.py:31
  21.1 6.9 %collective-permute-start.10 = (bf16[48,2048]{1,0:T(8,128)(2,1)S(1)}, bf16[48,2048]{1,0:T(8,128)(2,1)S(1)}, u32[]{:S(2)}, u32[]{:S(2)}) collective-permute-start(bf16[48,2048]{1,0:T(8,128)(2,1)S(1)} %collective-permute-done.6.refs_0_.refs_3_), channel_id=1, source_target_pairs={{0,4},{1,5},{4,8},{5,9},{8,12},{9,13},{12,14},{13,15},{14,10},{15,... | collective-permute-start | bytes 589832 | tf_op jit(solution)/shard_map/ppermute | solution.py:31
  26.5 10.3 %collective-permute-start.13 = (bf16[48,2048]{1,0:T(8,128)(2,1)S(1)}, bf16[48,2048]{1,0:T(8,128)(2,1)S(1)}, u32[]{:S(2)}, u32[]{:S(2)}) collective-permute-start(bf16[48,2048]{1,0:T(8,128)(2,1)S(1)} %collective-permute-done.12.refs_1_.refs_6_), channel_id=1, source_target_pairs={{0,1},{1,0},{2,3},{3,2},{4,5},{5,4},{6,7},{7,6},{8,9},{9,8},{10,11... | collective-permute-start | bytes 589832 | tf_op jit(solution)/shard_map/ppermute | solution.py:31
  28.0 8.9 %collective-permute-start.11 = (bf16[48,2048]{1,0:T(8,128)(2,1)S(1)}, bf16[48,2048]{1,0:T(8,128)(2,1)S(1)}, u32[]{:S(2)}, u32[]{:S(2)}) collective-permute-start(bf16[48,2048]{1,0:T(8,128)(2,1)S(1)} %collective-permute-done.10.refs_0_.refs_5_), channel_id=1, source_target_pairs={{0,1},{1,0},{2,3},{3,2},{4,5},{5,4},{6,7},{7,6},{8,9},{9,8},{10,11... | collective-permute-start | bytes 589832 | tf_op jit(solution)/shard_map/ppermute | solution.py:31
  28.1 6.6 %collective-permute-start.15 = (bf16[48,1024]{1,0:T(8,128)(2,1)S(1)}, bf16[48,1024]{1,0:T(8,128)(2,1)S(1)}, u32[]{:S(2)}, u32[]{:S(2)}) collective-permute-start(bf16[48,1024]{1,0:T(8,128)(2,1)S(1)} %slice.37), channel_id=1, source_target_pairs={{4,0},{5,1},{8,4},{9,5},{12,8},{13,9},{14,12},{15,13},{10,14},{11,... | collective-permute-start | bytes 294920 | tf_op jit(solution)/shard_map/ppermute | solution.py:31
  29.7 5.0 %collective-permute-start.14 = (bf16[48,1024]{1,0:T(8,128)(2,1)S(1)}, bf16[48,1024]{1,0:T(8,128)(2,1)S(1)}, u32[]{:S(2)}, u32[]{:S(2)}) collective-permute-start(bf16[48,1024]{1,0:T(8,128)(2,1)S(1)} %slice.36), channel_id=1, source_target_pairs={{0,4},{1,5},{4,8},{5,9},{8,12},{9,13},{12,14},{13,15},{14,10},{15,... | collective-permute-start | bytes 294920 | tf_op jit(solution)/shard_map/ppermute | solution.py:31
  34.7 2.2 %collective-permute-start.16 = (bf16[48,2048]{1,0:T(8,128)(2,1)S(1)}, bf16[48,2048]{1,0:T(8,128)(2,1)S(1)}, u32[]{:S(2)}, u32[]{:S(2)}) collective-permute-start(bf16[48,2048]{1,0:T(8,128)(2,1)S(1)} %constant_dynamic-update-slice_fusion.refs_2_.refs_7_), channel_id=1, source_target_pairs={{0,1},{1,0},{2,3},{3,2},{4,5},{5,4},{6,7},{7,6},{8,9},{9,8},{10,11... | collective-permute-start | bytes 589832 | tf_op jit(solution)/shard_map/ppermute | solution.py:31
  40.9 2.5 %collective-permute-start.17 = (bf16[96,2048]{1,0:T(8,128)(2,1)S(1)}, bf16[96,2048]{1,0:T(8,128)(2,1)S(1)}, u32[]{:S(2)}, u32[]{:S(2)}) collective-permute-start(bf16[96,2048]{1,0:T(8,128)(2,1)S(1)} %get-tuple-element.82), channel_id=1, source_target_pairs={{0,1},{1,0},{2,3},{3,2},{4,5},{5,4},{6,7},{7,6},{8,9},{9,8},{10,11... | collective-permute-start | bytes 1179656 | tf_op jit(solution)/shard_map/ppermute | solution.py:31
  41.4 9.5 %collective-permute-start.29 = (bf16[96,2048]{1,0:T(8,128)(2,1)S(1)}, bf16[96,2048]{1,0:T(8,128)(2,1)S(1)}, u32[]{:S(2)}, u32[]{:S(2)}) collective-permute-start(bf16[96,2048]{1,0:T(8,128)(2,1)S(1)} %get-tuple-element.80), channel_id=1, source_target_pairs={{0,1},{1,0},{2,3},{3,2},{4,5},{5,4},{6,7},{7,6},{8,9},{9,8},{10,11... | collective-permute-start | bytes 1179656 | tf_op jit(solution)/shard_map/ppermute | solution.py:31
  41.5 10.9 %collective-permute-start.20 = (bf16[96,2048]{1,0:T(8,128)(2,1)S(1)}, bf16[96,2048]{1,0:T(8,128)(2,1)S(1)}, u32[]{:S(2)}, u32[]{:S(2)}) collective-permute-start(bf16[96,2048]{1,0:T(8,128)(2,1)S(1)} %get-tuple-element.81), channel_id=1, source_target_pairs={{0,1},{1,0},{2,3},{3,2},{4,5},{5,4},{6,7},{7,6},{8,9},{9,8},{10,11... | collective-permute-start | bytes 1179656 | tf_op jit(solution)/shard_map/ppermute | solution.py:31
  43.4 6.9 %collective-permute-start.21 = (bf16[96,1024]{1,0:T(8,128)(2,1)S(1)}, bf16[96,1024]{1,0:T(8,128)(2,1)S(1)}, u32[]{:S(2)}, u32[]{:S(2)}) collective-permute-start(bf16[96,1024]{1,0:T(8,128)(2,1)S(1)} %get-tuple-element.56), channel_id=1, source_target_pairs={{0,4},{1,5},{4,8},{5,9},{8,12},{9,13},{12,14},{13,15},{14,10},{15,... | collective-permute-start | bytes 589832 | tf_op jit(solution)/shard_map/ppermute | solution.py:31
  44.3 6.6 %collective-permute-start.22 = (bf16[96,1024]{1,0:T(8,128)(2,1)S(1)}, bf16[96,1024]{1,0:T(8,128)(2,1)S(1)}, u32[]{:S(2)}, u32[]{:S(2)}) collective-permute-start(bf16[96,1024]{1,0:T(8,128)(2,1)S(1)} %get-tuple-element.61), channel_id=1, source_target_pairs={{4,0},{5,1},{8,4},{9,5},{12,8},{13,9},{14,12},{15,13},{10,14},{11,... | collective-permute-start | bytes 589832 | tf_op jit(solution)/shard_map/ppermute | solution.py:31
  49.9 3.4 %collective-permute-start.28 = (bf16[96,2048]{1,0:T(8,128)(2,1)S(1)}, bf16[96,2048]{1,0:T(8,128)(2,1)S(1)}, u32[]{:S(2)}, u32[]{:S(2)}) collective-permute-start(bf16[96,2048]{1,0:T(8,128)(2,1)S(1)} %get-tuple-element.75), channel_id=1, source_target_pairs={{0,1},{1,0},{2,3},{3,2},{4,5},{5,4},{6,7},{7,6},{8,9},{9,8},{10,11... | collective-permute-start | bytes 1179656 | tf_op jit(solution)/shard_map/ppermute | solution.py:31
  50.4 13.5 %collective-permute-start.19 = (bf16[96,2048]{1,0:T(8,128)(2,1)S(1)}, bf16[96,2048]{1,0:T(8,128)(2,1)S(1)}, u32[]{:S(2)}, u32[]{:S(2)}) collective-permute-start(bf16[96,2048]{1,0:T(8,128)(2,1)S(1)} %get-tuple-element.78), channel_id=1, source_target_pairs={{0,1},{1,0},{2,3},{3,2},{4,5},{5,4},{6,7},{7,6},{8,9},{9,8},{10,11... | collective-permute-start | bytes 1179656 | tf_op jit(solution)/shard_map/ppermute | solution.py:31
  51.0 11.1 %collective-permute-start.30 = (bf16[96,2048]{1,0:T(8,128)(2,1)S(1)}, bf16[96,2048]{1,0:T(8,128)(2,1)S(1)}, u32[]{:S(2)}, u32[]{:S(2)}) collective-permute-start(bf16[96,2048]{1,0:T(8,128)(2,1)S(1)} %merge.12), channel_id=1, source_target_pairs={{4,0},{5,1},{8,4},{9,5},{12,8},{13,9},{14,12},{15,13},{10,14},{11,... | collective-permute-start | bytes 1179656 | tf_op jit(solution)/shard_map/ppermute | solution.py:31
  52.6 11.3 %collective-permute-start.23 = (bf16[96,2048]{1,0:T(8,128)(2,1)S(1)}, bf16[96,2048]{1,0:T(8,128)(2,1)S(1)}, u32[]{:S(2)}, u32[]{:S(2)}) collective-permute-start(bf16[96,2048]{1,0:T(8,128)(2,1)S(1)} %merge.9), channel_id=1, source_target_pairs={{0,4},{1,5},{4,8},{5,9},{8,12},{9,13},{12,14},{13,15},{14,10},{15,... | collective-permute-start | bytes 1179656 | tf_op jit(solution)/shard_map/ppermute | solution.py:31
  53.3 11.2 %collective-permute-start.27 = (bf16[96,2048]{1,0:T(8,128)(2,1)S(1)}, bf16[96,2048]{1,0:T(8,128)(2,1)S(1)}, u32[]{:S(2)}, u32[]{:S(2)}) collective-permute-start(bf16[96,2048]{1,0:T(8,128)(2,1)S(1)} %get-tuple-element.76), channel_id=1, source_target_pairs={{0,1},{1,0},{2,3},{3,2},{4,5},{5,4},{6,7},{7,6},{8,9},{9,8},{10,11... | collective-permute-start | bytes 1179656 | tf_op jit(solution)/shard_map/ppermute | solution.py:31
  53.3 21.2 %collective-permute-start.18 = (bf16[96,2048]{1,0:T(8,128)(2,1)S(1)}, bf16[96,2048]{1,0:T(8,128)(2,1)S(1)}, u32[]{:S(2)}, u32[]{:S(2)}) collective-permute-start(bf16[96,2048]{1,0:T(8,128)(2,1)S(1)} %get-tuple-element.79), channel_id=1, source_target_pairs={{0,1},{1,0},{2,3},{3,2},{4,5},{5,4},{6,7},{7,6},{8,9},{9,8},{10,11... | collective-permute-start | bytes 1179656 | tf_op jit(solution)/shard_map/ppermute | solution.py:31
  62.2 10.2 %collective-permute-start.31 = (bf16[96,2048]{1,0:T(8,128)(2,1)S(1)}, bf16[96,2048]{1,0:T(8,128)(2,1)S(1)}, u32[]{:S(2)}, u32[]{:S(2)}) collective-permute-start(bf16[96,2048]{1,0:T(8,128)(2,1)S(1)} %merge.13), channel_id=1, source_target_pairs={{4,0},{5,1},{8,4},{9,5},{12,8},{13,9},{14,12},{15,13},{10,14},{11,... | collective-permute-start | bytes 1179656 | tf_op jit(solution)/shard_map/ppermute | solution.py:31
  64.0 10.5 %collective-permute-start.24 = (bf16[96,2048]{1,0:T(8,128)(2,1)S(1)}, bf16[96,2048]{1,0:T(8,128)(2,1)S(1)}, u32[]{:S(2)}, u32[]{:S(2)}) collective-permute-start(bf16[96,2048]{1,0:T(8,128)(2,1)S(1)} %merge.10), channel_id=1, source_target_pairs={{0,4},{1,5},{4,8},{5,9},{8,12},{9,13},{12,14},{13,15},{14,10},{15,... | collective-permute-start | bytes 1179656 | tf_op jit(solution)/shard_map/ppermute | solution.py:31
  64.5 19.4 %collective-permute-start.25 = (bf16[96,2048]{1,0:T(8,128)(2,1)S(1)}, bf16[96,2048]{1,0:T(8,128)(2,1)S(1)}, u32[]{:S(2)}, u32[]{:S(2)}) collective-permute-start(bf16[96,2048]{1,0:T(8,128)(2,1)S(1)} %get-tuple-element.77), channel_id=1, source_target_pairs={{0,1},{1,0},{2,3},{3,2},{4,5},{5,4},{6,7},{7,6},{8,9},{9,8},{10,11... | collective-permute-start | bytes 1179656 | tf_op jit(solution)/shard_map/ppermute | solution.py:31
  72.6 9.3 %collective-permute-start.32 = (bf16[96,2048]{1,0:T(8,128)(2,1)S(1)}, bf16[96,2048]{1,0:T(8,128)(2,1)S(1)}, u32[]{:S(2)}, u32[]{:S(2)}) collective-permute-start(bf16[96,2048]{1,0:T(8,128)(2,1)S(1)} %merge.14), channel_id=1, source_target_pairs={{4,0},{5,1},{8,4},{9,5},{12,8},{13,9},{14,12},{15,13},{10,14},{11,... | collective-permute-start | bytes 1179656 | tf_op jit(solution)/shard_map/ppermute | solution.py:31
  74.7 9.3 %collective-permute-start.26 = (bf16[96,2048]{1,0:T(8,128)(2,1)S(1)}, bf16[96,2048]{1,0:T(8,128)(2,1)S(1)}, u32[]{:S(2)}, u32[]{:S(2)}) collective-permute-start(bf16[96,2048]{1,0:T(8,128)(2,1)S(1)} %merge.11), channel_id=1, source_target_pairs={{0,4},{1,5},{4,8},{5,9},{8,12},{9,13},{12,14},{13,15},{14,10},{15,... | collective-permute-start | bytes 1179656 | tf_op jit(solution)/shard_map/ppermute | solution.py:31
  84.2 9.3 %collective-permute-start.34 = (bf16[96,2048]{1,0:T(8,128)(2,1)S(1)}, bf16[96,2048]{1,0:T(8,128)(2,1)S(1)}, u32[]{:S(2)}, u32[]{:S(2)}) collective-permute-start(bf16[96,2048]{1,0:T(8,128)(2,1)S(1)} %merge.15.refs_0_), channel_id=1, source_target_pairs={{0,4},{1,5},{4,8},{5,9},{8,12},{9,13},{12,14},{13,15},{14,10},{15,... | collective-permute-start | bytes 1179656 | tf_op jit(solution)/shard_map/ppermute | solution.py:31
  84.5 9.3 %collective-permute-start.35 = (bf16[96,2048]{1,0:T(8,128)(2,1)S(1)}, bf16[96,2048]{1,0:T(8,128)(2,1)S(1)}, u32[]{:S(2)}, u32[]{:S(2)}) collective-permute-start(bf16[96,2048]{1,0:T(8,128)(2,1)S(1)} %merge.15.refs_0_), channel_id=1, source_target_pairs={{4,0},{5,1},{8,4},{9,5},{12,8},{13,9},{14,12},{15,13},{10,14},{11,... | collective-permute-start | bytes 1179656 | tf_op jit(solution)/shard_map/ppermute | solution.py:31
  93.5 7.8 %collective-permute-start.36 = (bf16[96,2048]{1,0:T(8,128)(2,1)S(1)}, bf16[96,2048]{1,0:T(8,128)(2,1)S(1)}, u32[]{:S(2)}, u32[]{:S(2)}) collective-permute-start(bf16[96,2048]{1,0:T(8,128)(2,1)S(1)} %collective-permute-done.34.refs_1_), channel_id=1, source_target_pairs={{0,4},{1,5},{4,8},{5,9},{8,12},{9,13},{12,14},{13,15},{14,10},{15,... | collective-permute-start | bytes 1179656 | tf_op jit(solution)/shard_map/ppermute | solution.py:31
  93.8 7.8 %collective-permute-start.37 = (bf16[96,2048]{1,0:T(8,128)(2,1)S(1)}, bf16[96,2048]{1,0:T(8,128)(2,1)S(1)}, u32[]{:S(2)}, u32[]{:S(2)}) collective-permute-start(bf16[96,2048]{1,0:T(8,128)(2,1)S(1)} %collective-permute-done.35.refs_2_), channel_id=1, source_target_pairs={{4,0},{5,1},{8,4},{9,5},{12,8},{13,9},{14,12},{15,13},{10,14},{11,... | collective-permute-start | bytes 1179656 | tf_op jit(solution)/shard_map/ppermute | solution.py:31
  95.6 6.3 %collective-permute-start.38 = (bf16[96,2048]{1,0:T(8,128)(2,1)S(1)}, bf16[96,2048]{1,0:T(8,128)(2,1)S(1)}, u32[]{:S(2)}, u32[]{:S(2)}) collective-permute-start(bf16[96,2048]{1,0:T(8,128)(2,1)S(1)} %merge.15.refs_0_), channel_id=1, source_target_pairs={{0,1},{1,0},{2,3},{3,2},{4,5},{5,4},{6,7},{7,6},{8,9},{9,8},{10,11... | collective-permute-start | bytes 1179656 | tf_op jit(solution)/shard_map/ppermute | solution.py:31
  95.6 6.6 %collective-permute-start.39 = (bf16[96,2048]{1,0:T(8,128)(2,1)S(1)}, bf16[96,2048]{1,0:T(8,128)(2,1)S(1)}, u32[]{:S(2)}, u32[]{:S(2)}) collective-permute-start(bf16[96,2048]{1,0:T(8,128)(2,1)S(1)} %collective-permute-done.34.refs_1_), channel_id=1, source_target_pairs={{0,1},{1,0},{2,3},{3,2},{4,5},{5,4},{6,7},{7,6},{8,9},{9,8},{10,11... | collective-permute-start | bytes 1179656 | tf_op jit(solution)/shard_map/ppermute | solution.py:31
  96.1 7.8 %collective-permute-start.40 = (bf16[96,2048]{1,0:T(8,128)(2,1)S(1)}, bf16[96,2048]{1,0:T(8,128)(2,1)S(1)}, u32[]{:S(2)}, u32[]{:S(2)}) collective-permute-start(bf16[96,2048]{1,0:T(8,128)(2,1)S(1)} %collective-permute-done.35.refs_2_), channel_id=1, source_target_pairs={{0,1},{1,0},{2,3},{3,2},{4,5},{5,4},{6,7},{7,6},{8,9},{9,8},{10,11... | collective-permute-start | bytes 1179656 | tf_op jit(solution)/shard_map/ppermute | solution.py:31
  101.3 2.6 %collective-permute-start.41 = (bf16[96,2048]{1,0:T(8,128)(2,1)S(1)}, bf16[96,2048]{1,0:T(8,128)(2,1)S(1)}, u32[]{:S(2)}, u32[]{:S(2)}) collective-permute-start(bf16[96,2048]{1,0:T(8,128)(2,1)S(1)} %collective-permute-done.36.refs_3_), channel_id=1, source_target_pairs={{0,1},{1,0},{2,3},{3,2},{4,5},{5,4},{6,7},{7,6},{8,9},{9,8},{10,11... | collective-permute-start | bytes 1179656 | tf_op jit(solution)/shard_map/ppermute | solution.py:31
  101.6 2.3 %collective-permute-start.42 = (bf16[96,2048]{1,0:T(8,128)(2,1)S(1)}, bf16[96,2048]{1,0:T(8,128)(2,1)S(1)}, u32[]{:S(2)}, u32[]{:S(2)}) collective-permute-start(bf16[96,2048]{1,0:T(8,128)(2,1)S(1)} %collective-permute-done.37.refs_4_), channel_id=1, source_target_pairs={{0,1},{1,0},{2,3},{3,2},{4,5},{5,4},{6,7},{7,6},{8,9},{9,8},{10,11... | collective-permute-start | bytes 1179656 | tf_op jit(solution)/shard_map/ppermute | solution.py:31
  101.8 11.3 %collective-permute-start.43 = (bf16[96,2048]{1,0:T(8,128)(2,1)S(1)}, bf16[96,2048]{1,0:T(8,128)(2,1)S(1)}, u32[]{:S(2)}, u32[]{:S(2)}) collective-permute-start(bf16[96,2048]{1,0:T(8,128)(2,1)S(1)} %collective-permute-done.36.refs_3_), channel_id=1, source_target_pairs={{0,4},{1,5},{4,8},{5,9},{8,12},{9,13},{12,14},{13,15},{14,10},{15,... | collective-permute-start | bytes 1179656 | tf_op jit(solution)/shard_map/ppermute | solution.py:31
  102.1 11.4 %collective-permute-start.45 = (bf16[96,2048]{1,0:T(8,128)(2,1)S(1)}, bf16[96,2048]{1,0:T(8,128)(2,1)S(1)}, u32[]{:S(2)}, u32[]{:S(2)}) collective-permute-start(bf16[96,2048]{1,0:T(8,128)(2,1)S(1)} %collective-permute-done.37.refs_4_), channel_id=1, source_target_pairs={{4,0},{5,1},{8,4},{9,5},{12,8},{13,9},{14,12},{15,13},{10,14},{11,... | collective-permute-start | bytes 1179656 | tf_op jit(solution)/shard_map/ppermute | solution.py:31
  113.1 6.5 %collective-permute-start.47 = (bf16[96,1024]{1,0:T(8,128)(2,1)S(1)}, bf16[96,1024]{1,0:T(8,128)(2,1)S(1)}, u32[]{:S(2)}, u32[]{:S(2)}) collective-permute-start(bf16[96,1024]{1,0:T(8,128)(2,1)S(1)} %slice.46), channel_id=1, source_target_pairs={{0,4},{1,5},{4,8},{5,9},{8,12},{9,13},{12,14},{13,15},{14,10},{15,... | collective-permute-start | bytes 589832 | tf_op jit(solution)/shard_map/ppermute | solution.py:31
  113.5 6.3 %collective-permute-start.48 = (bf16[96,1024]{1,0:T(8,128)(2,1)S(1)}, bf16[96,1024]{1,0:T(8,128)(2,1)S(1)}, u32[]{:S(2)}, u32[]{:S(2)}) collective-permute-start(bf16[96,1024]{1,0:T(8,128)(2,1)S(1)} %slice.47), channel_id=1, source_target_pairs={{4,0},{5,1},{8,4},{9,5},{12,8},{13,9},{14,12},{15,13},{10,14},{11,... | collective-permute-start | bytes 589832 | tf_op jit(solution)/shard_map/ppermute | solution.py:31
  115.6 5.8 %collective-permute-start.46 = (bf16[96,2048]{1,0:T(8,128)(2,1)S(1)}, bf16[96,2048]{1,0:T(8,128)(2,1)S(1)}, u32[]{:S(2)}, u32[]{:S(2)}) collective-permute-start(bf16[96,2048]{1,0:T(8,128)(2,1)S(1)} %collective-permute-done.45.refs_1_), channel_id=1, source_target_pairs={{0,1},{1,0},{2,3},{3,2},{4,5},{5,4},{6,7},{7,6},{8,9},{9,8},{10,11... | collective-permute-start | bytes 1179656 | tf_op jit(solution)/shard_map/ppermute | solution.py:31
  115.6 5.8 %collective-permute-start.44 = (bf16[96,2048]{1,0:T(8,128)(2,1)S(1)}, bf16[96,2048]{1,0:T(8,128)(2,1)S(1)}, u32[]{:S(2)}, u32[]{:S(2)}) collective-permute-start(bf16[96,2048]{1,0:T(8,128)(2,1)S(1)} %collective-permute-done.43.refs_0_), channel_id=1, source_target_pairs={{0,1},{1,0},{2,3},{3,2},{4,5},{5,4},{6,7},{7,6},{8,9},{9,8},{10,11... | collective-permute-start | bytes 1179656 | tf_op jit(solution)/shard_map/ppermute | solution.py:31
  119.9 1.8 %collective-permute-start.49 = (bf16[96,2048]{1,0:T(8,128)(2,1)S(1)}, bf16[96,2048]{1,0:T(8,128)(2,1)S(1)}, u32[]{:S(2)}, u32[]{:S(2)}) collective-permute-start(bf16[96,2048]{1,0:T(8,128)(2,1)S(1)} %constant_dynamic-update-slice_fusion.2.refs_2_), channel_id=1, source_target_pairs={{0,1},{1,0},{2,3},{3,2},{4,5},{5,4},{6,7},{7,6},{8,9},{9,8},{10,11... | collective-permute-start | bytes 1179656 | tf_op jit(solution)/shard_map/ppermute | solution.py:31
  (3 other events, 26.8 us)
